TPU v7x, 32 devices: a whole 2x2x4 slice. The times are simulated.
32 devices in a mesh: groups: 2 (over y), dom: 4 (over z), sub: 2 (over x), rhs: 2 (over core).
Axes of the slice: x: 2, y: 2, z: 4, core: 2. Of those that a mesh axis runs over, the one named last changes fastest.
Arguments:
- traces: bfloat16 [2, 2, 30, 32, 4096], P(None, None, None, 'rhs', ('groups', 'dom', 'sub')), parts along dimension 4, may hold values from -6 to 6
- solver: bfloat16 [2, 2, 210, 120], P('groups'), parts along dimension 0, may hold values from -0.375 to 0.375
- mass: bfloat16 [1, 35, 35], replicated, as said below
- dom_lists: int32 [2, 256], P(None, ('dom', 'sub')), may hold values from 0 to 255
- sub_lists: int32 [2, 256], P(None, ('dom', 'sub')), may hold values from 0 to 255
- elem_face: int32 [4, 1024], P(None, ('dom', 'sub')), may hold values from 0 to 383, as said below
- volume: float32 [1024], P(('dom', 'sub')), may hold values from 0.3 to 3
- elem_owner: int32 [1024, 1], P(('dom', 'sub')), may hold values from 0 to 7; in each aligned block of 128 rows (0 to 127, 128 to 255, ...) at most 48 rows name the same one
- elem_slot: int32 [1024], P(('dom', 'sub')), may hold values from 0 to 127
Outputs:
- sensitivity: float32 [6, 32, 2048], P(None, 'rhs', ('groups', 'dom', 'sub')), parts along dimension 2
There are 2 independent parts, one for each index of `groups`. A program takes and returns all parts, laid end to end along the dimension named above; an argument that names none is the same for every part. Nothing has to cross between parts.
Inputs may be any that keep to these rules, and one draw needn't show every extreme that they name: `elem_face`: entries below 256 name an owned face; 256 + b * 32 + r names entry r of block b of the extended table (b = 0 lower slab neighbour, 1 upper, 2 + t the partition of sub index t). Partitions of the first slab never name block 0, those of the last never block 1. `elem_owner`: among the elements of one partition at most 48 name the same owner. `mass`: symmetric in its last two dimensions.
All inputs are finite; a program needn't handle non-finite values.
Results may differ from a plain program's by a relative error of at most 0.0041.
Values may be sent and summed in bfloat16 or wider, within the bound.
No kernel may reach another device: no remote copies, remote signals or barrier semaphores. Data moves between devices by JAX's collectives and lax.ppermute only.
A program may use at most 64 MiB of HBM per device.

v0:
```python
import math

import jax
import jax.numpy as jnp
from jax import lax
from jax.sharding import PartitionSpec as P

CELLS_DEV = 128
BASIS = 35
VOX_DEV = 128
ELEM_DEV = 128
FIELD = 210
TRACE = 30


def padded_2(x, sides, width):
    for axis, dim in sides:
        size, length = (lax.axis_size(axis), x.shape[dim])
        up = [(i, (i + 1) % size) for i in range(size - 1)]
        down = [(j, i) for i, j in up]
        last = lax.slice_in_dim(x, length - width, length, axis=dim)
        leading = lax.slice_in_dim(x, 0, width, axis=dim)
        before = lax.ppermute(last, axis, up)
        after = lax.ppermute(leading, axis, down)
        x = jnp.concatenate([before, x, after], axis=dim)
    return x


def element_terms(extended, solver, mass, face_refs, volumes):
    traces_block = jnp.take(extended, face_refs, axis=4)
    matrix = solver[0].reshape(2, FIELD, 4, TRACE)
    stacked = jnp.stack([jnp.stack([matrix[0], -matrix[1]]), jnp.stack([matrix[1], matrix[0]])])
    fields = jnp.einsum(
        "pqofn,aqncfe->poace", stacked, traces_block, preferred_element_type=jnp.float32
    ).astype(jnp.bfloat16)
    electric = fields[:, : 3 * BASIS].reshape(2, 3, BASIS, 2, fields.shape[3], CELLS_DEV)
    weighted = jnp.einsum(
        "xb,pibce->pixce", mass[0], electric[:, :, :, 0], preferred_element_type=jnp.float32
    )
    sign_flip = jnp.array([1.0, -1.0], jnp.float32).reshape(2, 1, 1, 1, 1)
    tensor = jnp.einsum(
        "pixce,pjxce->ijce",
        electric[:, :, :, 1].astype(jnp.float32),
        weighted * sign_flip,
        precision=lax.Precision.HIGHEST,
    )
    symmetric = jnp.stack(
        [
            tensor[0, 0],
            tensor[1, 1],
            tensor[2, 2],
            0.5 * (tensor[0, 1] + tensor[1, 0]),
            0.5 * (tensor[0, 2] + tensor[2, 0]),
            0.5 * (tensor[1, 2] + tensor[2, 1]),
        ]
    )
    norm_factor = 1.0 / math.sqrt(70.0 * ELEM_DEV / VOX_DEV)
    pieces = symmetric * (volumes * norm_factor)
    return pieces


def per_device(
    traces, solver, mass, dom_lists, sub_lists, elem_face, volume, elem_owner, elem_slot
):
    n_sub = lax.axis_size("sub")
    owners_count = lax.axis_size("dom") * n_sub
    columns = traces.shape[3]
    list_rows = dom_lists.shape[1]
    capacity = max(2, 3 * ELEM_DEV // owners_count)
    slab_publish = jnp.take(traces, dom_lists, axis=4)
    padded = padded_2(slab_publish, (("dom", 4),), 1)
    peer_publish = jnp.take(traces, sub_lists, axis=4)
    received = lax.all_to_all(peer_publish, "sub", split_axis=4, concat_axis=4, tiled=True)
    extended = jnp.concatenate(
        [
            traces,
            padded[:, :, :, :, 0],
            padded[:, :, :, :, 3],
            received.reshape(traces.shape[:4] + (n_sub * list_rows,)),
        ],
        axis=4,
    )
    terms = element_terms(extended, solver, mass, elem_face, volume)
    owner_ids = elem_owner[:, 0]
    position_row = lax.broadcasted_iota(jnp.int32, (ELEM_DEV, ELEM_DEV), 0)
    position_col = lax.broadcasted_iota(jnp.int32, (ELEM_DEV, ELEM_DEV), 1)
    earlier_same = (owner_ids[:, None] == owner_ids[None, :]) & (position_row < position_col)
    ranking = jnp.sum(earlier_same.astype(jnp.int32), axis=0)
    slot_index = owner_ids * capacity + ranking
    value_width = 6 * columns
    payload = terms.reshape(value_width, ELEM_DEV).T
    send_values = (
        jnp.zeros((owners_count * capacity, value_width), jnp.float32).at[slot_index].set(payload)
    )
    send_slots = jnp.zeros((owners_count * capacity,), jnp.int32).at[slot_index].set(elem_slot)
    send_values = send_values.reshape(owners_count, capacity * value_width)
    send_slots = send_slots.reshape(owners_count, capacity)
    got_values, got_slots = (
        lax.all_to_all(send_values, ("dom", "sub"), split_axis=0, concat_axis=0, tiled=True),
        lax.all_to_all(send_slots, ("dom", "sub"), split_axis=0, concat_axis=0, tiled=True),
    )
    got_values = got_values.reshape(owners_count * capacity, value_width)
    got_slots = got_slots.reshape(owners_count * capacity)
    voxel_iota = lax.broadcasted_iota(jnp.int32, (1, VOX_DEV), 1)
    indicator = (got_slots[:, None] == voxel_iota).astype(jnp.float32)
    summed = jnp.einsum("sm,sv->mv", got_values, indicator, precision=lax.Precision.HIGHEST)
    return summed.reshape(6, columns, VOX_DEV)


def solution(mesh):
    return jax.shard_map(
        per_device,
        mesh=mesh,
        in_specs=(
            P(None, None, None, "rhs", ("groups", "dom", "sub")),
            P("groups", None, None, None),
            P(),
            P(None, ("dom", "sub")),
            P(None, ("dom", "sub")),
            P(None, ("dom", "sub")),
            P(("dom", "sub")),
            P(("dom", "sub"), None),
            P(("dom", "sub")),
        ),
        out_specs=P(None, "rhs", ("groups", "dom", "sub")),
        check_vma=False,
    )
```

profile of v0, /device:TPU:0, one launch (start us, length us, event | category | flops | bytes accessed | tf_op | source)
XLA Modules:
  0.0 167.5 jit_solution(18413204043268010764)
XLA Ops:
  0.0 0.7 compare_select_fusion.1
  0.7 0.7 compare_and_fusion
  1.4 6.2 %copy.208 = bf16[2,2,30,16,256]{2,3,4,1,0:T(8,128)(2,1)} copy(bf16[2,2,30,16,256]{4,3,2,1,0:T(8,128)(2,1)} %param.12) | data formatting | bytes 1966080 | tf_op args[0]
  7.6 0.1 reshape.174
  7.7 3.0 %gather_fusion.2 = bf16[64,2,2,30,16]{3,4,2,1,0:T(8,128)(2,1)S(1)} fusion(bf16[2,2,30,16,256]{2,3,4,1,0:T(8,128)(2,1)} %copy.208, s32[1024]{0:T(1024)S(1)} %get-tuple-element.23), kind=kCustom, calls=%fused_computation.1.clone | custom fusion | bytes 491776 | tf_op jit(solution)/shard_map/jit(_take)/gather | solution.py:72
  10.7 0.0 copy-start.6
  10.7 1.9 %copy.211 = bf16[2,32,2,2,30,16]{1,5,4,3,2,0:T(8,128)(2,1)S(1)} copy(bf16[2,32,2,2,30,16]{4,5,3,2,1,0:T(8,128)(2,1)S(1)} %bitcast.94) | data formatting | bytes 491520 | tf_op jit(solution)/shard_map/jit(_take)/gather | solution.py:72
  12.6 0.1 fusion.33
  12.8 1.6 reshape.204
  14.4 4.2 %all-to-all-start = ((bf16[2,2,30720]{2,1,0:T(2,128)(2,1)}), bf16[2,2,30720]{2,1,0:T(2,128)(2,1)S(1)}, u32[]{:S(2)}, u32[]{:S(2)}) async-start(bf16[2,2,30720]{2,1,0:T(2,128)(2,1)} %reshape.204), calls=%async_computation | async-start | bytes 491520 | tf_op jit(solution)/shard_map/all_to_all | solution.py:73
  18.6 0.1 reshape.170
  18.7 3.0 %gather_fusion.1 = bf16[64,2,2,30,16]{3,4,2,1,0:T(8,128)(2,1)S(1)} fusion(bf16[2,2,30,16,256]{2,3,4,1,0:T(8,128)(2,1)} %copy.208, s32[1024]{0:T(1024)S(1)} %pad_clamp_fusion.2), kind=kCustom, calls=%fused_computation.clone | custom fusion | bytes 491776 | tf_op jit(solution)/shard_map/jit(_take)/gather | solution.py:70
  21.7 0.0 copy-start.3
  21.7 1.9 %copy.209 = bf16[2,32,2,2,30,16]{1,5,4,3,2,0:T(8,128)(2,1)S(1)} copy(bf16[2,32,2,2,30,16]{4,5,3,2,1,0:T(8,128)(2,1)S(1)} %bitcast.93) | data formatting | bytes 491520 | tf_op jit(solution)/shard_map/jit(_take)/gather | solution.py:70
  23.6 0.0 copy-start.8
  23.6 0.0 copy-start.9
  23.6 0.1 select_bitcast_fusion.1
  23.7 1.1 fusion.31
  24.9 4.2 %collective-permute-start = (bf16[2,2,30,16,1,32]{5,3,2,1,0,4:T(8,128)(2,1)}, bf16[2,2,30,16,1,32]{5,3,2,1,0,4:T(8,128)(2,1)S(1)}, u32[]{:S(2)}, u32[]{:S(2)}) collective-permute-start(bf16[2,2,30,16,1,32]{5,3,2,1,0,4:T(8,128)(2,1)} %get-tuple-element.16), channel_id=1, source_target_pairs={{0,4},{4,8},{8,12},{1,5},{5,9},{9,13},{2,6},{6,10},{10,14},{3,7},{... | collective-permute-start | bytes 368648 | tf_op jit(solution)/shard_map/ppermute | solution.py:23
  29.1 1.3 collective-permute-start.1
  30.4 0.2 fusion.32
  30.6 0.1 copy.203
  30.7 0.1 fusion.29
  30.8 0.1 copy.202
  30.9 0.0 copy-start.1
  30.9 0.1 copy.205
  31.0 0.1 convert_reduce_fusion
  31.1 0.1 maximum_bitcast_fusion.1
  31.3 1.1 scatter_custom_fusion.1
  32.4 0.7 all_to_all.18
  33.1 0.9 maximum_bitcast_fusion
  34.0 8.1 %all-to-all-start.2 = ((s32[8,1,48]{2,1,0:T(1,128)}), s32[8,1,48]{2,1,0:T(1,128)S(1)}, u32[]{:S(2)}, u32[]{:S(2)}) async-start(s32[8,1,48]{2,1,0:T(1,128)} %all_to_all.18), calls=%async_computation.2 | async-start | bytes 8192 | tf_op jit(solution)/shard_map/all_to_all | solution.py:100
  42.1 0.5 reshape.205
  42.6 1.5 copy.212
  44.1 1.3 reshape.121
  45.4 0.0 collective-permute-done
  45.4 0.0 collective-permute-done.1
  45.4 0.8 copy-done.2
  46.2 1.8 %pad_maximum_fusion = bf16[2,2,30,16,384]{4,3,2,1,0:T(8,128)(2,1)S(1)} fusion(bf16[2,2,30,16,64]{4,3,2,1,0:T(8,128)(2,1)} %reshape.121, bf16[2,2,30,16,32]{4,3,2,1,0:T(8,128)(2,1)} %bitcast.9, bf16[2,2,30,16,32]{4,3,2,1,0:T(8,128)(2,1)} %bitcast.98, bf16[2,2,30,16,256]{4,3,2,1,0:T(8,128)(2,1)S(1)} %copy-done.1), kind=kLoop, calls=%fused_computation.14 | loop fusion | flops 5898240 | bytes 2949120 | tf_op jit(solution)/shard_map/concatenate | solution.py:74
  48.0 6.6 %copy.213 = bf16[2,2,30,16,384]{2,3,4,1,0:T(8,128)(2,1)} copy(bf16[2,2,30,16,384]{4,3,2,1,0:T(8,128)(2,1)S(1)} %pad_maximum_fusion) | data formatting | bytes 2949120 | tf_op jit(solution)/shard_map/concatenate | solution.py:74
  54.6 23.2 %gather_fusion = bf16[512,2,2,30,16]{3,4,2,1,0:T(8,128)(2,1)} fusion(bf16[2,2,30,16,384]{2,3,4,1,0:T(8,128)(2,1)} %copy.213, s32[1024]{0:T(1024)S(1)} %get-tuple-element.22), kind=kCustom, calls=%fused_computation.2 | custom fusion | bytes 3934208 | tf_op jit(solution)/shard_map/jit(_take)/gather | solution.py:30
  77.8 10.1 %copy.214 = bf16[4,128,2,2,30,16]{1,4,3,0,5,2:T(8,128)(2,1)S(1)} copy(bf16[4,128,2,2,30,16]{4,5,3,2,1,0:T(8,128)(2,1)} %bitcast.91) | data formatting | bytes 3932160 | tf_op jit(solution)/shard_map/jit(_take)/gather | solution.py:30
  87.9 1.1 convolution_bitcast_fusion
  89.1 0.1 slice.119
  89.2 0.0 copy-start.7
  89.2 0.4 copy.216
  89.7 0.3 fusion.30
  90.0 0.4 multiply_bitcast_fusion
  90.4 5.9 %copy.219 = f32[2,3,35,16,128]{2,1,0,4,3:T(4,128)} copy(f32[2,3,35,16,128]{4,2,3,1,0:T(8,128)S(1)} %multiply_bitcast_fusion) | data formatting | bytes 3440640 | tf_op jit(solution)/shard_map/mul | solution.py:44
  96.3 3.7 %copy.230 = bf16[2,3,35,1,16,128]{2,1,0,5,4,3:T(4,128)(2,1)} copy(bf16[2,3,35,1,16,128]{5,4,3,2,1,0:T(8,128)(2,1)S(1)} %get-tuple-element.14) | data formatting | bytes 1720320
  100.1 12.6 %fusion.2 = f32[3,3,16,128]{0,1,3,2:T(4,128)S(1)} fusion(f32[2,3,35,16,128]{2,1,0,4,3:T(4,128)} %copy.219, bf16[2,3,35,1,16,128]{2,1,0,5,4,3:T(4,128)(2,1)} %copy.230), kind=kOutput, calls=%fused_computation.9 | convolution fusion | flops 15482880 | bytes 2654208 | tf_op jit(solution)/shard_map/pixce,pjxce->ijce/dot_general | solution.py:41
  112.7 37.9 %fusion.14 = (f32[16,128]{1,0:T(8,128)S(1)}, f32[16,128]{1,0:T(8,128)S(1)}, f32[16,128]{1,0:T(8,128)S(1)}, f32[16,128]{1,0:T(8,128)S(1)}, f32[16,128]{1,0:T(8,128)S(1)}, /*index=5*/f32[16,128]{1,0:T(8,128)S(1)}) fusion(f32[3,3,16,128]{0,1,3,2:T(4,128)S(1)} %fusion.2), kind=kLoop, calls=%fused_computation.27 | loop fusion | flops 12288 | bytes 122880 | tf_op jit(solution)/shard_map/mul | solution.py:54
  150.6 0.1 copy.220
  150.7 0.9 scatter_custom_fusion
  151.6 0.9 all_to_all.20
  152.5 6.0 %all-to-all-start.1 = ((f32[8,1,4608]{2,1,0:T(1,128)}), f32[8,1,4608]{2,1,0:T(1,128)S(1)}, u32[]{:S(2)}, u32[]{:S(2)}) async-start(f32[8,1,4608]{2,1,0:T(1,128)} %all_to_all.20), calls=%async_computation.1 | async-start | bytes 294912 | tf_op jit(solution)/shard_map/all_to_all | solution.py:99
  158.5 0.5 broadcast.102
  159.0 0.7 reduce.16
  159.7 0.1 eq.34
  159.8 6.2 %all-to-all-done.1 = f32[8,1,4608]{2,1,0:T(1,128)S(1)} async-done(((f32[8,1,4608]{2,1,0:T(1,128)}), f32[8,1,4608]{2,1,0:T(1,128)S(1)}, u32[]{:S(2)}, u32[]{:S(2)}) %all-to-all-start.1) | async-done | bytes 147488 | tf_op jit(solution)/shard_map/all_to_all | solution.py:99
  166.0 0.4 reduce.6
  166.3 0.1 reshape.123
  166.4 0.1 copy.222
  166.6 0.9 fusion.17
  (32 shorter events, 0.2 us)
Async XLA Ops:
  0.0 90.0 %copy-start = (bf16[1,35,35]{2,1,0:T(8,128)(2,1)S(1)}, bf16[1,35,35]{2,1,0:T(8,128)(2,1)}, u32[]{:S(2)}) copy-start(bf16[1,35,35]{2,1,0:T(8,128)(2,1)} %param.14) | copy-start | bytes 7354
  0.0 7.6 %copy-start.5 = (s32[4,128]{1,0:T(4,128)S(1)}, s32[4,128]{1,0:T(4,128)}, u32[]{:S(2)}) copy-start(s32[4,128]{1,0:T(4,128)} %param.17) | copy-start | bytes 6148
  10.7 7.9 %copy-start.6 = (s32[2,32]{1,0:T(2,128)S(1)}, s32[2,32]{1,0:T(2,128)}, u32[]{:S(2)}) copy-start(s32[2,32]{1,0:T(2,128)} %param.15) | copy-start | bytes 772
  14.4 19.6 %all-to-all-start = ((bf16[2,2,30720]{2,1,0:T(2,128)(2,1)}), bf16[2,2,30720]{2,1,0:T(2,128)(2,1)S(1)}, u32[]{:S(2)}, u32[]{:S(2)}) async-start(bf16[2,2,30720]{2,1,0:T(2,128)(2,1)} %reshape.204), calls=%async_computation | async-start | bytes 491520 | tf_op jit(solution)/shard_map/all_to_all | solution.py:73
  21.7 8.7 %copy-start.3 = (bf16[1,2,210,120]{3,1,2,0:T(2,128)(2,1)S(1)}, bf16[1,2,210,120]{3,1,2,0:T(2,128)(2,1)}, u32[]{:S(2)}) copy-start(bf16[1,2,210,120]{3,1,2,0:T(2,128)(2,1)} %param.13) | copy-start | bytes 302404
  23.6 7.4 %copy-start.8 = (f32[128]{0:T(128)S(1)}, f32[128]{0:T(128)}, u32[]{:S(2)}) copy-start(f32[128]{0:T(128)} %param.18) | copy-start | bytes 1540
  23.6 7.4 %copy-start.9 = (s32[128,1]{0,1:T(1,128)S(1)}, s32[128,1]{0,1:T(1,128)}, u32[]{:S(2)}) copy-start(s32[128,1]{0,1:T(1,128)} %param.19) | copy-start | bytes 1540
  24.9 20.5 %collective-permute-start = (bf16[2,2,30,16,1,32]{5,3,2,1,0,4:T(8,128)(2,1)}, bf16[2,2,30,16,1,32]{5,3,2,1,0,4:T(8,128)(2,1)S(1)}, u32[]{:S(2)}, u32[]{:S(2)}) collective-permute-start(bf16[2,2,30,16,1,32]{5,3,2,1,0,4:T(8,128)(2,1)} %get-tuple-element.16), channel_id=1, source_target_pairs={{0,4},{4,8},{8,12},{1,5},{5,9},{9,13},{2,6},{6,10},{10,14},{3,7},{... | collective-permute-start | bytes 368648 | tf_op jit(solution)/shard_map/ppermute | solution.py:23
  29.1 16.3 %collective-permute-start.1 = (bf16[2,2,30,16,1,32]{5,3,2,1,0,4:T(8,128)(2,1)}, bf16[2,2,30,16,1,32]{5,3,2,1,0,4:T(8,128)(2,1)}, u32[]{:S(2)}, u32[]{:S(2)}) collective-permute-start(bf16[2,2,30,16,1,32]{5,3,2,1,0,4:T(8,128)(2,1)} %get-tuple-element.17), channel_id=1, source_target_pairs={{4,0},{8,4},{12,8},{5,1},{9,5},{13,9},{6,2},{10,6},{14,10},{7,3},{... | collective-permute-start | bytes 368648 | tf_op jit(solution)/shard_map/ppermute | solution.py:24
  30.9 15.3 %copy-start.1 = (bf16[2,2,30,16,256]{4,3,2,1,0:T(8,128)(2,1)S(1)}, bf16[2,2,30,16,256]{4,3,2,1,0:T(8,128)(2,1)}, u32[]{:S(2)}) copy-start(bf16[2,2,30,16,256]{4,3,2,1,0:T(8,128)(2,1)} %param.12) | copy-start | bytes 2949124
  34.0 118.5 %all-to-all-start.2 = ((s32[8,1,48]{2,1,0:T(1,128)}), s32[8,1,48]{2,1,0:T(1,128)S(1)}, u32[]{:S(2)}, u32[]{:S(2)}) async-start(s32[8,1,48]{2,1,0:T(1,128)} %all_to_all.18), calls=%async_computation.2 | async-start | bytes 8192 | tf_op jit(solution)/shard_map/all_to_all | solution.py:100
  45.4 0.8 copy-start.2
  77.8 10.1 %copy-start.4 = (bf16[2,2,210,4,30,1,1]{2,3,4,1,0,6,5:T(4,128)(2,1)S(1)}, bf16[2,2,210,4,30,1,1]{2,3,4,1,0,6,5:T(4,128)(2,1)}, u32[]{:S(2)}) copy-start(bf16[2,2,210,4,30,1,1]{2,3,4,1,0,6,5:T(4,128)(2,1)} %maximum_bitcast_fusion) | copy-start | bytes 604804
  89.2 0.8 copy-start.7
  152.5 13.5 %all-to-all-start.1 = ((f32[8,1,4608]{2,1,0:T(1,128)}), f32[8,1,4608]{2,1,0:T(1,128)S(1)}, u32[]{:S(2)}, u32[]{:S(2)}) async-start(f32[8,1,4608]{2,1,0:T(1,128)} %all_to_all.20), calls=%async_computation.1 | async-start | bytes 294912 | tf_op jit(solution)/shard_map/all_to_all | solution.py:99
where the time goes:
time: 168 us; the launch traced here: 167 us
  local copies, waits for them, and re-layouts  78.4 us (47%)
  other arithmetic  43.5 us (26%)
  starting transfers between devices  23.8 us (14%)
  matrix products  15.1 us (9%)
  waiting for transfers between devices  6.21 us (4%)
    mul x1, other arithmetic, element_terms(): 0.5 * (tensor[1, 2] + tensor[2, 1])  37.9 us
    gather x2, local copies, waits for them, and re-layouts, element_terms(): traces_block = jnp.take(extended, face_refs, axis=4)  33.3 us
    unnamed x29, local copies, waits for them, and re-layouts  12.9 us
    dot_general x1, matrix products, element_terms(): jnp.einsum('pixce,pjxce->ijce', electric[:, :, :, 1].astype(jnp.float32),...  12.6 us
    all_to_all x1, starting transfers between devices, per_device(): lax.all_to_all(send_slots, ('dom', 'sub'), split_axis=0, concat_axis=0, t...  8.12 us
    concatenate x1, local copies, waits for them, and re-layouts, per_device(): jnp.concatenate([traces, padded[:, :, :, :, 0], padded[:, :, :, :, 3], re...  6.62 us
    all_to_all x1, waiting for transfers between devices, per_device(): lax.all_to_all(send_values, ('dom', 'sub'), split_axis=0, concat_axis=0,...  6.2 us
    all_to_all x1, starting transfers between devices, per_device(): lax.all_to_all(send_values, ('dom', 'sub'), split_axis=0, concat_axis=0,...  6 us
  transfers between devices with their start and end apart: 5, of which 1 were waited for; matrix products, arithmetic and copies ran while one was open for 71% of the time, Pallas kernels for 0%

commit v1 on v0

v1 whole, which is shorter than its diff:
```python
import math

import jax
import jax.numpy as jnp
from jax import lax
from jax.experimental import pallas as pl
from jax.experimental.pallas import tpu as pltpu
from jax.sharding import PartitionSpec as P

BASIS = 35
HALF = 3 * BASIS
GROUP = 40
NODES = 30
BLOCK = 256
VMEM_LIMIT = 48 * 1024 * 1024

NT = (((1,), (1,)), ((), ()))
NN = (((1,), (0,)), ((), ()))
TN = (((0,), (0,)), ((), ()))


def dot(a, b, dims=NN):
    return lax.dot_general(a, b, dims, preferred_element_type=jnp.float32)


def iota(shape, axis):
    return lax.broadcasted_iota(jnp.int32, shape, axis)


def one_hot(condition):
    return jnp.where(condition, 1.0, 0.0).astype(jnp.bfloat16)


def pair_index(index, k, size):
    if size & (size - 1) == 0:
        return index ^ k, index ^ k
    return lax.rem(index + k, size), lax.rem(index + size - k, size)


def pack_kernel(n_sub, rows, dom_ref, sub_ref, traces_ref, *out_refs):
    faces = traces_ref.shape[1]
    parity = lax.rem(lax.axis_index("dom"), 2)
    within = lax.axis_index("sub")
    lists = [dom_ref[pl.ds(1 - parity, 1), :], dom_ref[pl.ds(parity, 1), :]]
    for k in range(1, n_sub):
        lists.append(sub_ref[pl.ds(pair_index(within, k, n_sub)[0], 1), :])
    face = iota((faces, rows), 0)
    picks = [jnp.where(face == row, 1.0, 0.0).T for row in lists]
    picks = jnp.concatenate(picks, axis=0).astype(jnp.bfloat16)
    packed = dot(picks, traces_ref[...], NT).astype(jnp.bfloat16)
    for k, out_ref in enumerate(out_refs):
        out_ref[...] = packed[k * rows : (k + 1) * rows]


def element_kernel(
    n_sub,
    capacity,
    columns,
    sub_ref,
    traces_ref,
    solver_ref,
    mass_ref,
    elem_ref,
    volume_ref,
    owner_ref,
    slot_ref,
    *refs,
):
    halo_refs = refs[: n_sub + 1]
    out_ref, gathered_ref, sums_ref = refs[n_sub + 1 :]
    faces = traces_ref.shape[1]
    elems = elem_ref.shape[1]
    rows = sub_ref.shape[1]
    slots = out_ref.shape[0]
    parity = lax.rem(lax.axis_index("dom"), 2)
    within = lax.axis_index("sub")
    face_rows = [elem_ref[f : f + 1, :] for f in range(4)]

    def picks(size, start):
        return jnp.concatenate(
            [jnp.where(iota((size, elems), 0) + start == row, 1.0, 0.0) for row in face_rows],
            axis=1,
        )

    own_list = sub_ref[pl.ds(within, 1), :]
    own_list = one_hot(iota((faces, rows), 0) == own_list)
    own_block = picks(rows, faces + (2 + within) * rows).astype(jnp.bfloat16)
    own = (picks(faces, 0) + dot(own_list, own_block)).astype(jnp.bfloat16)
    blocks = [1 - parity, parity]
    for k in range(1, n_sub):
        blocks.append(2 + pair_index(within, k, n_sub)[1])
    halo = [picks(rows, faces + block * rows).astype(jnp.bfloat16) for block in blocks]
    table = jnp.concatenate([own] + halo, axis=0)

    per_block = BLOCK // columns
    row = iota((BLOCK, BLOCK), 0)
    col = iota((BLOCK, BLOCK), 1)
    reorder = one_hot(
        lax.rem(row, per_block) * columns + lax.div(row, per_block) == col
    )
    half = 2 * NODES * columns
    starts = []
    for a in range(2):
        first = a * half - (a * half) % 128
        starts += [first + b * BLOCK for b in range(4)]
    halo_rows = jnp.concatenate([ref[...] for ref in halo_refs], axis=0)
    for b, start in enumerate(starts):
        mine = dot(reorder, traces_ref[start : start + BLOCK, :])
        others = dot(reorder, halo_rows[:, start : start + BLOCK], NT)
        both = jnp.concatenate([mine, others], axis=1).astype(jnp.bfloat16)
        got = dot(both, table).astype(jnp.bfloat16)
        gathered_ref[b] = got.reshape(columns, per_block, 4 * elems)

    place = iota((3 * GROUP, HALF), 0)
    source = iota((3 * GROUP, HALF), 1)
    spread = one_hot(
        (lax.div(place, GROUP) == lax.div(source, BASIS))
        & (lax.rem(place, GROUP) == lax.rem(source, BASIS))
    )
    real = dot(spread, solver_ref[0, :HALF, :]).astype(jnp.bfloat16)
    imag = dot(spread, solver_ref[1, :HALF, :]).astype(jnp.bfloat16)
    matrices = []
    for a in range(2):
        shift = ((a * half) % 128) // columns
        source = iota((4 * NODES, BLOCK), 0)
        place = iota((4 * NODES, BLOCK), 1)
        target = lax.div(source, NODES) * 64 + lax.rem(source, NODES) + shift
        for_real = one_hot(target == place)
        for_imag = one_hot(target + NODES == place)
        top = dot(real, for_real) - dot(imag, for_imag)
        bottom = dot(imag, for_real) + dot(real, for_imag)
        matrices.append(jnp.concatenate([top, bottom], axis=0).astype(jnp.bfloat16))

    size = 6 * GROUP
    spread = one_hot(lax.rem(iota((size, BASIS), 0), GROUP) == iota((size, BASIS), 1))
    tiles = dot(dot(spread, mass_ref[0]).astype(jnp.bfloat16), spread, NT)
    row = iota((size, size), 0)
    col = iota((size, size), 1)
    tiles = jnp.where(lax.div(row, GROUP) == lax.div(col, GROUP), tiles, 0.0)
    masses = jnp.where(row < 3 * GROUP, tiles, -tiles).astype(jnp.bfloat16)

    pairs = [(0, 0), (1, 1), (2, 2), (0, 1), (0, 2), (1, 2)]

    def step(index, carry):
        fields = []
        for a in range(2):
            parts = []
            for c in range(2):
                taken = [gathered_ref[a * 4 + b, 2 * index + c] for b in range(4)]
                parts.append(
                    jnp.concatenate(
                        [
                            taken[b][:, f * elems : (f + 1) * elems]
                            for f in range(4)
                            for b in range(4)
                        ],
                        axis=0,
                    )
                )
            values = dot(matrices[a], jnp.concatenate(parts, axis=1))
            fields.append(values.astype(jnp.bfloat16))
        weighted = dot(masses, fields[0])
        shape = (2, 3, GROUP // 8, 8, 2 * elems)
        adjoint = fields[1].astype(jnp.float32).reshape(shape)
        weighted = weighted.reshape(shape)
        for m, (i, j) in enumerate(pairs):
            products = adjoint[:, i] * weighted[:, j]
            if i != j:
                products = products + adjoint[:, j] * weighted[:, i]
            total = jnp.sum(products, axis=(0, 1))
            for c in range(2):
                start = pl.multiple_of((m * columns + 2 * index + c) * 8, 8)
                sums_ref[pl.ds(start, 8), :] = total[:, c * elems : (c + 1) * elems]
        return carry

    lax.fori_loop(0, columns // 2, step, 0)

    width = 6 * columns
    total = sums_ref[pl.ds(0, width, stride=8), :]
    for k in range(1, 8):
        total = total + sums_ref[pl.ds(k, width, stride=8), :]
    norm = 1.0 / math.sqrt(70.0)
    factor = jnp.where(iota((width, 1), 0) < 3 * columns, norm, 0.5 * norm)
    terms = total * (factor * volume_ref[...])

    owner = owner_ref[...]
    owners = iota((max(8, slots // capacity), elems), 0) == owner
    earlier = one_hot(iota((elems, elems), 0) < iota((elems, elems), 1))
    counts = dot(one_hot(owners), earlier)
    rank = jnp.sum(jnp.where(owners, counts, 0.0), axis=0, keepdims=True)
    target = owner * capacity + rank.astype(jnp.int32)
    sends = one_hot(iota((slots, elems), 0) == target)
    slot = jnp.broadcast_to(slot_ref[...].astype(jnp.float32), (128 - width, elems))
    payload = jnp.concatenate([terms, slot], axis=0).astype(jnp.bfloat16)
    out_ref[...] = dot(sends, payload, NT).astype(jnp.bfloat16)


def voxel_kernel(width, got_ref, out_ref):
    got = got_ref[...]
    slot = got[:, width : width + 1].astype(jnp.int32)
    voxels = out_ref.shape[1]
    members = one_hot(slot == iota((got.shape[0], voxels), 1))
    out_ref[...] = dot(got, members, TN)[:width]


def per_device(
    traces, solver, mass, dom_lists, sub_lists, elem_face, volume, elem_owner, elem_slot
):
    n_dom, n_sub = lax.axis_size("dom"), lax.axis_size("sub")
    owners = n_dom * n_sub
    columns, faces = traces.shape[3:]
    rows = dom_lists.shape[1]
    elems = elem_face.shape[1]
    capacity = max(2, 3 * elems // owners)
    width = 6 * columns
    table = traces.reshape(-1, faces)
    values = table.shape[0]
    params = pltpu.CompilerParams(vmem_limit_bytes=VMEM_LIMIT)

    packed = pl.pallas_call(
        lambda *refs: pack_kernel(n_sub, rows, *refs),
        out_shape=[jax.ShapeDtypeStruct((rows, values), jnp.bfloat16)] * (n_sub + 1),
        compiler_params=params,
        name="pack",
    )(dom_lists, sub_lists, table)

    even = [(i, i + 1) for i in range(0, n_dom - 1, 2)]
    odd = [(i, i + 1) for i in range(1, n_dom - 1, 2)]
    halos = [
        lax.ppermute(part, "dom", pairs + [(j, i) for i, j in pairs])
        for part, pairs in zip(packed, (even, odd))
    ]
    for k in range(1, n_sub):
        pairs = [(i, pair_index(i, k, n_sub)[0]) for i in range(n_sub)]
        halos.append(lax.ppermute(packed[1 + k], "sub", [(i, int(j)) for i, j in pairs]))

    sent = pl.pallas_call(
        lambda *refs: element_kernel(n_sub, capacity, columns, *refs),
        out_shape=jax.ShapeDtypeStruct((owners * capacity, 128), jnp.bfloat16),
        scratch_shapes=[
            pltpu.VMEM((8, columns, BLOCK // columns, 4 * elems), jnp.bfloat16),
            pltpu.VMEM((8 * width, elems), jnp.float32),
        ],
        compiler_params=params,
        name="elements",
    )(
        sub_lists,
        table,
        solver[0],
        mass,
        elem_face,
        volume.reshape(1, elems),
        elem_owner.reshape(1, elems),
        elem_slot.reshape(1, elems),
        *halos,
    )
    got = lax.all_to_all(sent, ("dom", "sub"), split_axis=0, concat_axis=0, tiled=True)
    summed = pl.pallas_call(
        lambda *refs: voxel_kernel(width, *refs),
        out_shape=jax.ShapeDtypeStruct((width, elems), jnp.float32),
        compiler_params=params,
        name="voxels",
    )(got)
    return summed.reshape(6, columns, elems)


def solution(mesh):
    return jax.shard_map(
        per_device,
        mesh=mesh,
        in_specs=(
            P(None, None, None, "rhs", ("groups", "dom", "sub")),
            P("groups", None, None, None),
            P(),
            P(None, ("dom", "sub")),
            P(None, ("dom", "sub")),
            P(None, ("dom", "sub")),
            P(("dom", "sub")),
            P(("dom", "sub"), None),
            P(("dom", "sub")),
        ),
        out_specs=P(None, "rhs", ("groups", "dom", "sub")),
        check_vma=False,
    )
```

time: 168 us -> 33.5 us (0.20)
  local copies, waits for them, and re-layouts: 78.4 us -> 4.17 us
  other arithmetic: 43.5 us -> 0 us
  starting transfers between devices: 23.8 us -> 5.3 us
  matrix products: 15.1 us -> 0 us
  blocking collectives: 0 us -> 13.5 us
  Pallas kernels: 0 us -> 7.69 us
  waiting for transfers between devices: 6.21 us -> 2.46 us
    gather x6 -> x0, local copies, waits for them, and re-layouts: 43.1 us -> none  [the longest x2 33.3 us: element_terms(): traces_block = jnp.take(extended, face_refs, axis=4)]
    mul x3 -> x0, other arithmetic: 37.9 us -> none  [the longest x1 37.9 us: element_terms(): 0.5 * (tensor[1, 2] + tensor[2, 1])]
    all_to_all x3 -> x0, starting transfers between devices: 18.3 us -> none  [the longest x1 8.12 us: per_device(): lax.all_to_all(send_slots, ('dom', 'sub'), split_axis=0, concat_axis=0, t...]
    dot_general x4 -> x0, matrix products: 15.1 us -> none  [the longest x1 12.6 us: element_terms(): jnp.einsum('pixce,pjxce->ijce', electric[:, :, :, 1].astype(jnp.float32),...]
    all_to_all x0 -> x1, blocking collectives: none -> 13.5 us  [per_device(): lax.all_to_all(sent, ('dom', 'sub'), split_axis=0, concat_axis=0, tiled=T...]
    unnamed x29 -> x19, local copies, waits for them, and re-layouts: 12.9 us -> 4.17 us
    pallas_call x0 -> x3, Pallas kernels: none -> 7.69 us  [the longest x1 6.33 us: per_device(): pl.pallas_call(lambda *refs: element_kernel(n_sub, capacity, columns, *re...]
    concatenate x1 -> x0, local copies, waits for them, and re-layouts: 6.62 us -> none  [per_device(): jnp.concatenate([traces, padded[:, :, :, :, 0], padded[:, :, :, :, 3], re...]
  transfers between devices with their start and end apart: 5 -> 3, of which waited for: 1 -> 2; matrix products, arithmetic and copies ran while one was open for 71% -> 3% of each run, Pallas kernels for 0% -> 0%
where the time goes in v1:
time: 33.5 us; the launch traced here: 33.2 us
  blocking collectives  13.5 us (40%)
  Pallas kernels  7.69 us (23%)
  starting transfers between devices  5.3 us (16%)
  local copies, waits for them, and re-layouts  4.17 us (12%)
  waiting for transfers between devices  2.46 us (7%)
    all_to_all x1, blocking collectives, per_device(): lax.all_to_all(sent, ('dom', 'sub'), split_axis=0, concat_axis=0, tiled=T...  13.5 us
    pallas_call x1, Pallas kernels, per_device(): pl.pallas_call(lambda *refs: element_kernel(n_sub, capacity, columns, *re...  6.33 us
    unnamed x19, local copies, waits for them, and re-layouts  4.17 us
    ppermute x2, starting transfers between devices, per_device(): lax.ppermute(part, 'dom', pairs + [(j, i) for i, j in pairs])  3.75 us
    ppermute x1, waiting for transfers between devices, per_device(): lax.ppermute(packed[1 + k], 'sub', [(i, int(j)) for i, j in pairs])  2.28 us
    ppermute x1, starting transfers between devices, per_device(): lax.ppermute(packed[1 + k], 'sub', [(i, int(j)) for i, j in pairs])  1.55 us
    pallas_call x1, Pallas kernels, per_device(): pl.pallas_call(lambda *refs: voxel_kernel(width, *refs), out_shape=jax.Sh...  0.89 us
  transfers between devices with their start and end apart: 3, of which 2 were waited for; matrix products, arithmetic and copies ran while one was open for 3% of the time, Pallas kernels for 0%

profile of v1, /device:TPU:0, one launch (start us, length us, event | category | flops | bytes accessed | tf_op | source)
XLA Modules:
  0.0 33.2 jit_solution(17242555312188898838)
XLA Ops:
  0.0 0.0 copy-start.3
  0.0 0.7 %copy-done.3 = s32[2,32]{1,0:T(2,128)S(1)} copy-done((s32[2,32]{1,0:T(2,128)S(1)}, s32[2,32]{1,0:T(2,128)}, u32[]{:S(2)}) %copy-start.3) | copy-done | bytes 280
  0.7 0.0 copy-start
  0.7 1.2 %copy-done = bf16[2,2,30,16,256]{4,3,2,1,0:T(8,128)(2,1)S(1)} copy-done((bf16[2,2,30,16,256]{4,3,2,1,0:T(8,128)(2,1)S(1)}, bf16[2,2,30,16,256]{4,3,2,1,0:T(8,128)(2,1)}, u32[]{:S(2)}) %copy-start) | copy-done | bytes 983064
  1.9 0.0 copy-start.5
  1.9 0.7 %copy-done.5 = s32[2,32]{1,0:T(2,128)S(1)} copy-done((s32[2,32]{1,0:T(2,128)S(1)}, s32[2,32]{1,0:T(2,128)}, u32[]{:S(2)}) %copy-start.5) | copy-done | bytes 280
  2.6 0.0 copy-start.1
  2.6 0.5 %pack.1 = (bf16[32,1920]{1,0:T(8,128)(2,1)S(1)}, bf16[32,1920]{1,0:T(8,128)(2,1)S(1)}, bf16[32,1920]{1,0:T(8,128)(2,1)S(1)}) custom-call(s32[2,32]{1,0:T(2,128)S(1)} %copy-done.5, s32[2,32]{1,0:T(2,128)S(1)} %copy-done.3, bf16[1920,256]{1,0:T(8,128)(2,1)S(1)} %bitcast.10), custom_call_target="tpu_custom_call" | custom-call | tf_op jit(solution)/shard_map/pack/pallas_call | solution.py:220
  3.0 3.1 %collective-permute-start = (bf16[32,1920]{1,0:T(8,128)(2,1)S(1)}, bf16[32,1920]{1,0:T(8,128)(2,1)S(1)}, u32[]{:S(2)}, u32[]{:S(2)}) collective-permute-start(bf16[32,1920]{1,0:T(8,128)(2,1)S(1)} %get-tuple-element.8), channel_id=1, source_target_pairs={{0,4},{8,12},{4,0},{12,8},{1,5},{9,13},{5,1},{13,9},{2,6},{10,14},... | collective-permute-start | bytes 368648 | tf_op jit(solution)/shard_map/ppermute | solution.py:230
  6.1 0.7 %collective-permute-start.1 = (bf16[32,1920]{1,0:T(8,128)(2,1)S(1)}, bf16[32,1920]{1,0:T(8,128)(2,1)S(1)}, u32[]{:S(2)}, u32[]{:S(2)}) collective-permute-start(bf16[32,1920]{1,0:T(8,128)(2,1)S(1)} %get-tuple-element.9), channel_id=1, source_target_pairs={{4,8},{8,4},{5,9},{9,5},{6,10},{10,6},{7,11},{11,7},{20,24},{24,20... | collective-permute-start | bytes 368648 | tf_op jit(solution)/shard_map/ppermute | solution.py:230
  6.8 1.6 %collective-permute-start.2 = (bf16[32,1920]{1,0:T(8,128)(2,1)S(1)}, bf16[32,1920]{1,0:T(8,128)(2,1)S(1)}, u32[]{:S(2)}, u32[]{:S(2)}) collective-permute-start(bf16[32,1920]{1,0:T(8,128)(2,1)S(1)} %get-tuple-element.10), channel_id=1, source_target_pairs={{0,2},{2,0},{1,3},{3,1},{4,6},{6,4},{5,7},{7,5},{8,10},{10,8},{9,1... | collective-permute-start | bytes 368648 | tf_op jit(solution)/shard_map/ppermute | solution.py:235
  8.3 0.0 copy-start.2
  8.3 0.9 %copy.12 = bf16[1,2,210,120]{3,2,1,0:T(8,128)(2,1)S(1)} copy(bf16[1,2,210,120]{3,1,2,0:T(2,128)(2,1)} %param.10) | data formatting | bytes 201600 | tf_op args[1]
  9.3 0.2 collective-permute-done.refs_8_
  9.5 0.0 collective-permute-done.1.refs_9_
  9.5 2.3 %collective-permute-done.2.refs_10_ = bf16[32,1920]{1,0:T(8,128)(2,1)S(1)} collective-permute-done((bf16[32,1920]{1,0:T(8,128)(2,1)S(1)}, bf16[32,1920]{1,0:T(8,128)(2,1)S(1)}, u32[]{:S(2)}, u32[]{:S(2)}) %collective-permute-start.2) | collective-permute-done | bytes 122912 | tf_op jit(solution)/shard_map/ppermute | solution.py:235
  11.7 0.0 copy-start.4
  11.7 0.0 copy-start.6
  11.7 0.0 copy-start.7
  11.7 0.0 copy-start.8
  11.7 0.0 copy-done.1
  11.8 0.0 copy-done.2
  11.8 0.7 %copy-done.4 = s32[4,128]{1,0:T(4,128)S(1)} copy-done((s32[4,128]{1,0:T(4,128)S(1)}, s32[4,128]{1,0:T(4,128)}, u32[]{:S(2)}) %copy-start.4) | copy-done | bytes 2072
  12.4 0.0 copy-done.6
  12.4 0.0 copy-done.7
  12.4 0.0 copy-done.8
  12.4 6.3 %elements.1 = bf16[384,128]{1,0:T(8,128)(2,1)S(1)} custom-call(s32[2,32]{1,0:T(2,128)S(1)} %copy-done.3, bf16[1920,256]{1,0:T(8,128)(2,1)S(1)} %bitcast.11, bf16[2,210,120]{2,1,0:T(8,128)(2,1)S(1)} %bitcast.12, bf16[1,35,35]{2,1,0:T(8,128)(2,1)S(1)} %copy-done.2, s32[4,128]{1,0:T(4,128)S(1)} %copy-done.4, f32[1,128]{1,0:T(1,128)S(1)} %bitcast.15, ...), custom_call_target="tpu_custom_call" | custom-call | tf_op jit(solution)/shard_map/elements/pallas_call | solution.py:237
  18.8 13.5 %all_to_all.11 = bf16[8,48,128]{2,1,0:T(8,128)(2,1)S(1)} all-to-all(bf16[8,48,128]{2,1,0:T(8,128)(2,1)S(1)} %bitcast.13), channel_id=1, replica_groups=mesh['groups'=2,'dom'=4,'sub'=2,'rhs'=2] {'dom','sub'}, dimensions={0} | all-to-all | bytes 196608 | tf_op jit(solution)/shard_map/all_to_all | solution.py:257
  32.3 0.9 %voxels.1 = f32[96,128]{1,0:T(8,128)} custom-call(bf16[384,128]{1,0:T(8,128)(2,1)S(1)} %bitcast.14), custom_call_target="tpu_custom_call" | custom-call | tf_op jit(solution)/shard_map/voxels/pallas_call | solution.py:258
Async XLA Ops:
  0.0 0.7 %copy-start.3 = (s32[2,32]{1,0:T(2,128)S(1)}, s32[2,32]{1,0:T(2,128)}, u32[]{:S(2)}) copy-start(s32[2,32]{1,0:T(2,128)} %refs_0_.3) | copy-start | bytes 772
  0.7 1.2 %copy-start = (bf16[2,2,30,16,256]{4,3,2,1,0:T(8,128)(2,1)S(1)}, bf16[2,2,30,16,256]{4,3,2,1,0:T(8,128)(2,1)}, u32[]{:S(2)}) copy-start(bf16[2,2,30,16,256]{4,3,2,1,0:T(8,128)(2,1)} %param.9) | copy-start | bytes 2949124
  1.9 0.7 %copy-start.5 = (s32[2,32]{1,0:T(2,128)S(1)}, s32[2,32]{1,0:T(2,128)}, u32[]{:S(2)}) copy-start(s32[2,32]{1,0:T(2,128)} %refs_0_.2) | copy-start | bytes 772
  2.6 9.2 %copy-start.1 = (bf16[2,2,30,16,256]{4,3,2,1,0:T(8,128)(2,1)S(1)}, bf16[2,2,30,16,256]{4,3,2,1,0:T(8,128)(2,1)}, u32[]{:S(2)}) copy-start(bf16[2,2,30,16,256]{4,3,2,1,0:T(8,128)(2,1)} %param.9) | copy-start | bytes 2949124
  3.0 6.4 %collective-permute-start = (bf16[32,1920]{1,0:T(8,128)(2,1)S(1)}, bf16[32,1920]{1,0:T(8,128)(2,1)S(1)}, u32[]{:S(2)}, u32[]{:S(2)}) collective-permute-start(bf16[32,1920]{1,0:T(8,128)(2,1)S(1)} %get-tuple-element.8), channel_id=1, source_target_pairs={{0,4},{8,12},{4,0},{12,8},{1,5},{9,13},{5,1},{13,9},{2,6},{10,14},... | collective-permute-start | bytes 368648 | tf_op jit(solution)/shard_map/ppermute | solution.py:230
  6.1 3.3 %collective-permute-start.1 = (bf16[32,1920]{1,0:T(8,128)(2,1)S(1)}, bf16[32,1920]{1,0:T(8,128)(2,1)S(1)}, u32[]{:S(2)}, u32[]{:S(2)}) collective-permute-start(bf16[32,1920]{1,0:T(8,128)(2,1)S(1)} %get-tuple-element.9), channel_id=1, source_target_pairs={{4,8},{8,4},{5,9},{9,5},{6,10},{10,6},{7,11},{11,7},{20,24},{24,20... | collective-permute-start | bytes 368648 | tf_op jit(solution)/shard_map/ppermute | solution.py:230
  6.8 4.9 %collective-permute-start.2 = (bf16[32,1920]{1,0:T(8,128)(2,1)S(1)}, bf16[32,1920]{1,0:T(8,128)(2,1)S(1)}, u32[]{:S(2)}, u32[]{:S(2)}) collective-permute-start(bf16[32,1920]{1,0:T(8,128)(2,1)S(1)} %get-tuple-element.10), channel_id=1, source_target_pairs={{0,2},{2,0},{1,3},{3,1},{4,6},{6,4},{5,7},{7,5},{8,10},{10,8},{9,1... | collective-permute-start | bytes 368648 | tf_op jit(solution)/shard_map/ppermute | solution.py:235
  8.3 3.4 %copy-start.2 = (bf16[1,35,35]{2,1,0:T(8,128)(2,1)S(1)}, bf16[1,35,35]{2,1,0:T(8,128)(2,1)}, u32[]{:S(2)}) copy-start(bf16[1,35,35]{2,1,0:T(8,128)(2,1)} %refs_3_.1) | copy-start | bytes 7354
  11.7 0.7 %copy-start.4 = (s32[4,128]{1,0:T(4,128)S(1)}, s32[4,128]{1,0:T(4,128)}, u32[]{:S(2)}) copy-start(s32[4,128]{1,0:T(4,128)} %refs_4_.1) | copy-start | bytes 6148
  11.7 0.7 %copy-start.6 = (f32[128]{0:T(128)S(1)}, f32[128]{0:T(128)}, u32[]{:S(2)}) copy-start(f32[128]{0:T(128)} %param.15) | copy-start | bytes 1540
  11.7 0.7 %copy-start.7 = (s32[128,1]{0,1:T(1,128)S(1)}, s32[128,1]{0,1:T(1,128)}, u32[]{:S(2)}) copy-start(s32[128,1]{0,1:T(1,128)} %param.16) | copy-start | bytes 1540
  11.7 0.7 %copy-start.8 = (s32[128]{0:T(128)S(1)}, s32[128]{0:T(128)}, u32[]{:S(2)}) copy-start(s32[128]{0:T(128)} %param.17) | copy-start | bytes 1540

commit v2 on v1

--- a/solution.py
+++ b/solution.py
@@ -12,7 +12,10 @@
 GROUP = 40
 NODES = 30
 BLOCK = 256
-VMEM_LIMIT = 48 * 1024 * 1024
+N_INPUTS = 9
+CHUNKS = 5
+UNROLL = 1
+VMEM_LIMIT = 24 * 1024 * 1024
 
 NT = (((1,), (1,)), ((), ()))
 NN = (((1,), (0,)), ((), ()))
@@ -37,8 +40,29 @@
     return lax.rem(index + k, size), lax.rem(index + size - k, size)
 
 
-def pack_kernel(n_sub, rows, dom_ref, sub_ref, traces_ref, *out_refs):
-    faces = traces_ref.shape[1]
+def pack_kernel(n_sub, rows, *refs):
+    hbm_refs, refs = refs[:N_INPUTS], refs[N_INPUTS:]
+    vmem_refs, refs = refs[:N_INPUTS], refs[N_INPUTS:]
+    out_refs, (sems, chunk_sems) = refs[: n_sub + 1], refs[n_sub + 1 :]
+    copies = [
+        pltpu.make_async_copy(hbm_refs[i], vmem_refs[i], sems.at[i]) for i in range(1, N_INPUTS)
+    ]
+    for copy in copies[:2]:
+        copy.start()
+    table_ref, dom_ref, sub_ref = vmem_refs[:3]
+    values, faces = table_ref.shape
+    step = values // CHUNKS
+    chunks = []
+    for k in range(CHUNKS):
+        part = pl.ds(k * step, step)
+        chunks.append(
+            pltpu.make_async_copy(hbm_refs[0].at[part, :], table_ref.at[part, :], chunk_sems.at[k])
+        )
+        chunks[k].start()
+    for copy in copies[2:]:
+        copy.start()
+    for copy in copies[:2]:
+        copy.wait()
     parity = lax.rem(lax.axis_index("dom"), 2)
     within = lax.axis_index("sub")
     lists = [dom_ref[pl.ds(1 - parity, 1), :], dom_ref[pl.ds(parity, 1), :]]
@@ -47,31 +71,48 @@
     face = iota((faces, rows), 0)
     picks = [jnp.where(face == row, 1.0, 0.0).T for row in lists]
     picks = jnp.concatenate(picks, axis=0).astype(jnp.bfloat16)
-    packed = dot(picks, traces_ref[...], NT).astype(jnp.bfloat16)
-    for k, out_ref in enumerate(out_refs):
-        out_ref[...] = packed[k * rows : (k + 1) * rows]
-
-
-def element_kernel(
+    for k in range(CHUNKS):
+        chunks[k].wait()
+        part = slice(k * step, (k + 1) * step)
+        packed = dot(picks, table_ref[part, :], NT).astype(jnp.bfloat16)
+        for i, out_ref in enumerate(out_refs):
+            out_ref[:, part] = packed[i * rows : (i + 1) * rows]
+    for copy in copies[2:]:
+        copy.wait()
+
+
+def reorder_matrix(columns):
+    per_block = BLOCK // columns
+    row = iota((BLOCK, BLOCK), 0)
+    col = iota((BLOCK, BLOCK), 1)
+    return one_hot(lax.rem(row, per_block) * columns + lax.div(row, per_block) == col)
+
+
+def block_starts(columns):
+    half = 2 * NODES * columns
+    return [a * half - (a * half) % 128 + b * BLOCK for a in range(2) for b in range(4)]
+
+
+def prepare_kernel(
     n_sub,
     capacity,
     columns,
     sub_ref,
-    traces_ref,
+    table_ref,
     solver_ref,
     mass_ref,
     elem_ref,
-    volume_ref,
     owner_ref,
-    slot_ref,
-    *refs,
+    own_ref,
+    halo_ref,
+    matrix_ref,
+    masses_ref,
+    sends_ref,
 ):
-    halo_refs = refs[: n_sub + 1]
-    out_ref, gathered_ref, sums_ref = refs[n_sub + 1 :]
-    faces = traces_ref.shape[1]
+    faces = table_ref.shape[1]
     elems = elem_ref.shape[1]
     rows = sub_ref.shape[1]
-    slots = out_ref.shape[0]
+    slots = sends_ref.shape[0]
     parity = lax.rem(lax.axis_index("dom"), 2)
     within = lax.axis_index("sub")
     face_rows = [elem_ref[f : f + 1, :] for f in range(4)]
@@ -89,27 +130,15 @@
     blocks = [1 - parity, parity]
     for k in range(1, n_sub):
         blocks.append(2 + pair_index(within, k, n_sub)[1])
-    halo = [picks(rows, faces + block * rows).astype(jnp.bfloat16) for block in blocks]
-    table = jnp.concatenate([own] + halo, axis=0)
-
-    per_block = BLOCK // columns
-    row = iota((BLOCK, BLOCK), 0)
-    col = iota((BLOCK, BLOCK), 1)
-    reorder = one_hot(
-        lax.rem(row, per_block) * columns + lax.div(row, per_block) == col
-    )
-    half = 2 * NODES * columns
-    starts = []
-    for a in range(2):
-        first = a * half - (a * half) % 128
-        starts += [first + b * BLOCK for b in range(4)]
-    halo_rows = jnp.concatenate([ref[...] for ref in halo_refs], axis=0)
-    for b, start in enumerate(starts):
-        mine = dot(reorder, traces_ref[start : start + BLOCK, :])
-        others = dot(reorder, halo_rows[:, start : start + BLOCK], NT)
-        both = jnp.concatenate([mine, others], axis=1).astype(jnp.bfloat16)
-        got = dot(both, table).astype(jnp.bfloat16)
-        gathered_ref[b] = got.reshape(columns, per_block, 4 * elems)
+    for i, block in enumerate(blocks):
+        halo_ref[i * rows : (i + 1) * rows, :] = picks(rows, faces + block * rows).astype(
+            jnp.bfloat16
+        )
+
+    reorder = reorder_matrix(columns)
+    for b, start in enumerate(block_starts(columns)):
+        mine = dot(reorder, table_ref[start : start + BLOCK, :]).astype(jnp.bfloat16)
+        own_ref[b] = dot(mine, own).astype(jnp.bfloat16)
 
     place = iota((3 * GROUP, HALF), 0)
     source = iota((3 * GROUP, HALF), 1)
@@ -117,9 +146,10 @@
         (lax.div(place, GROUP) == lax.div(source, BASIS))
         & (lax.rem(place, GROUP) == lax.rem(source, BASIS))
     )
-    real = dot(spread, solver_ref[0, :HALF, :]).astype(jnp.bfloat16)
-    imag = dot(spread, solver_ref[1, :HALF, :]).astype(jnp.bfloat16)
-    matrices = []
+    solver = solver_ref[:HALF].astype(jnp.float32)
+    real = dot(spread, solver[:, 0, :].astype(jnp.bfloat16)).astype(jnp.bfloat16)
+    imag = dot(spread, solver[:, 1, :].astype(jnp.bfloat16)).astype(jnp.bfloat16)
+    half = 2 * NODES * columns
     for a in range(2):
         shift = ((a * half) % 128) // columns
         source = iota((4 * NODES, BLOCK), 0)
@@ -129,16 +159,48 @@
         for_imag = one_hot(target + NODES == place)
         top = dot(real, for_real) - dot(imag, for_imag)
         bottom = dot(imag, for_real) + dot(real, for_imag)
-        matrices.append(jnp.concatenate([top, bottom], axis=0).astype(jnp.bfloat16))
+        matrix_ref[a] = jnp.concatenate([top, bottom], axis=0).astype(jnp.bfloat16)
 
     size = 6 * GROUP
     spread = one_hot(lax.rem(iota((size, BASIS), 0), GROUP) == iota((size, BASIS), 1))
-    tiles = dot(dot(spread, mass_ref[0]).astype(jnp.bfloat16), spread, NT)
+    tiles = dot(dot(spread, mass_ref[...]).astype(jnp.bfloat16), spread, NT)
     row = iota((size, size), 0)
     col = iota((size, size), 1)
     tiles = jnp.where(lax.div(row, GROUP) == lax.div(col, GROUP), tiles, 0.0)
-    masses = jnp.where(row < 3 * GROUP, tiles, -tiles).astype(jnp.bfloat16)
-
+    masses_ref[...] = jnp.where(row < 3 * GROUP, tiles, -tiles).astype(jnp.bfloat16)
+
+    owner = owner_ref[...]
+    owners = iota((max(8, slots // capacity), elems), 0) == owner
+    earlier = one_hot(iota((elems, elems), 0) < iota((elems, elems), 1))
+    counts = dot(one_hot(owners), earlier)
+    rank = jnp.sum(jnp.where(owners, counts, 0.0), axis=0, keepdims=True)
+    target = owner * capacity + rank.astype(jnp.int32)
+    sends_ref[...] = one_hot(iota((slots, elems), 0) == target)
+
+
+def element_kernel(
+    columns,
+    volume_ref,
+    slot_ref,
+    own_ref,
+    halo_ref,
+    matrix_ref,
+    masses_ref,
+    sends_ref,
+    *refs,
+):
+    halo_refs = refs[:-3]
+    out_ref, gathered_ref, sums_ref = refs[-3:]
+    elems = volume_ref.shape[1]
+    per_block = BLOCK // columns
+    reorder = reorder_matrix(columns)
+    halo_rows = jnp.concatenate([ref[...] for ref in halo_refs], axis=0)
+    for b, start in enumerate(block_starts(columns)):
+        others = dot(reorder, halo_rows[:, start : start + BLOCK], NT).astype(jnp.bfloat16)
+        got = own_ref[b] + dot(others, halo_ref[...]).astype(jnp.bfloat16)
+        gathered_ref[b] = got.reshape(columns, per_block, 4 * elems)
+
+    masses = masses_ref[...]
     pairs = [(0, 0), (1, 1), (2, 2), (0, 1), (0, 2), (1, 2)]
 
     def step(index, carry):
@@ -157,7 +219,7 @@
                         axis=0,
                     )
                 )
-            values = dot(matrices[a], jnp.concatenate(parts, axis=1))
+            values = dot(matrix_ref[a], jnp.concatenate(parts, axis=1))
             fields.append(values.astype(jnp.bfloat16))
         weighted = dot(masses, fields[0])
         shape = (2, 3, GROUP // 8, 8, 2 * elems)
@@ -173,7 +235,7 @@
                 sums_ref[pl.ds(start, 8), :] = total[:, c * elems : (c + 1) * elems]
         return carry
 
-    lax.fori_loop(0, columns // 2, step, 0)
+    lax.fori_loop(0, columns // 2, step, 0, unroll=UNROLL)
 
     width = 6 * columns
     total = sums_ref[pl.ds(0, width, stride=8), :]
@@ -182,17 +244,9 @@
     norm = 1.0 / math.sqrt(70.0)
     factor = jnp.where(iota((width, 1), 0) < 3 * columns, norm, 0.5 * norm)
     terms = total * (factor * volume_ref[...])
-
-    owner = owner_ref[...]
-    owners = iota((max(8, slots // capacity), elems), 0) == owner
-    earlier = one_hot(iota((elems, elems), 0) < iota((elems, elems), 1))
-    counts = dot(one_hot(owners), earlier)
-    rank = jnp.sum(jnp.where(owners, counts, 0.0), axis=0, keepdims=True)
-    target = owner * capacity + rank.astype(jnp.int32)
-    sends = one_hot(iota((slots, elems), 0) == target)
     slot = jnp.broadcast_to(slot_ref[...].astype(jnp.float32), (128 - width, elems))
     payload = jnp.concatenate([terms, slot], axis=0).astype(jnp.bfloat16)
-    out_ref[...] = dot(sends, payload, NT).astype(jnp.bfloat16)
+    out_ref[...] = dot(sends_ref[...], payload, NT).astype(jnp.bfloat16)
 
 
 def voxel_kernel(width, got_ref, out_ref):
@@ -217,12 +271,33 @@
     values = table.shape[0]
     params = pltpu.CompilerParams(vmem_limit_bytes=VMEM_LIMIT)
 
-    packed = pl.pallas_call(
+    inputs = [
+        table,
+        dom_lists,
+        sub_lists,
+        solver[0].transpose(1, 0, 2),
+        mass[0],
+        elem_face,
+        volume.reshape(1, elems),
+        elem_owner.reshape(1, elems),
+        elem_slot.reshape(1, elems),
+    ]
+    inputs = [pltpu.with_memory_space_constraint(x, pltpu.HBM) for x in inputs]
+    outs = pl.pallas_call(
         lambda *refs: pack_kernel(n_sub, rows, *refs),
-        out_shape=[jax.ShapeDtypeStruct((rows, values), jnp.bfloat16)] * (n_sub + 1),
+        in_specs=[pl.BlockSpec(memory_space=pltpu.HBM)] * N_INPUTS,
+        out_shape=[pltpu.VMEM(x.shape, x.dtype) for x in inputs]
+        + [pltpu.VMEM((rows, values), jnp.bfloat16)] * (n_sub + 1),
+        out_specs=[pl.BlockSpec(memory_space=pltpu.VMEM)] * (N_INPUTS + n_sub + 1),
+        scratch_shapes=[
+            pltpu.SemaphoreType.DMA((N_INPUTS,)),
+            pltpu.SemaphoreType.DMA((CHUNKS,)),
+        ],
         compiler_params=params,
         name="pack",
-    )(dom_lists, sub_lists, table)
+    )(*inputs)
+    table, _, sub, matrix, mass, elem_face, volume, owner, slot = outs[:N_INPUTS]
+    packed = outs[N_INPUTS:]
 
     even = [(i, i + 1) for i in range(0, n_dom - 1, 2)]
     odd = [(i, i + 1) for i in range(1, n_dom - 1, 2)]
@@ -234,26 +309,32 @@
         pairs = [(i, pair_index(i, k, n_sub)[0]) for i in range(n_sub)]
         halos.append(lax.ppermute(packed[1 + k], "sub", [(i, int(j)) for i, j in pairs]))
 
+    slots = owners * capacity
+    fixed = pl.pallas_call(
+        lambda *refs: prepare_kernel(n_sub, capacity, columns, *refs),
+        out_shape=[
+            jax.ShapeDtypeStruct((8, BLOCK, 4 * elems), jnp.bfloat16),
+            jax.ShapeDtypeStruct(((n_sub + 1) * rows, 4 * elems), jnp.bfloat16),
+            jax.ShapeDtypeStruct((2, 6 * GROUP, BLOCK), jnp.bfloat16),
+            jax.ShapeDtypeStruct((6 * GROUP, 6 * GROUP), jnp.bfloat16),
+            jax.ShapeDtypeStruct((slots, elems), jnp.bfloat16),
+        ],
+        compiler_params=params,
+        cost_estimate=pl.CostEstimate(
+            flops=8 * BLOCK * faces * 8 * elems, bytes_accessed=4 << 20, transcendentals=0
+        ),
+        name="prepare",
+    )(sub, table, matrix, mass, elem_face, owner)
     sent = pl.pallas_call(
-        lambda *refs: element_kernel(n_sub, capacity, columns, *refs),
-        out_shape=jax.ShapeDtypeStruct((owners * capacity, 128), jnp.bfloat16),
+        lambda *refs: element_kernel(columns, *refs),
+        out_shape=jax.ShapeDtypeStruct((slots, 128), jnp.bfloat16),
         scratch_shapes=[
             pltpu.VMEM((8, columns, BLOCK // columns, 4 * elems), jnp.bfloat16),
             pltpu.VMEM((8 * width, elems), jnp.float32),
         ],
         compiler_params=params,
         name="elements",
-    )(
-        sub_lists,
-        table,
-        solver[0],
-        mass,
-        elem_face,
-        volume.reshape(1, elems),
-        elem_owner.reshape(1, elems),
-        elem_slot.reshape(1, elems),
-        *halos,
-    )
+    )(volume, slot, *fixed, *halos)
     got = lax.all_to_all(sent, ("dom", "sub"), split_axis=0, concat_axis=0, tiled=True)
     summed = pl.pallas_call(
         lambda *refs: voxel_kernel(width, *refs),

time: 33.5 us -> 31.2 us (0.931)
  local copies, waits for them, and re-layouts: 4.17 us -> 0 us
  Pallas kernels: 7.69 us -> 11.1 us
  waiting for transfers between devices: 2.46 us -> 1.03 us
    unnamed x19 -> x0, local copies, waits for them, and re-layouts: 4.17 us -> none
    pallas_call x2 -> x3, Pallas kernels: 6.79 us -> 10.2 us  [the longest x1 5.09 us: per_device(): pl.pallas_call(lambda *refs: element_kernel(columns, *refs), out_shape=ja...]
    ppermute x1, waiting for transfers between devices: 2.28 us -> 1.03 us  [per_device(): lax.ppermute(packed[1 + k], 'sub', [(i, int(j)) for i, j in pairs])]
  transfers between devices with their start and end apart: 3 -> 3, of which waited for: 2 -> 1; matrix products, arithmetic and copies ran while one was open for 3% -> 0% of each run, Pallas kernels for 0% -> 8%
where the time goes in v2:
time: 31.2 us; the launch traced here: 31 us
  blocking collectives  13.5 us (43%)
  Pallas kernels  11.1 us (36%)
  starting transfers between devices  5.3 us (17%)
  waiting for transfers between devices  1.03 us (3%)
    all_to_all x1, blocking collectives, per_device(): lax.all_to_all(sent, ('dom', 'sub'), split_axis=0, concat_axis=0, tiled=T...  13.5 us
    pallas_call x1, Pallas kernels, per_device(): pl.pallas_call(lambda *refs: element_kernel(columns, *refs), out_shape=ja...  5.09 us
    ppermute x2, starting transfers between devices, per_device(): lax.ppermute(part, 'dom', pairs + [(j, i) for i, j in pairs])  3.74 us
    pallas_call x1, Pallas kernels, per_device(): pl.pallas_call(lambda *refs: pack_kernel(n_sub, rows, *refs), in_specs=[p...  2.81 us
    pallas_call x1, Pallas kernels, per_device(): pl.pallas_call(lambda *refs: prepare_kernel(n_sub, capacity, columns, *re...  2.33 us
    ppermute x1, starting transfers between devices, per_device(): lax.ppermute(packed[1 + k], 'sub', [(i, int(j)) for i, j in pairs])  1.56 us
    ppermute x1, waiting for transfers between devices, per_device(): lax.ppermute(packed[1 + k], 'sub', [(i, int(j)) for i, j in pairs])  1.03 us
    pallas_call x1, Pallas kernels, per_device(): pl.pallas_call(lambda *refs: voxel_kernel(width, *refs), out_shape=jax.Sh...  0.89 us
  transfers between devices with their start and end apart: 3, of which 1 were waited for; matrix products, arithmetic and copies ran while one was open for 0% of the time, Pallas kernels for 8%

profile of v2, /device:TPU:0, one launch (start us, length us, event | category | flops | bytes accessed | tf_op | source)
XLA Modules:
  0.0 31.0 jit_solution(16018626305155955374)
XLA Ops:
  0.0 2.8 %pack.1 = (bf16[1920,256]{1,0:T(8,128)(2,1)S(1)}, s32[2,32]{1,0:T(2,128)}, s32[2,32]{1,0:T(2,128)S(1)}, bf16[210,2,120]{2,1,0:T(2,128)(2,1)S(1)}, bf16[35,35]{1,...) custom-call(bf16[1920,256]{1,0:T(8,128)(2,1)} %bitcast.13, ...), custom_call_target="tpu_custom_call" | custom-call | tf_op jit(solution)/shard_map/pack/pallas_call | solution.py:286
  2.8 3.1 %collective-permute-start = (bf16[32,1920]{1,0:T(8,128)(2,1)S(1)}, bf16[32,1920]{1,0:T(8,128)(2,1)S(1)}, u32[]{:S(2)}, u32[]{:S(2)}) collective-permute-start(bf16[32,1920]{1,0:T(8,128)(2,1)S(1)} %get-tuple-element.34), channel_id=1, source_target_pairs={{0,4},{8,12},{4,0},{12,8},{1,5},{9,13},{5,1},{13,9},{2,6},{10,14},... | collective-permute-start | bytes 368648 | tf_op jit(solution)/shard_map/ppermute | solution.py:305
  5.9 0.7 %collective-permute-start.1 = (bf16[32,1920]{1,0:T(8,128)(2,1)S(1)}, bf16[32,1920]{1,0:T(8,128)(2,1)S(1)}, u32[]{:S(2)}, u32[]{:S(2)}) collective-permute-start(bf16[32,1920]{1,0:T(8,128)(2,1)S(1)} %get-tuple-element.35), channel_id=1, source_target_pairs={{4,8},{8,4},{5,9},{9,5},{6,10},{10,6},{7,11},{11,7},{20,24},{24,20... | collective-permute-start | bytes 368648 | tf_op jit(solution)/shard_map/ppermute | solution.py:305
  6.6 1.6 %collective-permute-start.2 = (bf16[32,1920]{1,0:T(8,128)(2,1)S(1)}, bf16[32,1920]{1,0:T(8,128)(2,1)S(1)}, u32[]{:S(2)}, u32[]{:S(2)}) collective-permute-start(bf16[32,1920]{1,0:T(8,128)(2,1)S(1)} %get-tuple-element.36), channel_id=1, source_target_pairs={{0,2},{2,0},{1,3},{3,1},{4,6},{6,4},{5,7},{7,5},{8,10},{10,8},{9,1... | collective-permute-start | bytes 368648 | tf_op jit(solution)/shard_map/ppermute | solution.py:310
  8.1 2.3 %prepare.1 = (bf16[8,256,512]{2,1,0:T(8,128)(2,1)S(1)}, bf16[96,512]{1,0:T(8,128)(2,1)S(1)}, bf16[2,240,256]{2,1,0:T(8,128)(2,1)S(1)}, bf16[240,240]{1,0:T(8,128)(2,1)S(1)}, bf16[384,128]{1,0:T(8,128)(2,1)S(1)}) custom-call(s32[2,32]{1,0:T(2,128)S(1)} %get-tuple-element.23.refs_0_, bf16[1920,256]{1,0:T(8,128)(2,1)S(1)} %get-tuple-element.24.refs_1_, ...), custom_call_target="tpu_custom_call" | custom-call | flops 536870912 | bytes 4194304 | tf_op jit(solution)/shard_map/prepare/pallas_call | solution.py:313
  10.5 0.0 collective-permute-done.refs_7_
  10.5 0.0 collective-permute-done.1.refs_8_
  10.5 1.0 %collective-permute-done.2.refs_9_ = bf16[32,1920]{1,0:T(8,128)(2,1)S(1)} collective-permute-done((bf16[32,1920]{1,0:T(8,128)(2,1)S(1)}, bf16[32,1920]{1,0:T(8,128)(2,1)S(1)}, u32[]{:S(2)}, u32[]{:S(2)}) %collective-permute-start.2) | collective-permute-done | bytes 122912 | tf_op jit(solution)/shard_map/ppermute | solution.py:310
  11.5 5.1 %elements.1 = bf16[384,128]{1,0:T(8,128)(2,1)S(1)} custom-call(f32[1,128]{1,0:T(1,128)S(1)} %get-tuple-element.21.refs_0_, s32[1,128]{1,0:T(1,128)S(1)} %get-tuple-element.22.refs_1_, bf16[8,256,512]{2,1,0:T(8,128)(2,1)S(1)} %get-tuple-element.29.refs_2_, bf16[96,512]{1,0:T(8,128)(2,1)S(1)} %get-tuple-element.30.refs_3_, ...), custom_call_target="tpu_custom_call" | custom-call | tf_op jit(solution)/shard_map/elements/pallas_call | solution.py:328
  16.6 13.5 %all_to_all.11 = bf16[8,48,128]{2,1,0:T(8,128)(2,1)S(1)} all-to-all(bf16[8,48,128]{2,1,0:T(8,128)(2,1)S(1)} %bitcast.11), channel_id=1, replica_groups=mesh['groups'=2,'dom'=4,'sub'=2,'rhs'=2] {'dom','sub'}, dimensions={0} | all-to-all | bytes 196608 | tf_op jit(solution)/shard_map/all_to_all | solution.py:338
  30.1 0.9 %voxels.1 = f32[96,128]{1,0:T(8,128)} custom-call(bf16[384,128]{1,0:T(8,128)(2,1)S(1)} %bitcast.12), custom_call_target="tpu_custom_call" | custom-call | tf_op jit(solution)/shard_map/voxels/pallas_call | solution.py:339
Async XLA Ops:
  2.8 7.7 %collective-permute-start = (bf16[32,1920]{1,0:T(8,128)(2,1)S(1)}, bf16[32,1920]{1,0:T(8,128)(2,1)S(1)}, u32[]{:S(2)}, u32[]{:S(2)}) collective-permute-start(bf16[32,1920]{1,0:T(8,128)(2,1)S(1)} %get-tuple-element.34), channel_id=1, source_target_pairs={{0,4},{8,12},{4,0},{12,8},{1,5},{9,13},{5,1},{13,9},{2,6},{10,14},... | collective-permute-start | bytes 368648 | tf_op jit(solution)/shard_map/ppermute | solution.py:305
  5.9 4.6 %collective-permute-start.1 = (bf16[32,1920]{1,0:T(8,128)(2,1)S(1)}, bf16[32,1920]{1,0:T(8,128)(2,1)S(1)}, u32[]{:S(2)}, u32[]{:S(2)}) collective-permute-start(bf16[32,1920]{1,0:T(8,128)(2,1)S(1)} %get-tuple-element.35), channel_id=1, source_target_pairs={{4,8},{8,4},{5,9},{9,5},{6,10},{10,6},{7,11},{11,7},{20,24},{24,20... | collective-permute-start | bytes 368648 | tf_op jit(solution)/shard_map/ppermute | solution.py:305
  6.6 4.9 %collective-permute-start.2 = (bf16[32,1920]{1,0:T(8,128)(2,1)S(1)}, bf16[32,1920]{1,0:T(8,128)(2,1)S(1)}, u32[]{:S(2)}, u32[]{:S(2)}) collective-permute-start(bf16[32,1920]{1,0:T(8,128)(2,1)S(1)} %get-tuple-element.36), channel_id=1, source_target_pairs={{0,2},{2,0},{1,3},{3,1},{4,6},{6,4},{5,7},{7,5},{8,10},{10,8},{9,1... | collective-permute-start | bytes 368648 | tf_op jit(solution)/shard_map/ppermute | solution.py:310

commit v3 on v2

--- a/solution.py
+++ b/solution.py
@@ -14,7 +14,7 @@
 BLOCK = 256
 N_INPUTS = 9
 CHUNKS = 5
-UNROLL = 1
+UNROLL = 8
 VMEM_LIMIT = 24 * 1024 * 1024
 
 NT = (((1,), (1,)), ((), ()))
@@ -104,7 +104,7 @@
     elem_ref,
     owner_ref,
     own_ref,
-    halo_ref,
+    places_ref,
     matrix_ref,
     masses_ref,
     sends_ref,
@@ -130,10 +130,11 @@
     blocks = [1 - parity, parity]
     for k in range(1, n_sub):
         blocks.append(2 + pair_index(within, k, n_sub)[1])
+    place = jnp.full(elem_ref.shape, -1, jnp.int32)
     for i, block in enumerate(blocks):
-        halo_ref[i * rows : (i + 1) * rows, :] = picks(rows, faces + block * rows).astype(
-            jnp.bfloat16
-        )
+        offset = elem_ref[...] - (faces + block * rows)
+        place = jnp.where((offset >= 0) & (offset < rows), offset + i * rows, place)
+    places_ref[...] = place
 
     reorder = reorder_matrix(columns)
     for b, start in enumerate(block_starts(columns)):
@@ -183,7 +184,7 @@
     volume_ref,
     slot_ref,
     own_ref,
-    halo_ref,
+    places_ref,
     matrix_ref,
     masses_ref,
     sends_ref,
@@ -194,11 +195,31 @@
     elems = volume_ref.shape[1]
     per_block = BLOCK // columns
     reorder = reorder_matrix(columns)
-    halo_rows = jnp.concatenate([ref[...] for ref in halo_refs], axis=0)
+    halo_rows = [ref[...] for ref in halo_refs]
+    count = sum(rows.shape[0] for rows in halo_rows)
+    tiles = -(-count // 128)
+    halo_rows.append(jnp.zeros((tiles * 128 - count, halo_rows[0].shape[1]), jnp.bfloat16))
+    halo_rows = jnp.concatenate(halo_rows, axis=0)
+    lanes, inside = [], []
+    for f in range(4):
+        place = jnp.broadcast_to(places_ref[f : f + 1, :], (BLOCK, elems))
+        for t in range(tiles):
+            lanes.append(jnp.clip(place - t * 128, 0, 127))
+            inside.append((place >= t * 128) & (place < (t + 1) * 128))
     for b, start in enumerate(block_starts(columns)):
-        others = dot(reorder, halo_rows[:, start : start + BLOCK], NT).astype(jnp.bfloat16)
-        got = own_ref[b] + dot(others, halo_ref[...]).astype(jnp.bfloat16)
-        gathered_ref[b] = got.reshape(columns, per_block, 4 * elems)
+        others = dot(reorder, halo_rows[:, start : start + BLOCK], NT)
+        for f in range(4):
+            part = slice(f * elems, (f + 1) * elems)
+            got = own_ref[b, :, part]
+            for t in range(tiles):
+                found = jnp.take_along_axis(
+                    others[:, t * 128 : (t + 1) * 128],
+                    lanes[f * tiles + t],
+                    axis=1,
+                    mode="promise_in_bounds",
+                )
+                got = got + jnp.where(inside[f * tiles + t], found, 0.0).astype(jnp.bfloat16)
+            gathered_ref[b, :, :, part] = got.reshape(columns, per_block, elems)
 
     masses = masses_ref[...]
     pairs = [(0, 0), (1, 1), (2, 2), (0, 1), (0, 2), (1, 2)]
@@ -314,7 +335,7 @@
         lambda *refs: prepare_kernel(n_sub, capacity, columns, *refs),
         out_shape=[
             jax.ShapeDtypeStruct((8, BLOCK, 4 * elems), jnp.bfloat16),
-            jax.ShapeDtypeStruct(((n_sub + 1) * rows, 4 * elems), jnp.bfloat16),
+            jax.ShapeDtypeStruct((4, elems), jnp.int32),
             jax.ShapeDtypeStruct((2, 6 * GROUP, BLOCK), jnp.bfloat16),
             jax.ShapeDtypeStruct((6 * GROUP, 6 * GROUP), jnp.bfloat16),
             jax.ShapeDtypeStruct((slots, elems), jnp.bfloat16),

time: 31.2 us -> 28.4 us (0.910)
  Pallas kernels: 11.1 us -> 8.29 us
    pallas_call x1, Pallas kernels: 5.09 us -> 2.26 us  [per_device(): pl.pallas_call(lambda *refs: element_kernel(columns, *refs), out_shape=ja...]
where the time goes in v3:
time: 28.4 us; the launch traced here: 28.2 us
  blocking collectives  13.5 us (48%)
  Pallas kernels  8.29 us (29%)
  starting transfers between devices  5.3 us (19%)
  waiting for transfers between devices  1.04 us (4%)
    all_to_all x1, blocking collectives, per_device(): lax.all_to_all(sent, ('dom', 'sub'), split_axis=0, concat_axis=0, tiled=T...  13.5 us
    ppermute x2, starting transfers between devices, per_device(): lax.ppermute(part, 'dom', pairs + [(j, i) for i, j in pairs])  3.74 us
    pallas_call x1, Pallas kernels, per_device(): pl.pallas_call(lambda *refs: pack_kernel(n_sub, rows, *refs), in_specs=[p...  2.81 us
    pallas_call x1, Pallas kernels, per_device(): pl.pallas_call(lambda *refs: prepare_kernel(n_sub, capacity, columns, *re...  2.32 us
    pallas_call x1, Pallas kernels, per_device(): pl.pallas_call(lambda *refs: element_kernel(columns, *refs), out_shape=ja...  2.26 us
    ppermute x1, starting transfers between devices, per_device(): lax.ppermute(packed[1 + k], 'sub', [(i, int(j)) for i, j in pairs])  1.56 us
    ppermute x1, waiting for transfers between devices, per_device(): lax.ppermute(packed[1 + k], 'sub', [(i, int(j)) for i, j in pairs])  1.04 us
    pallas_call x1, Pallas kernels, per_device(): pl.pallas_call(lambda *refs: voxel_kernel(width, *refs), out_shape=jax.Sh...  0.89 us
  transfers between devices with their start and end apart: 3, of which 1 were waited for; matrix products, arithmetic and copies ran while one was open for 0% of the time, Pallas kernels for 8%

profile of v3, /device:TPU:0, one launch (start us, length us, event | category | flops | bytes accessed | tf_op | source)
XLA Modules:
  0.0 28.2 jit_solution(18122910593906151572)
XLA Ops:
  0.0 2.8 %pack.1 = (bf16[1920,256]{1,0:T(8,128)(2,1)S(1)}, s32[2,32]{1,0:T(2,128)}, s32[2,32]{1,0:T(2,128)S(1)}, bf16[210,2,120]{2,1,0:T(2,128)(2,1)S(1)}, bf16[35,35]{1,...) custom-call(bf16[1920,256]{1,0:T(8,128)(2,1)} %bitcast.13, ...), custom_call_target="tpu_custom_call" | custom-call | tf_op jit(solution)/shard_map/pack/pallas_call | solution.py:307
  2.8 3.1 %collective-permute-start = (bf16[32,1920]{1,0:T(8,128)(2,1)S(1)}, bf16[32,1920]{1,0:T(8,128)(2,1)S(1)}, u32[]{:S(2)}, u32[]{:S(2)}) collective-permute-start(bf16[32,1920]{1,0:T(8,128)(2,1)S(1)} %get-tuple-element.34), channel_id=1, source_target_pairs={{0,4},{8,12},{4,0},{12,8},{1,5},{9,13},{5,1},{13,9},{2,6},{10,14},... | collective-permute-start | bytes 368648 | tf_op jit(solution)/shard_map/ppermute | solution.py:326
  5.9 0.7 %collective-permute-start.1 = (bf16[32,1920]{1,0:T(8,128)(2,1)S(1)}, bf16[32,1920]{1,0:T(8,128)(2,1)S(1)}, u32[]{:S(2)}, u32[]{:S(2)}) collective-permute-start(bf16[32,1920]{1,0:T(8,128)(2,1)S(1)} %get-tuple-element.35), channel_id=1, source_target_pairs={{4,8},{8,4},{5,9},{9,5},{6,10},{10,6},{7,11},{11,7},{20,24},{24,20... | collective-permute-start | bytes 368648 | tf_op jit(solution)/shard_map/ppermute | solution.py:326
  6.6 1.6 %collective-permute-start.2 = (bf16[32,1920]{1,0:T(8,128)(2,1)S(1)}, bf16[32,1920]{1,0:T(8,128)(2,1)S(1)}, u32[]{:S(2)}, u32[]{:S(2)}) collective-permute-start(bf16[32,1920]{1,0:T(8,128)(2,1)S(1)} %get-tuple-element.36), channel_id=1, source_target_pairs={{0,2},{2,0},{1,3},{3,1},{4,6},{6,4},{5,7},{7,5},{8,10},{10,8},{9,1... | collective-permute-start | bytes 368648 | tf_op jit(solution)/shard_map/ppermute | solution.py:331
  8.1 2.3 %prepare.1 = (bf16[8,256,512]{2,1,0:T(8,128)(2,1)S(1)}, s32[4,128]{1,0:T(4,128)S(1)}, bf16[2,240,256]{2,1,0:T(8,128)(2,1)S(1)}, bf16[240,240]{1,0:T(8,128)(2,1)S(1)}, bf16[384,128]{1,0:T(8,128)(2,1)S(1)}) custom-call(s32[2,32]{1,0:T(2,128)S(1)} %get-tuple-element.23.refs_0_, bf16[1920,256]{1,0:T(8,128)(2,1)S(1)} %get-tuple-element.24.refs_1_, ...), custom_call_target="tpu_custom_call" | custom-call | flops 536870912 | bytes 4194304 | tf_op jit(solution)/shard_map/prepare/pallas_call | solution.py:334
  10.5 0.0 collective-permute-done.refs_7_
  10.5 0.0 collective-permute-done.1.refs_8_
  10.5 1.0 %collective-permute-done.2.refs_9_ = bf16[32,1920]{1,0:T(8,128)(2,1)S(1)} collective-permute-done((bf16[32,1920]{1,0:T(8,128)(2,1)S(1)}, bf16[32,1920]{1,0:T(8,128)(2,1)S(1)}, u32[]{:S(2)}, u32[]{:S(2)}) %collective-permute-start.2) | collective-permute-done | bytes 122912 | tf_op jit(solution)/shard_map/ppermute | solution.py:331
  11.5 2.3 %elements.1 = bf16[384,128]{1,0:T(8,128)(2,1)S(1)} custom-call(f32[1,128]{1,0:T(1,128)S(1)} %get-tuple-element.21.refs_0_, s32[1,128]{1,0:T(1,128)S(1)} %get-tuple-element.22.refs_1_, bf16[8,256,512]{2,1,0:T(8,128)(2,1)S(1)} %get-tuple-element.29.refs_2_, s32[4,128]{1,0:T(4,128)S(1)} %get-tuple-element.30.refs_3_, ...), custom_call_target="tpu_custom_call" | custom-call | tf_op jit(solution)/shard_map/elements/pallas_call | solution.py:349
  13.8 13.5 %all_to_all.11 = bf16[8,48,128]{2,1,0:T(8,128)(2,1)S(1)} all-to-all(bf16[8,48,128]{2,1,0:T(8,128)(2,1)S(1)} %bitcast.11), channel_id=1, replica_groups=mesh['groups'=2,'dom'=4,'sub'=2,'rhs'=2] {'dom','sub'}, dimensions={0} | all-to-all | bytes 196608 | tf_op jit(solution)/shard_map/all_to_all | solution.py:359
  27.3 0.9 %voxels.1 = f32[96,128]{1,0:T(8,128)} custom-call(bf16[384,128]{1,0:T(8,128)(2,1)S(1)} %bitcast.12), custom_call_target="tpu_custom_call" | custom-call | tf_op jit(solution)/shard_map/voxels/pallas_call | solution.py:360
Async XLA Ops:
  2.8 7.6 %collective-permute-start = (bf16[32,1920]{1,0:T(8,128)(2,1)S(1)}, bf16[32,1920]{1,0:T(8,128)(2,1)S(1)}, u32[]{:S(2)}, u32[]{:S(2)}) collective-permute-start(bf16[32,1920]{1,0:T(8,128)(2,1)S(1)} %get-tuple-element.34), channel_id=1, source_target_pairs={{0,4},{8,12},{4,0},{12,8},{1,5},{9,13},{5,1},{13,9},{2,6},{10,14},... | collective-permute-start | bytes 368648 | tf_op jit(solution)/shard_map/ppermute | solution.py:326
  5.9 4.6 %collective-permute-start.1 = (bf16[32,1920]{1,0:T(8,128)(2,1)S(1)}, bf16[32,1920]{1,0:T(8,128)(2,1)S(1)}, u32[]{:S(2)}, u32[]{:S(2)}) collective-permute-start(bf16[32,1920]{1,0:T(8,128)(2,1)S(1)} %get-tuple-element.35), channel_id=1, source_target_pairs={{4,8},{8,4},{5,9},{9,5},{6,10},{10,6},{7,11},{11,7},{20,24},{24,20... | collective-permute-start | bytes 368648 | tf_op jit(solution)/shard_map/ppermute | solution.py:326
  6.6 4.9 %collective-permute-start.2 = (bf16[32,1920]{1,0:T(8,128)(2,1)S(1)}, bf16[32,1920]{1,0:T(8,128)(2,1)S(1)}, u32[]{:S(2)}, u32[]{:S(2)}) collective-permute-start(bf16[32,1920]{1,0:T(8,128)(2,1)S(1)} %get-tuple-element.36), channel_id=1, source_target_pairs={{0,2},{2,0},{1,3},{3,1},{4,6},{6,4},{5,7},{7,5},{8,10},{10,8},{9,1... | collective-permute-start | bytes 368648 | tf_op jit(solution)/shard_map/ppermute | solution.py:331

commit v4 on v3

--- a/solution.py
+++ b/solution.py
@@ -13,7 +13,7 @@
 NODES = 30
 BLOCK = 256
 N_INPUTS = 9
-CHUNKS = 5
+CHUNKS = 1
 UNROLL = 8
 VMEM_LIMIT = 24 * 1024 * 1024
 
@@ -320,12 +320,20 @@
     table, _, sub, matrix, mass, elem_face, volume, owner, slot = outs[:N_INPUTS]
     packed = outs[N_INPUTS:]
 
-    even = [(i, i + 1) for i in range(0, n_dom - 1, 2)]
-    odd = [(i, i + 1) for i in range(1, n_dom - 1, 2)]
-    halos = [
-        lax.ppermute(part, "dom", pairs + [(j, i) for i, j in pairs])
-        for part, pairs in zip(packed, (even, odd))
-    ]
+    n_rhs = lax.axis_size("rhs")
+    halos = []
+    for odd, part in enumerate(packed[:2]):
+        pairs = []
+        for d in range(n_dom):
+            other = d + 1 if (d - odd) % 2 == 0 else d - 1
+            inside = 0 <= other < n_dom
+            for s in range(n_sub):
+                for c in range(n_rhs):
+                    target = (other * n_sub + s) * n_rhs + c
+                    if not inside:
+                        target = (d * n_sub + s) * n_rhs + n_rhs - 1 - c
+                    pairs.append(((d * n_sub + s) * n_rhs + c, target))
+        halos.append(lax.ppermute(part, ("dom", "sub", "rhs"), pairs))
     for k in range(1, n_sub):
         pairs = [(i, pair_index(i, k, n_sub)[0]) for i in range(n_sub)]
         halos.append(lax.ppermute(packed[1 + k], "sub", [(i, int(j)) for i, j in pairs]))

time: 28.4 us -> 26.2 us (0.923)
  blocking collectives: 13.5 us -> 11.6 us
  waiting for transfers between devices: 1.04 us -> 1.9 us
  starting transfers between devices: 5.3 us -> 4.58 us
  Pallas kernels: 8.29 us -> 7.87 us
    all_to_all x1, blocking collectives: 13.5 us -> 11.6 us  [per_device(): lax.all_to_all(sent, ('dom', 'sub'), split_axis=0, concat_axis=0, tiled=T...]
    ppermute x1, waiting for transfers between devices: 1.04 us -> 1.89 us  [per_device(): lax.ppermute(packed[1 + k], 'sub', [(i, int(j)) for i, j in pairs])]
    ppermute x2, starting transfers between devices: 3.74 us -> 3.09 us  [per_device(): halos.append(lax.ppermute(part, ('dom', 'sub', 'rhs'), pairs))]
    pallas_call x1, Pallas kernels: 2.81 us -> 2.39 us  [per_device(): pl.pallas_call(lambda *refs: pack_kernel(n_sub, rows, *refs), in_specs=[p...]
  transfers between devices with their start and end apart: 3 -> 3, of which waited for: 1 -> 1; matrix products, arithmetic and copies ran while one was open for 0% -> 0% of each run, Pallas kernels for 8% -> 9%
where the time goes in v4:
time: 26.2 us; the launch traced here: 26 us
  blocking collectives  11.6 us (44%)
  Pallas kernels  7.87 us (30%)
  starting transfers between devices  4.58 us (17%)
  waiting for transfers between devices  1.9 us (7%)
    all_to_all x1, blocking collectives, per_device(): lax.all_to_all(sent, ('dom', 'sub'), split_axis=0, concat_axis=0, tiled=T...  11.6 us
    ppermute x2, starting transfers between devices, per_device(): halos.append(lax.ppermute(part, ('dom', 'sub', 'rhs'), pairs))  3.09 us
    pallas_call x1, Pallas kernels, per_device(): pl.pallas_call(lambda *refs: pack_kernel(n_sub, rows, *refs), in_specs=[p...  2.39 us
    pallas_call x1, Pallas kernels, per_device(): pl.pallas_call(lambda *refs: prepare_kernel(n_sub, capacity, columns, *re...  2.32 us
    pallas_call x1, Pallas kernels, per_device(): pl.pallas_call(lambda *refs: element_kernel(columns, *refs), out_shape=ja...  2.26 us
    ppermute x1, waiting for transfers between devices, per_device(): lax.ppermute(packed[1 + k], 'sub', [(i, int(j)) for i, j in pairs])  1.89 us
    ppermute x1, starting transfers between devices, per_device(): lax.ppermute(packed[1 + k], 'sub', [(i, int(j)) for i, j in pairs])  1.49 us
    pallas_call x1, Pallas kernels, per_device(): pl.pallas_call(lambda *refs: voxel_kernel(width, *refs), out_shape=jax.Sh...  0.89 us
  transfers between devices with their start and end apart: 3, of which 1 were waited for; matrix products, arithmetic and copies ran while one was open for 0% of the time, Pallas kernels for 9%

profile of v4, /device:TPU:0, one launch (start us, length us, event | category | flops | bytes accessed | tf_op | source)
XLA Modules:
  0.0 26.0 jit_solution(9871257533640049720)
XLA Ops:
  0.0 2.4 %pack.1 = (bf16[1920,256]{1,0:T(8,128)(2,1)S(1)}, s32[2,32]{1,0:T(2,128)}, s32[2,32]{1,0:T(2,128)S(1)}, bf16[210,2,120]{2,1,0:T(2,128)(2,1)S(1)}, bf16[35,35]{1,...) custom-call(bf16[1920,256]{1,0:T(8,128)(2,1)} %bitcast.13, ...), custom_call_target="tpu_custom_call" | custom-call | tf_op jit(solution)/shard_map/pack/pallas_call | solution.py:307
  2.4 3.1 %collective-permute-start = (bf16[32,1920]{1,0:T(8,128)(2,1)S(1)}, bf16[32,1920]{1,0:T(8,128)(2,1)S(1)}, u32[]{:S(2)}, u32[]{:S(2)}) collective-permute-start(bf16[32,1920]{1,0:T(8,128)(2,1)S(1)} %get-tuple-element.34), channel_id=1, source_target_pairs={{0,4},{1,5},{2,6},{3,7},{4,0},{5,1},{6,2},{7,3},{8,12},{9,13},{10,... | collective-permute-start | bytes 368648 | tf_op jit(solution)/shard_map/ppermute | solution.py:336
  5.5 0.0 collective-permute-start.1
  5.5 1.5 %collective-permute-start.2 = (bf16[32,1920]{1,0:T(8,128)(2,1)S(1)}, bf16[32,1920]{1,0:T(8,128)(2,1)S(1)}, u32[]{:S(2)}, u32[]{:S(2)}) collective-permute-start(bf16[32,1920]{1,0:T(8,128)(2,1)S(1)} %get-tuple-element.36), channel_id=1, source_target_pairs={{0,2},{2,0},{1,3},{3,1},{4,6},{6,4},{5,7},{7,5},{8,10},{10,8},{9,1... | collective-permute-start | bytes 368648 | tf_op jit(solution)/shard_map/ppermute | solution.py:339
  7.0 2.3 %prepare.1 = (bf16[8,256,512]{2,1,0:T(8,128)(2,1)S(1)}, s32[4,128]{1,0:T(4,128)S(1)}, bf16[2,240,256]{2,1,0:T(8,128)(2,1)S(1)}, bf16[240,240]{1,0:T(8,128)(2,1)S(1)}, bf16[384,128]{1,0:T(8,128)(2,1)S(1)}) custom-call(s32[2,32]{1,0:T(2,128)S(1)} %get-tuple-element.23.refs_0_, bf16[1920,256]{1,0:T(8,128)(2,1)S(1)} %get-tuple-element.24.refs_1_, ...), custom_call_target="tpu_custom_call" | custom-call | flops 536870912 | bytes 4194304 | tf_op jit(solution)/shard_map/prepare/pallas_call | solution.py:342
  9.3 0.0 collective-permute-done.refs_7_
  9.3 0.0 collective-permute-done.1.refs_8_
  9.3 1.9 %collective-permute-done.2.refs_9_ = bf16[32,1920]{1,0:T(8,128)(2,1)S(1)} collective-permute-done((bf16[32,1920]{1,0:T(8,128)(2,1)S(1)}, bf16[32,1920]{1,0:T(8,128)(2,1)S(1)}, u32[]{:S(2)}, u32[]{:S(2)}) %collective-permute-start.2) | collective-permute-done | bytes 122912 | tf_op jit(solution)/shard_map/ppermute | solution.py:339
  11.2 2.3 %elements.1 = bf16[384,128]{1,0:T(8,128)(2,1)S(1)} custom-call(f32[1,128]{1,0:T(1,128)S(1)} %get-tuple-element.21.refs_0_, s32[1,128]{1,0:T(1,128)S(1)} %get-tuple-element.22.refs_1_, bf16[8,256,512]{2,1,0:T(8,128)(2,1)S(1)} %get-tuple-element.29.refs_2_, s32[4,128]{1,0:T(4,128)S(1)} %get-tuple-element.30.refs_3_, ...), custom_call_target="tpu_custom_call" | custom-call | tf_op jit(solution)/shard_map/elements/pallas_call | solution.py:357
  13.5 11.6 %all_to_all.11 = bf16[8,48,128]{2,1,0:T(8,128)(2,1)S(1)} all-to-all(bf16[8,48,128]{2,1,0:T(8,128)(2,1)S(1)} %bitcast.11), channel_id=1, replica_groups=mesh['groups'=2,'dom'=4,'sub'=2,'rhs'=2] {'dom','sub'}, dimensions={0} | all-to-all | bytes 196608 | tf_op jit(solution)/shard_map/all_to_all | solution.py:367
  25.1 0.9 %voxels.1 = f32[96,128]{1,0:T(8,128)} custom-call(bf16[384,128]{1,0:T(8,128)(2,1)S(1)} %bitcast.12), custom_call_target="tpu_custom_call" | custom-call | tf_op jit(solution)/shard_map/voxels/pallas_call | solution.py:368
Async XLA Ops:
  2.4 6.9 %collective-permute-start = (bf16[32,1920]{1,0:T(8,128)(2,1)S(1)}, bf16[32,1920]{1,0:T(8,128)(2,1)S(1)}, u32[]{:S(2)}, u32[]{:S(2)}) collective-permute-start(bf16[32,1920]{1,0:T(8,128)(2,1)S(1)} %get-tuple-element.34), channel_id=1, source_target_pairs={{0,4},{1,5},{2,6},{3,7},{4,0},{5,1},{6,2},{7,3},{8,12},{9,13},{10,... | collective-permute-start | bytes 368648 | tf_op jit(solution)/shard_map/ppermute | solution.py:336
  5.5 3.8 %collective-permute-start.1 = (bf16[32,1920]{1,0:T(8,128)(2,1)S(1)}, bf16[32,1920]{1,0:T(8,128)(2,1)S(1)}, u32[]{:S(2)}, u32[]{:S(2)}) collective-permute-start(bf16[32,1920]{1,0:T(8,128)(2,1)S(1)} %get-tuple-element.35), channel_id=1, source_target_pairs={{0,1},{1,0},{2,3},{3,2},{4,8},{5,9},{6,10},{7,11},{8,4},{9,5},{10,... | collective-permute-start | bytes 368648 | tf_op jit(solution)/shard_map/ppermute | solution.py:336
  5.5 5.7 %collective-permute-start.2 = (bf16[32,1920]{1,0:T(8,128)(2,1)S(1)}, bf16[32,1920]{1,0:T(8,128)(2,1)S(1)}, u32[]{:S(2)}, u32[]{:S(2)}) collective-permute-start(bf16[32,1920]{1,0:T(8,128)(2,1)S(1)} %get-tuple-element.36), channel_id=1, source_target_pairs={{0,2},{2,0},{1,3},{3,1},{4,6},{6,4},{5,7},{7,5},{8,10},{10,8},{9,1... | collective-permute-start | bytes 368648 | tf_op jit(solution)/shard_map/ppermute | solution.py:339

commit v5 on v4

--- a/solution.py
+++ b/solution.py
@@ -9,11 +9,11 @@
 
 BASIS = 35
 HALF = 3 * BASIS
-GROUP = 40
 NODES = 30
 BLOCK = 256
-N_INPUTS = 9
-CHUNKS = 1
+N_SMALL = 6
+FULL = 32
+ROWS = 216
 UNROLL = 8
 VMEM_LIMIT = 24 * 1024 * 1024
 
@@ -40,26 +40,12 @@
     return lax.rem(index + k, size), lax.rem(index + size - k, size)
 
 
-def pack_kernel(n_sub, rows, *refs):
-    hbm_refs, refs = refs[:N_INPUTS], refs[N_INPUTS:]
-    vmem_refs, refs = refs[:N_INPUTS], refs[N_INPUTS:]
-    out_refs, (sems, chunk_sems) = refs[: n_sub + 1], refs[n_sub + 1 :]
-    copies = [
-        pltpu.make_async_copy(hbm_refs[i], vmem_refs[i], sems.at[i]) for i in range(1, N_INPUTS)
-    ]
-    for copy in copies[:2]:
-        copy.start()
-    table_ref, dom_ref, sub_ref = vmem_refs[:3]
-    values, faces = table_ref.shape
-    step = values // CHUNKS
-    chunks = []
-    for k in range(CHUNKS):
-        part = pl.ds(k * step, step)
-        chunks.append(
-            pltpu.make_async_copy(hbm_refs[0].at[part, :], table_ref.at[part, :], chunk_sems.at[k])
-        )
-        chunks[k].start()
-    for copy in copies[2:]:
+def pack_kernel(n_sub, rows, traces_hbm, dom_hbm, sub_hbm, table_ref, sub_ref, *refs):
+    out_refs, (dom_ref, sems) = refs[: n_sub + 1], refs[n_sub + 1 :]
+    faces = table_ref.shape[1]
+    pairs = [(dom_hbm, dom_ref), (sub_hbm, sub_ref), (traces_hbm, table_ref)]
+    copies = [pltpu.make_async_copy(*pair, sems.at[i]) for i, pair in enumerate(pairs)]
+    for copy in copies:
         copy.start()
     for copy in copies[:2]:
         copy.wait()
@@ -71,14 +57,10 @@
     face = iota((faces, rows), 0)
     picks = [jnp.where(face == row, 1.0, 0.0).T for row in lists]
     picks = jnp.concatenate(picks, axis=0).astype(jnp.bfloat16)
-    for k in range(CHUNKS):
-        chunks[k].wait()
-        part = slice(k * step, (k + 1) * step)
-        packed = dot(picks, table_ref[part, :], NT).astype(jnp.bfloat16)
-        for i, out_ref in enumerate(out_refs):
-            out_ref[:, part] = packed[i * rows : (i + 1) * rows]
-    for copy in copies[2:]:
-        copy.wait()
+    copies[2].wait()
+    packed = dot(picks, table_ref[...], NT).astype(jnp.bfloat16)
+    for i, out_ref in enumerate(out_refs):
+        out_ref[...] = packed[i * rows : (i + 1) * rows]
 
 
 def reorder_matrix(columns):
@@ -93,22 +75,27 @@
     return [a * half - (a * half) % 128 + b * BLOCK for a in range(2) for b in range(4)]
 
 
-def prepare_kernel(
-    n_sub,
-    capacity,
-    columns,
-    sub_ref,
-    table_ref,
-    solver_ref,
-    mass_ref,
-    elem_ref,
-    owner_ref,
-    own_ref,
-    places_ref,
-    matrix_ref,
-    masses_ref,
-    sends_ref,
-):
+def field_row(part, axis, basis):
+    tail = 6 * FULL + axis * 8 + part * (BASIS - FULL) + basis - FULL
+    return jnp.where(basis < FULL, (part * 3 + axis) * FULL + basis, tail)
+
+
+def prepare_kernel(n_sub, capacity, columns, sub_ref, table_ref, *refs):
+    hbm_refs, refs = refs[:N_SMALL], refs[N_SMALL:]
+    own_ref, places_ref, matrix_ref, sends_ref, volume_ref, slot_ref = refs[:6]
+    solver_ref, mass_ref, elem_ref, owner_ref, mine_ref, sems = refs[6:]
+    vmem_refs = [elem_ref, owner_ref, solver_ref, mass_ref, volume_ref, slot_ref]
+    copies = [
+        pltpu.make_async_copy(hbm_refs[i], vmem_refs[i], sems.at[i]) for i in range(N_SMALL)
+    ]
+    for copy in copies:
+        copy.start()
+    reorder = reorder_matrix(columns)
+    for b, start in enumerate(block_starts(columns)):
+        mine = dot(reorder, table_ref[start : start + BLOCK, :])
+        mine_ref[b] = mine.astype(jnp.bfloat16)
+    for copy in copies:
+        copy.wait()
     faces = table_ref.shape[1]
     elems = elem_ref.shape[1]
     rows = sub_ref.shape[1]
@@ -136,39 +123,42 @@
         place = jnp.where((offset >= 0) & (offset < rows), offset + i * rows, place)
     places_ref[...] = place
 
-    reorder = reorder_matrix(columns)
-    for b, start in enumerate(block_starts(columns)):
-        mine = dot(reorder, table_ref[start : start + BLOCK, :]).astype(jnp.bfloat16)
-        own_ref[b] = dot(mine, own).astype(jnp.bfloat16)
-
-    place = iota((3 * GROUP, HALF), 0)
-    source = iota((3 * GROUP, HALF), 1)
-    spread = one_hot(
-        (lax.div(place, GROUP) == lax.div(source, BASIS))
-        & (lax.rem(place, GROUP) == lax.rem(source, BASIS))
-    )
+    for b in range(8):
+        own_ref[b] = dot(mine_ref[b], own).astype(jnp.bfloat16)
+
+    source = iota((ROWS, HALF), 1)
+    axis, basis = lax.div(source, BASIS), lax.rem(source, BASIS)
+    place = iota((ROWS, HALF), 0)
+    spread = [one_hot(place == field_row(part, axis, basis)) for part in range(2)]
+    mass = mass_ref[...]
+    source = iota((HALF, BASIS), 0)
+    column = iota((HALF, BASIS), 1)
     solver = solver_ref[:HALF].astype(jnp.float32)
-    real = dot(spread, solver[:, 0, :].astype(jnp.bfloat16)).astype(jnp.bfloat16)
-    imag = dot(spread, solver[:, 1, :].astype(jnp.bfloat16)).astype(jnp.bfloat16)
+    real, imag = solver[:, 0, :], solver[:, 1, :]
     half = 2 * NODES * columns
     for a in range(2):
+        if a == 0:
+            tall = one_hot(lax.rem(source, BASIS) == column)
+            wide = dot(dot(tall, mass).astype(jnp.bfloat16), tall, NT)
+            same = lax.div(iota((HALF, HALF), 0), BASIS) == lax.div(iota((HALF, HALF), 1), BASIS)
+            wide = jnp.where(same, wide, 0.0).astype(jnp.bfloat16)
+            parts = [dot(wide, x.astype(jnp.bfloat16)) for x in (real, imag)]
+            signs = (1.0, -1.0)
+        else:
+            parts = [real, imag]
+            signs = (1.0, 1.0)
+        parts = [x.astype(jnp.bfloat16) for x in parts]
         shift = ((a * half) % 128) // columns
-        source = iota((4 * NODES, BLOCK), 0)
-        place = iota((4 * NODES, BLOCK), 1)
-        target = lax.div(source, NODES) * 64 + lax.rem(source, NODES) + shift
-        for_real = one_hot(target == place)
-        for_imag = one_hot(target + NODES == place)
-        top = dot(real, for_real) - dot(imag, for_imag)
-        bottom = dot(imag, for_real) + dot(real, for_imag)
-        matrix_ref[a] = jnp.concatenate([top, bottom], axis=0).astype(jnp.bfloat16)
-
-    size = 6 * GROUP
-    spread = one_hot(lax.rem(iota((size, BASIS), 0), GROUP) == iota((size, BASIS), 1))
-    tiles = dot(dot(spread, mass_ref[...]).astype(jnp.bfloat16), spread, NT)
-    row = iota((size, size), 0)
-    col = iota((size, size), 1)
-    tiles = jnp.where(lax.div(row, GROUP) == lax.div(col, GROUP), tiles, 0.0)
-    masses_ref[...] = jnp.where(row < 3 * GROUP, tiles, -tiles).astype(jnp.bfloat16)
+        source_k = iota((4 * NODES, BLOCK), 0)
+        place_k = iota((4 * NODES, BLOCK), 1)
+        target = lax.div(source_k, NODES) * 64 + lax.rem(source_k, NODES) + shift
+        for_real = one_hot(target == place_k)
+        for_imag = one_hot(target + NODES == place_k)
+        top = signs[0] * (dot(parts[0], for_real) - dot(parts[1], for_imag))
+        bottom = signs[1] * (dot(parts[1], for_real) + dot(parts[0], for_imag))
+        matrix = dot(spread[0], top.astype(jnp.bfloat16))
+        matrix = matrix + dot(spread[1], bottom.astype(jnp.bfloat16))
+        matrix_ref[a] = matrix.astype(jnp.bfloat16)
 
     owner = owner_ref[...]
     owners = iota((max(8, slots // capacity), elems), 0) == owner
@@ -181,13 +171,12 @@
 
 def element_kernel(
     columns,
-    volume_ref,
-    slot_ref,
     own_ref,
     places_ref,
     matrix_ref,
-    masses_ref,
     sends_ref,
+    volume_ref,
+    slot_ref,
     *refs,
 ):
     halo_refs = refs[:-3]
@@ -221,7 +210,6 @@
                 got = got + jnp.where(inside[f * tiles + t], found, 0.0).astype(jnp.bfloat16)
             gathered_ref[b, :, :, part] = got.reshape(columns, per_block, elems)
 
-    masses = masses_ref[...]
     pairs = [(0, 0), (1, 1), (2, 2), (0, 1), (0, 2), (1, 2)]
 
     def step(index, carry):
@@ -240,17 +228,21 @@
                         axis=0,
                     )
                 )
-            values = dot(matrix_ref[a], jnp.concatenate(parts, axis=1))
-            fields.append(values.astype(jnp.bfloat16))
-        weighted = dot(masses, fields[0])
-        shape = (2, 3, GROUP // 8, 8, 2 * elems)
-        adjoint = fields[1].astype(jnp.float32).reshape(shape)
-        weighted = weighted.reshape(shape)
+            fields.append(dot(matrix_ref[a], jnp.concatenate(parts, axis=1)))
+        weighted = fields[0]
+        adjoint = fields[1].astype(jnp.bfloat16).astype(jnp.float32)
+        split = 6 * FULL
+        shape = (2, 3, FULL // 8, 8, 2 * elems)
+        tail = (3, 8, 2 * elems)
+        weighted, weighted_tail = weighted[:split].reshape(shape), weighted[split:].reshape(tail)
+        adjoint, adjoint_tail = adjoint[:split].reshape(shape), adjoint[split:].reshape(tail)
         for m, (i, j) in enumerate(pairs):
             products = adjoint[:, i] * weighted[:, j]
+            rest = adjoint_tail[i] * weighted_tail[j]
             if i != j:
                 products = products + adjoint[:, j] * weighted[:, i]
-            total = jnp.sum(products, axis=(0, 1))
+                rest = rest + adjoint_tail[j] * weighted_tail[i]
+            total = jnp.sum(products, axis=(0, 1)) + rest
             for c in range(2):
                 start = pl.multiple_of((m * columns + 2 * index + c) * 8, 8)
                 sums_ref[pl.ds(start, 8), :] = total[:, c * elems : (c + 1) * elems]
@@ -292,33 +284,25 @@
     values = table.shape[0]
     params = pltpu.CompilerParams(vmem_limit_bytes=VMEM_LIMIT)
 
-    inputs = [
-        table,
-        dom_lists,
-        sub_lists,
-        solver[0].transpose(1, 0, 2),
-        mass[0],
-        elem_face,
-        volume.reshape(1, elems),
-        elem_owner.reshape(1, elems),
-        elem_slot.reshape(1, elems),
-    ]
-    inputs = [pltpu.with_memory_space_constraint(x, pltpu.HBM) for x in inputs]
-    outs = pl.pallas_call(
+    vmem = pl.BlockSpec(memory_space=pltpu.VMEM)
+    hbm = pl.BlockSpec(memory_space=pltpu.HBM)
+
+    def in_hbm(*arrays):
+        return [pltpu.with_memory_space_constraint(x, pltpu.HBM) for x in arrays]
+
+    table, sub, *packed = pl.pallas_call(
         lambda *refs: pack_kernel(n_sub, rows, *refs),
-        in_specs=[pl.BlockSpec(memory_space=pltpu.HBM)] * N_INPUTS,
-        out_shape=[pltpu.VMEM(x.shape, x.dtype) for x in inputs]
+        in_specs=[hbm] * 3,
+        out_shape=[pltpu.VMEM(x.shape, x.dtype) for x in (table, sub_lists)]
         + [pltpu.VMEM((rows, values), jnp.bfloat16)] * (n_sub + 1),
-        out_specs=[pl.BlockSpec(memory_space=pltpu.VMEM)] * (N_INPUTS + n_sub + 1),
+        out_specs=[vmem] * (n_sub + 3),
         scratch_shapes=[
-            pltpu.SemaphoreType.DMA((N_INPUTS,)),
-            pltpu.SemaphoreType.DMA((CHUNKS,)),
+            pltpu.VMEM(dom_lists.shape, jnp.int32),
+            pltpu.SemaphoreType.DMA((3,)),
         ],
         compiler_params=params,
         name="pack",
-    )(*inputs)
-    table, _, sub, matrix, mass, elem_face, volume, owner, slot = outs[:N_INPUTS]
-    packed = outs[N_INPUTS:]
+    )(*in_hbm(table, dom_lists, sub_lists))
 
     n_rhs = lax.axis_size("rhs")
     halos = []
@@ -339,21 +323,44 @@
         halos.append(lax.ppermute(packed[1 + k], "sub", [(i, int(j)) for i, j in pairs]))
 
     slots = owners * capacity
+    matrix = solver[0].transpose(1, 0, 2)
     fixed = pl.pallas_call(
         lambda *refs: prepare_kernel(n_sub, capacity, columns, *refs),
+        in_specs=[vmem] * 2 + [hbm] * N_SMALL,
         out_shape=[
-            jax.ShapeDtypeStruct((8, BLOCK, 4 * elems), jnp.bfloat16),
-            jax.ShapeDtypeStruct((4, elems), jnp.int32),
-            jax.ShapeDtypeStruct((2, 6 * GROUP, BLOCK), jnp.bfloat16),
-            jax.ShapeDtypeStruct((6 * GROUP, 6 * GROUP), jnp.bfloat16),
-            jax.ShapeDtypeStruct((slots, elems), jnp.bfloat16),
+            pltpu.VMEM((8, BLOCK, 4 * elems), jnp.bfloat16),
+            pltpu.VMEM((4, elems), jnp.int32),
+            pltpu.VMEM((2, ROWS, BLOCK), jnp.bfloat16),
+            pltpu.VMEM((slots, elems), jnp.bfloat16),
+            pltpu.VMEM((1, elems), jnp.float32),
+            pltpu.VMEM((1, elems), jnp.int32),
+        ],
+        out_specs=[vmem] * 6,
+        scratch_shapes=[
+            pltpu.VMEM(matrix.shape, jnp.bfloat16),
+            pltpu.VMEM(mass.shape[1:], jnp.bfloat16),
+            pltpu.VMEM((4, elems), jnp.int32),
+            pltpu.VMEM((1, elems), jnp.int32),
+            pltpu.VMEM((8, BLOCK, faces), jnp.bfloat16),
+            pltpu.SemaphoreType.DMA((N_SMALL,)),
         ],
         compiler_params=params,
         cost_estimate=pl.CostEstimate(
             flops=8 * BLOCK * faces * 8 * elems, bytes_accessed=4 << 20, transcendentals=0
         ),
         name="prepare",
-    )(sub, table, matrix, mass, elem_face, owner)
+    )(
+        sub,
+        table,
+        *in_hbm(
+            elem_face,
+            elem_owner.reshape(1, elems),
+            matrix,
+            mass[0],
+            volume.reshape(1, elems),
+            elem_slot.reshape(1, elems),
+        ),
+    )
     sent = pl.pallas_call(
         lambda *refs: element_kernel(columns, *refs),
         out_shape=jax.ShapeDtypeStruct((slots, 128), jnp.bfloat16),
@@ -363,7 +370,7 @@
         ],
         compiler_params=params,
         name="elements",
-    )(volume, slot, *fixed, *halos)
+    )(*fixed, *halos)
     got = lax.all_to_all(sent, ("dom", "sub"), split_axis=0, concat_axis=0, tiled=True)
     summed = pl.pallas_call(
         lambda *refs: voxel_kernel(width, *refs),

time: 26.2 us -> 25.2 us (0.962)
  waiting for transfers between devices: 1.9 us -> 1.27 us
  Pallas kernels: 7.87 us -> 7.49 us
    pallas_call x1, Pallas kernels: 2.39 us -> 1.7 us  [per_device(): pl.pallas_call(lambda *refs: pack_kernel(n_sub, rows, *refs), in_specs=[h...]
    ppermute x1, waiting for transfers between devices: 1.89 us -> 1.27 us  [per_device(): lax.ppermute(packed[1 + k], 'sub', [(i, int(j)) for i, j in pairs])]
    pallas_call x1, Pallas kernels: 2.32 us -> 2.95 us  [per_device(): pl.pallas_call(lambda *refs: prepare_kernel(n_sub, capacity, columns, *re...]
    pallas_call x1, Pallas kernels: 2.26 us -> 1.95 us  [per_device(): pl.pallas_call(lambda *refs: element_kernel(columns, *refs), out_shape=ja...]
  transfers between devices with their start and end apart: 3 -> 3, of which waited for: 1 -> 1; matrix products, arithmetic and copies ran while one was open for 0% -> 0% of each run, Pallas kernels for 9% -> 12%
where the time goes in v5:
time: 25.2 us; the launch traced here: 25 us
  blocking collectives  11.6 us (46%)
  Pallas kernels  7.49 us (30%)
  starting transfers between devices  4.58 us (18%)
  waiting for transfers between devices  1.27 us (5%)
    all_to_all x1, blocking collectives, per_device(): lax.all_to_all(sent, ('dom', 'sub'), split_axis=0, concat_axis=0, tiled=T...  11.6 us
    ppermute x2, starting transfers between devices, per_device(): halos.append(lax.ppermute(part, ('dom', 'sub', 'rhs'), pairs))  3.09 us
    pallas_call x1, Pallas kernels, per_device(): pl.pallas_call(lambda *refs: prepare_kernel(n_sub, capacity, columns, *re...  2.95 us
    pallas_call x1, Pallas kernels, per_device(): pl.pallas_call(lambda *refs: element_kernel(columns, *refs), out_shape=ja...  1.95 us
    pallas_call x1, Pallas kernels, per_device(): pl.pallas_call(lambda *refs: pack_kernel(n_sub, rows, *refs), in_specs=[h...  1.7 us
    ppermute x1, starting transfers between devices, per_device(): lax.ppermute(packed[1 + k], 'sub', [(i, int(j)) for i, j in pairs])  1.49 us
    ppermute x1, waiting for transfers between devices, per_device(): lax.ppermute(packed[1 + k], 'sub', [(i, int(j)) for i, j in pairs])  1.27 us
    pallas_call x1, Pallas kernels, per_device(): pl.pallas_call(lambda *refs: voxel_kernel(width, *refs), out_shape=jax.Sh...  0.89 us
  transfers between devices with their start and end apart: 3, of which 1 were waited for; matrix products, arithmetic and copies ran while one was open for 0% of the time, Pallas kernels for 12%

profile of v5, /device:TPU:0, one launch (start us, length us, event | category | flops | bytes accessed | tf_op | source)
XLA Modules:
  0.0 25.0 jit_solution(12791132777935227699)
XLA Ops:
  0.0 1.7 %pack.1 = (bf16[1920,256]{1,0:T(8,128)(2,1)S(1)}, s32[2,32]{1,0:T(2,128)S(1)}, bf16[32,1920]{1,0:T(8,128)(2,1)S(1)}, bf16[32,1920]{1,0:T(8,128)(2,1)S(1)}, bf16[32,1920]{1,0:T(8,128)(2,1)S(1)}) custom-call(bf16[1920,256]{1,0:T(8,128)(2,1)} %bitcast.13, s32[2,32]{1,0:T(2,128)} %refs_1_.1, s32[2,32]{1,0:T(2,128)} %refs_2_.2), custom_call_target="tpu_custom_call" | custom-call | tf_op jit(solution)/shard_map/pack/pallas_call | solution.py:293
  1.7 3.1 %collective-permute-start = (bf16[32,1920]{1,0:T(8,128)(2,1)S(1)}, bf16[32,1920]{1,0:T(8,128)(2,1)S(1)}, u32[]{:S(2)}, u32[]{:S(2)}) collective-permute-start(bf16[32,1920]{1,0:T(8,128)(2,1)S(1)} %get-tuple-element.24), channel_id=1, source_target_pairs={{0,4},{1,5},{2,6},{3,7},{4,0},{5,1},{6,2},{7,3},{8,12},{9,13},{10,... | collective-permute-start | bytes 368648 | tf_op jit(solution)/shard_map/ppermute | solution.py:320
  4.8 0.0 collective-permute-start.1
  4.8 1.5 %collective-permute-start.2 = (bf16[32,1920]{1,0:T(8,128)(2,1)S(1)}, bf16[32,1920]{1,0:T(8,128)(2,1)S(1)}, u32[]{:S(2)}, u32[]{:S(2)}) collective-permute-start(bf16[32,1920]{1,0:T(8,128)(2,1)S(1)} %get-tuple-element.26), channel_id=1, source_target_pairs={{0,2},{2,0},{1,3},{3,1},{4,6},{6,4},{5,7},{7,5},{8,10},{10,8},{9,1... | collective-permute-start | bytes 368648 | tf_op jit(solution)/shard_map/ppermute | solution.py:323
  6.3 2.9 %prepare.1 = (bf16[8,256,512]{2,1,0:T(8,128)(2,1)S(1)}, s32[4,128]{1,0:T(4,128)S(1)}, bf16[2,216,256]{2,1,0:T(8,128)(2,1)S(1)}, bf16[384,128]{1,0:T(8,128)(2,1)S...) custom-call(s32[2,32]{1,0:T(2,128)S(1)} %get-tuple-element.16.refs_0_, bf16[1920,256]{1,0:T(8,128)(2,1)S(1)} %get-tuple-element.17.refs_1_, ...), custom_call_target="tpu_custom_call" | custom-call | flops 536870912 | bytes 4194304 | tf_op jit(solution)/shard_map/prepare/pallas_call | solution.py:327
  9.2 0.0 collective-permute-done.refs_6_
  9.3 0.0 collective-permute-done.1.refs_7_
  9.3 1.3 %collective-permute-done.2.refs_8_ = bf16[32,1920]{1,0:T(8,128)(2,1)S(1)} collective-permute-done((bf16[32,1920]{1,0:T(8,128)(2,1)S(1)}, bf16[32,1920]{1,0:T(8,128)(2,1)S(1)}, u32[]{:S(2)}, u32[]{:S(2)}) %collective-permute-start.2) | collective-permute-done | bytes 122912 | tf_op jit(solution)/shard_map/ppermute | solution.py:323
  10.5 2.0 %elements.1 = bf16[384,128]{1,0:T(8,128)(2,1)S(1)} custom-call(bf16[8,256,512]{2,1,0:T(8,128)(2,1)S(1)} %get-tuple-element.18.refs_0_, s32[4,128]{1,0:T(4,128)S(1)} %get-tuple-element.19.refs_1_, bf16[2,216,256]{2,1,0:T(8,128)(2,1)S(1)} %get-tuple-element.20.refs_2_, bf16[384,128]{1,0:T(8,128)(2,1)S(1)} %get-tuple-element.21.refs_3_, ...), custom_call_target="tpu_custom_call" | custom-call | tf_op jit(solution)/shard_map/elements/pallas_call | solution.py:364
  12.5 11.6 %all_to_all.11 = bf16[8,48,128]{2,1,0:T(8,128)(2,1)S(1)} all-to-all(bf16[8,48,128]{2,1,0:T(8,128)(2,1)S(1)} %bitcast.11), channel_id=1, replica_groups=mesh['groups'=2,'dom'=4,'sub'=2,'rhs'=2] {'dom','sub'}, dimensions={0} | all-to-all | bytes 196608 | tf_op jit(solution)/shard_map/all_to_all | solution.py:374
  24.1 0.9 %voxels.1 = f32[96,128]{1,0:T(8,128)} custom-call(bf16[384,128]{1,0:T(8,128)(2,1)S(1)} %bitcast.12), custom_call_target="tpu_custom_call" | custom-call | tf_op jit(solution)/shard_map/voxels/pallas_call | solution.py:375
Async XLA Ops:
  1.7 7.5 %collective-permute-start = (bf16[32,1920]{1,0:T(8,128)(2,1)S(1)}, bf16[32,1920]{1,0:T(8,128)(2,1)S(1)}, u32[]{:S(2)}, u32[]{:S(2)}) collective-permute-start(bf16[32,1920]{1,0:T(8,128)(2,1)S(1)} %get-tuple-element.24), channel_id=1, source_target_pairs={{0,4},{1,5},{2,6},{3,7},{4,0},{5,1},{6,2},{7,3},{8,12},{9,13},{10,... | collective-permute-start | bytes 368648 | tf_op jit(solution)/shard_map/ppermute | solution.py:320
  4.8 4.5 %collective-permute-start.1 = (bf16[32,1920]{1,0:T(8,128)(2,1)S(1)}, bf16[32,1920]{1,0:T(8,128)(2,1)S(1)}, u32[]{:S(2)}, u32[]{:S(2)}) collective-permute-start(bf16[32,1920]{1,0:T(8,128)(2,1)S(1)} %get-tuple-element.25), channel_id=1, source_target_pairs={{0,1},{1,0},{2,3},{3,2},{4,8},{5,9},{6,10},{7,11},{8,4},{9,5},{10,... | collective-permute-start | bytes 368648 | tf_op jit(solution)/shard_map/ppermute | solution.py:320
  4.8 5.7 %collective-permute-start.2 = (bf16[32,1920]{1,0:T(8,128)(2,1)S(1)}, bf16[32,1920]{1,0:T(8,128)(2,1)S(1)}, u32[]{:S(2)}, u32[]{:S(2)}) collective-permute-start(bf16[32,1920]{1,0:T(8,128)(2,1)S(1)} %get-tuple-element.26), channel_id=1, source_target_pairs={{0,2},{2,0},{1,3},{3,1},{4,6},{6,4},{5,7},{7,5},{8,10},{10,8},{9,1... | collective-permute-start | bytes 368648 | tf_op jit(solution)/shard_map/ppermute | solution.py:323

commit v6 on v5

--- a/solution.py
+++ b/solution.py
@@ -14,7 +14,7 @@
 N_SMALL = 6
 FULL = 32
 ROWS = 216
-UNROLL = 8
+PADDED = 112
 VMEM_LIMIT = 24 * 1024 * 1024
 
 NT = (((1,), (1,)), ((), ()))
@@ -38,6 +38,10 @@
     if size & (size - 1) == 0:
         return index ^ k, index ^ k
     return lax.rem(index + k, size), lax.rem(index + size - k, size)
+
+
+def halo_order(n_sub):
+    return [1, 0] + list(range(2, n_sub + 1))
 
 
 def pack_kernel(n_sub, rows, traces_hbm, dom_hbm, sub_hbm, table_ref, sub_ref, *refs):
@@ -75,9 +79,15 @@
     return [a * half - (a * half) % 128 + b * BLOCK for a in range(2) for b in range(4)]
 
 
-def field_row(part, axis, basis):
-    tail = 6 * FULL + axis * 8 + part * (BASIS - FULL) + basis - FULL
-    return jnp.where(basis < FULL, (part * 3 + axis) * FULL + basis, tail)
+def row_group(row):
+    tail = row - 6 * FULL
+    within = lax.rem(tail, 8)
+    late = BASIS - FULL
+    head = row < 6 * FULL
+    group = jnp.where(head, lax.div(row, FULL), lax.div(within, late) * 3 + lax.div(tail, 8))
+    basis = jnp.where(head, lax.rem(row, FULL), FULL + lax.rem(within, late))
+    used = head | (within < 2 * late)
+    return jnp.where(used, group, -1), basis
 
 
 def prepare_kernel(n_sub, capacity, columns, sub_ref, table_ref, *refs):
@@ -90,79 +100,81 @@
     ]
     for copy in copies:
         copy.start()
-    reorder = reorder_matrix(columns)
-    for b, start in enumerate(block_starts(columns)):
-        mine = dot(reorder, table_ref[start : start + BLOCK, :])
-        mine_ref[b] = mine.astype(jnp.bfloat16)
-    for copy in copies:
-        copy.wait()
     faces = table_ref.shape[1]
     elems = elem_ref.shape[1]
     rows = sub_ref.shape[1]
     slots = sends_ref.shape[0]
     parity = lax.rem(lax.axis_index("dom"), 2)
     within = lax.axis_index("sub")
-    face_rows = [elem_ref[f : f + 1, :] for f in range(4)]
-
-    def picks(size, start):
-        return jnp.concatenate(
-            [jnp.where(iota((size, elems), 0) + start == row, 1.0, 0.0) for row in face_rows],
-            axis=1,
-        )
-
+
+    reorder = reorder_matrix(columns)
+    for b, start in enumerate(block_starts(columns)):
+        mine = dot(reorder, table_ref[start : start + BLOCK, :])
+        mine_ref[b] = mine.astype(jnp.bfloat16)
     own_list = sub_ref[pl.ds(within, 1), :]
-    own_list = one_hot(iota((faces, rows), 0) == own_list)
-    own_block = picks(rows, faces + (2 + within) * rows).astype(jnp.bfloat16)
-    own = (picks(faces, 0) + dot(own_list, own_block)).astype(jnp.bfloat16)
+    square = iota((rows, rows), 0) == iota((rows, rows), 1)
+    own_list = jnp.sum(jnp.where(square, own_list, 0), axis=1, keepdims=True)
+    half = 2 * NODES * columns
+    source = iota((4 * NODES, BLOCK), 0)
+    place = iota((4 * NODES, BLOCK), 1)
+    target = lax.div(source, NODES) * 64 + lax.rem(source, NODES)
+    spots = []
+    for a in range(2):
+        first = target + ((a * half) % 128) // columns
+        spots += [one_hot(first == place), one_hot(first + NODES == place)]
+    spots = jnp.concatenate(spots, axis=1)
+    group, basis = row_group(iota((ROWS, 1), 0))
+    column = iota((1, 2 * PADDED), 1)
+    field = lax.rem(column, PADDED)
+    column_group = lax.div(column, PADDED) * 3 + lax.div(field, BASIS)
+    column_basis = lax.rem(field, BASIS)
+    same = (group == column_group) & (field < HALF)
+    spread = one_hot(same & (basis == column_basis))
+    sign = jnp.where(same, jnp.where(column < PADDED, 1.0, -1.0), 0.0)
+    tall = one_hot(basis == iota((ROWS, BASIS), 1))
+    wide = one_hot(iota((BASIS, 2 * PADDED), 0) == column_basis)
+    earlier = one_hot(iota((elems, elems), 0) < iota((elems, elems), 1))
+    for copy in copies:
+        copy.wait()
+
+    elem_face = elem_ref[...]
+    offset = elem_face - (faces + (2 + within) * rows)
+    own = []
+    for f in range(4):
+        found = jnp.where(iota((rows, elems), 0) == offset[f : f + 1, :], own_list, 0)
+        found = jnp.sum(found, axis=0, keepdims=True)
+        inside = (offset[f : f + 1, :] >= 0) & (offset[f : f + 1, :] < rows)
+        index = jnp.where(inside, found, elem_face[f : f + 1, :])
+        own.append(one_hot(iota((faces, elems), 0) == index))
+    own = jnp.concatenate(own, axis=1)
+    for b in range(8):
+        own_ref[b] = dot(mine_ref[b], own).astype(jnp.bfloat16)
     blocks = [1 - parity, parity]
     for k in range(1, n_sub):
         blocks.append(2 + pair_index(within, k, n_sub)[1])
-    place = jnp.full(elem_ref.shape, -1, jnp.int32)
-    for i, block in enumerate(blocks):
-        offset = elem_ref[...] - (faces + block * rows)
-        place = jnp.where((offset >= 0) & (offset < rows), offset + i * rows, place)
-    places_ref[...] = place
-
-    for b in range(8):
-        own_ref[b] = dot(mine_ref[b], own).astype(jnp.bfloat16)
-
-    source = iota((ROWS, HALF), 1)
-    axis, basis = lax.div(source, BASIS), lax.rem(source, BASIS)
-    place = iota((ROWS, HALF), 0)
-    spread = [one_hot(place == field_row(part, axis, basis)) for part in range(2)]
-    mass = mass_ref[...]
-    source = iota((HALF, BASIS), 0)
-    column = iota((HALF, BASIS), 1)
-    solver = solver_ref[:HALF].astype(jnp.float32)
-    real, imag = solver[:, 0, :], solver[:, 1, :]
-    half = 2 * NODES * columns
+    blocks = [blocks[i] for i in halo_order(n_sub)]
+    per_tile = 128 // rows - 1
+    for t in range(places_ref.shape[0] // 4):
+        lane = jnp.full(elem_face.shape, 127, jnp.int32)
+        for i, block in enumerate(blocks[t * per_tile : (t + 1) * per_tile]):
+            offset = elem_face - (faces + block * rows)
+            lane = jnp.where((offset >= 0) & (offset < rows), offset + i * rows, lane)
+        places_ref[4 * t : 4 * t + 4, :] = lane
+
+    solver = solver_ref[:PADDED].astype(jnp.float32)
+    solver = jnp.concatenate([solver[:, 0, :], solver[:, 1, :]], axis=0).astype(jnp.bfloat16)
+    placed = dot(solver, spots)
+    masses = dot(dot(tall, mass_ref[...]).astype(jnp.bfloat16), wide) * sign
+    spreads = [masses.astype(jnp.bfloat16), spread]
     for a in range(2):
-        if a == 0:
-            tall = one_hot(lax.rem(source, BASIS) == column)
-            wide = dot(dot(tall, mass).astype(jnp.bfloat16), tall, NT)
-            same = lax.div(iota((HALF, HALF), 0), BASIS) == lax.div(iota((HALF, HALF), 1), BASIS)
-            wide = jnp.where(same, wide, 0.0).astype(jnp.bfloat16)
-            parts = [dot(wide, x.astype(jnp.bfloat16)) for x in (real, imag)]
-            signs = (1.0, -1.0)
-        else:
-            parts = [real, imag]
-            signs = (1.0, 1.0)
-        parts = [x.astype(jnp.bfloat16) for x in parts]
-        shift = ((a * half) % 128) // columns
-        source_k = iota((4 * NODES, BLOCK), 0)
-        place_k = iota((4 * NODES, BLOCK), 1)
-        target = lax.div(source_k, NODES) * 64 + lax.rem(source_k, NODES) + shift
-        for_real = one_hot(target == place_k)
-        for_imag = one_hot(target + NODES == place_k)
-        top = signs[0] * (dot(parts[0], for_real) - dot(parts[1], for_imag))
-        bottom = signs[1] * (dot(parts[1], for_real) + dot(parts[0], for_imag))
-        matrix = dot(spread[0], top.astype(jnp.bfloat16))
-        matrix = matrix + dot(spread[1], bottom.astype(jnp.bfloat16))
-        matrix_ref[a] = matrix.astype(jnp.bfloat16)
+        first, second = (placed[:, (2 * a + i) * BLOCK : (2 * a + i + 1) * BLOCK] for i in range(2))
+        top = first[:PADDED] - second[PADDED:]
+        bottom = first[PADDED:] + second[:PADDED]
+        both = jnp.concatenate([top, bottom], axis=0).astype(jnp.bfloat16)
+        matrix_ref[a] = dot(spreads[a], both).astype(jnp.bfloat16)
 
     owner = owner_ref[...]
     owners = iota((max(8, slots // capacity), elems), 0) == owner
-    earlier = one_hot(iota((elems, elems), 0) < iota((elems, elems), 1))
     counts = dot(one_hot(owners), earlier)
     rank = jnp.sum(jnp.where(owners, counts, 0.0), axis=0, keepdims=True)
     target = owner * capacity + rank.astype(jnp.int32)
@@ -179,61 +191,56 @@
     slot_ref,
     *refs,
 ):
-    halo_refs = refs[:-3]
-    out_ref, gathered_ref, sums_ref = refs[-3:]
+    halo_refs, (out_ref, gathered_ref, sums_ref) = refs[:-3], refs[-3:]
     elems = volume_ref.shape[1]
     per_block = BLOCK // columns
+    tiles = places_ref.shape[0] // 4
     reorder = reorder_matrix(columns)
-    halo_rows = [ref[...] for ref in halo_refs]
-    count = sum(rows.shape[0] for rows in halo_rows)
-    tiles = -(-count // 128)
-    halo_rows.append(jnp.zeros((tiles * 128 - count, halo_rows[0].shape[1]), jnp.bfloat16))
-    halo_rows = jnp.concatenate(halo_rows, axis=0)
-    lanes, inside = [], []
-    for f in range(4):
-        place = jnp.broadcast_to(places_ref[f : f + 1, :], (BLOCK, elems))
-        for t in range(tiles):
-            lanes.append(jnp.clip(place - t * 128, 0, 127))
-            inside.append((place >= t * 128) & (place < (t + 1) * 128))
-    for b, start in enumerate(block_starts(columns)):
-        others = dot(reorder, halo_rows[:, start : start + BLOCK], NT)
+    rows, values = halo_refs[0].shape
+    per_tile = 128 // rows - 1
+    tables = []
+    for t in range(tiles):
+        parts = [ref[...] for ref in halo_refs[t * per_tile : (t + 1) * per_tile]]
+        parts.append(jnp.zeros((128 - rows * len(parts), values), jnp.bfloat16))
+        tables.append(jnp.concatenate(parts, axis=0))
+    lanes = [jnp.broadcast_to(places_ref[i : i + 1, :], (BLOCK, elems)) for i in range(4 * tiles)]
+    starts = block_starts(columns)
+
+    def gather(b):
+        part = slice(starts[b], starts[b] + BLOCK)
+        others = [dot(reorder, table[:, part], NT) for table in tables]
         for f in range(4):
             part = slice(f * elems, (f + 1) * elems)
             got = own_ref[b, :, part]
             for t in range(tiles):
                 found = jnp.take_along_axis(
-                    others[:, t * 128 : (t + 1) * 128],
-                    lanes[f * tiles + t],
-                    axis=1,
-                    mode="promise_in_bounds",
+                    others[t], lanes[4 * t + f], axis=1, mode="promise_in_bounds"
                 )
-                got = got + jnp.where(inside[f * tiles + t], found, 0.0).astype(jnp.bfloat16)
+                got = got + found.astype(jnp.bfloat16)
             gathered_ref[b, :, :, part] = got.reshape(columns, per_block, elems)
 
+    def fields(a, index):
+        parts = []
+        for c in range(2):
+            taken = [gathered_ref[a * 4 + b, 2 * index + c] for b in range(4)]
+            parts.append(
+                jnp.concatenate(
+                    [taken[b][:, f * elems : (f + 1) * elems] for f in range(4) for b in range(4)],
+                    axis=0,
+                )
+            )
+        return dot(matrix_ref[a], jnp.concatenate(parts, axis=1))
+
+    for b in range(8):
+        gather(b)
+
     pairs = [(0, 0), (1, 1), (2, 2), (0, 1), (0, 2), (1, 2)]
-
-    def step(index, carry):
-        fields = []
-        for a in range(2):
-            parts = []
-            for c in range(2):
-                taken = [gathered_ref[a * 4 + b, 2 * index + c] for b in range(4)]
-                parts.append(
-                    jnp.concatenate(
-                        [
-                            taken[b][:, f * elems : (f + 1) * elems]
-                            for f in range(4)
-                            for b in range(4)
-                        ],
-                        axis=0,
-                    )
-                )
-            fields.append(dot(matrix_ref[a], jnp.concatenate(parts, axis=1)))
-        weighted = fields[0]
-        adjoint = fields[1].astype(jnp.bfloat16).astype(jnp.float32)
-        split = 6 * FULL
-        shape = (2, 3, FULL // 8, 8, 2 * elems)
-        tail = (3, 8, 2 * elems)
+    split = 6 * FULL
+    shape = (2, 3, FULL // 8, 8, 2 * elems)
+    tail = (3, 8, 2 * elems)
+    for index in range(columns // 2):
+        weighted = fields(0, index)
+        adjoint = fields(1, index).astype(jnp.bfloat16).astype(jnp.float32)
         weighted, weighted_tail = weighted[:split].reshape(shape), weighted[split:].reshape(tail)
         adjoint, adjoint_tail = adjoint[:split].reshape(shape), adjoint[split:].reshape(tail)
         for m, (i, j) in enumerate(pairs):
@@ -244,11 +251,8 @@
                 rest = rest + adjoint_tail[j] * weighted_tail[i]
             total = jnp.sum(products, axis=(0, 1)) + rest
             for c in range(2):
-                start = pl.multiple_of((m * columns + 2 * index + c) * 8, 8)
-                sums_ref[pl.ds(start, 8), :] = total[:, c * elems : (c + 1) * elems]
-        return carry
-
-    lax.fori_loop(0, columns // 2, step, 0, unroll=UNROLL)
+                start = (m * columns + 2 * index + c) * 8
+                sums_ref[start : start + 8, :] = total[:, c * elems : (c + 1) * elems]
 
     width = 6 * columns
     total = sums_ref[pl.ds(0, width, stride=8), :]
@@ -323,13 +327,14 @@
         halos.append(lax.ppermute(packed[1 + k], "sub", [(i, int(j)) for i, j in pairs]))
 
     slots = owners * capacity
+    tiles = -(-(n_sub + 1) // (128 // rows - 1))
     matrix = solver[0].transpose(1, 0, 2)
     fixed = pl.pallas_call(
         lambda *refs: prepare_kernel(n_sub, capacity, columns, *refs),
         in_specs=[vmem] * 2 + [hbm] * N_SMALL,
         out_shape=[
             pltpu.VMEM((8, BLOCK, 4 * elems), jnp.bfloat16),
-            pltpu.VMEM((4, elems), jnp.int32),
+            pltpu.VMEM((4 * tiles, elems), jnp.int32),
             pltpu.VMEM((2, ROWS, BLOCK), jnp.bfloat16),
             pltpu.VMEM((slots, elems), jnp.bfloat16),
             pltpu.VMEM((1, elems), jnp.float32),
@@ -370,7 +375,7 @@
         ],
         compiler_params=params,
         name="elements",
-    )(*fixed, *halos)
+    )(*fixed, *[halos[i] for i in halo_order(n_sub)])
     got = lax.all_to_all(sent, ("dom", "sub"), split_axis=0, concat_axis=0, tiled=True)
     summed = pl.pallas_call(
         lambda *refs: voxel_kernel(width, *refs),

time: 25.2 us -> 25 us (level)
  starting transfers between devices: 4.58 us -> 6.16 us
  blocking collectives: 11.6 us -> 10.7 us
  waiting for transfers between devices: 1.27 us -> 0.75 us
  Pallas kernels: 7.49 us -> 7.13 us
    ppermute x2, starting transfers between devices: 3.09 us -> 4.67 us  [per_device(): halos.append(lax.ppermute(part, ('dom', 'sub', 'rhs'), pairs))]
    all_to_all x1, blocking collectives: 11.6 us -> 10.7 us  [per_device(): lax.all_to_all(sent, ('dom', 'sub'), split_axis=0, concat_axis=0, tiled=T...]
    ppermute x1, waiting for transfers between devices: 1.27 us -> 0.74 us  [per_device(): lax.ppermute(packed[1 + k], 'sub', [(i, int(j)) for i, j in pairs])]
    pallas_call x1, Pallas kernels: 2.95 us -> 2.62 us  [per_device(): pl.pallas_call(lambda *refs: prepare_kernel(n_sub, capacity, columns, *re...]
  transfers between devices with their start and end apart: 3 -> 3, of which waited for: 1 -> 1; matrix products, arithmetic and copies ran while one was open for 0% -> 0% of each run, Pallas kernels for 12% -> 11%
where the time goes in v6:
time: 25 us; the launch traced here: 24.8 us
  blocking collectives  10.7 us (43%)
  Pallas kernels  7.13 us (29%)
  starting transfers between devices  6.16 us (25%)
  waiting for transfers between devices  0.75 us (3%)
    all_to_all x1, blocking collectives, per_device(): lax.all_to_all(sent, ('dom', 'sub'), split_axis=0, concat_axis=0, tiled=T...  10.7 us
    ppermute x2, starting transfers between devices, per_device(): halos.append(lax.ppermute(part, ('dom', 'sub', 'rhs'), pairs))  4.67 us
    pallas_call x1, Pallas kernels, per_device(): pl.pallas_call(lambda *refs: prepare_kernel(n_sub, capacity, columns, *re...  2.62 us
    pallas_call x1, Pallas kernels, per_device(): pl.pallas_call(lambda *refs: element_kernel(columns, *refs), out_shape=ja...  1.92 us
    pallas_call x1, Pallas kernels, per_device(): pl.pallas_call(lambda *refs: pack_kernel(n_sub, rows, *refs), in_specs=[h...  1.7 us
    ppermute x1, starting transfers between devices, per_device(): lax.ppermute(packed[1 + k], 'sub', [(i, int(j)) for i, j in pairs])  1.49 us
    pallas_call x1, Pallas kernels, per_device(): pl.pallas_call(lambda *refs: voxel_kernel(width, *refs), out_shape=jax.Sh...  0.89 us
    ppermute x1, waiting for transfers between devices, per_device(): lax.ppermute(packed[1 + k], 'sub', [(i, int(j)) for i, j in pairs])  0.74 us
  transfers between devices with their start and end apart: 3, of which 1 were waited for; matrix products, arithmetic and copies ran while one was open for 0% of the time, Pallas kernels for 11%

profile of v6, /device:TPU:0, one launch (start us, length us, event | category | flops | bytes accessed | tf_op | source)
XLA Modules:
  0.0 24.8 jit_solution(17937199308115623821)
XLA Ops:
  0.0 1.7 %pack.1 = (bf16[1920,256]{1,0:T(8,128)(2,1)S(1)}, s32[2,32]{1,0:T(2,128)S(1)}, bf16[32,1920]{1,0:T(8,128)(2,1)S(1)}, bf16[32,1920]{1,0:T(8,128)(2,1)S(1)}, bf16[32,1920]{1,0:T(8,128)(2,1)S(1)}) custom-call(bf16[1920,256]{1,0:T(8,128)(2,1)} %bitcast.13, s32[2,32]{1,0:T(2,128)} %refs_1_.1, s32[2,32]{1,0:T(2,128)} %refs_2_.2), custom_call_target="tpu_custom_call" | custom-call | tf_op jit(solution)/shard_map/pack/pallas_call | solution.py:297
  1.7 0.5 %collective-permute-start = (bf16[32,1920]{1,0:T(8,128)(2,1)S(1)}, bf16[32,1920]{1,0:T(8,128)(2,1)S(1)}, u32[]{:S(2)}, u32[]{:S(2)}) collective-permute-start(bf16[32,1920]{1,0:T(8,128)(2,1)S(1)} %get-tuple-element.24), channel_id=1, source_target_pairs={{0,1},{1,0},{2,3},{3,2},{4,8},{5,9},{6,10},{7,11},{8,4},{9,5},{10,... | collective-permute-start | bytes 368648 | tf_op jit(solution)/shard_map/ppermute | solution.py:324
  2.2 4.1 %collective-permute-start.1 = (bf16[32,1920]{1,0:T(8,128)(2,1)S(1)}, bf16[32,1920]{1,0:T(8,128)(2,1)S(1)}, u32[]{:S(2)}, u32[]{:S(2)}) collective-permute-start(bf16[32,1920]{1,0:T(8,128)(2,1)S(1)} %get-tuple-element.25), channel_id=1, source_target_pairs={{0,4},{1,5},{2,6},{3,7},{4,0},{5,1},{6,2},{7,3},{8,12},{9,13},{10,... | collective-permute-start | bytes 368648 | tf_op jit(solution)/shard_map/ppermute | solution.py:324
  6.4 1.5 %collective-permute-start.2 = (bf16[32,1920]{1,0:T(8,128)(2,1)S(1)}, bf16[32,1920]{1,0:T(8,128)(2,1)S(1)}, u32[]{:S(2)}, u32[]{:S(2)}) collective-permute-start(bf16[32,1920]{1,0:T(8,128)(2,1)S(1)} %get-tuple-element.26), channel_id=1, source_target_pairs={{0,2},{2,0},{1,3},{3,1},{4,6},{6,4},{5,7},{7,5},{8,10},{10,8},{9,1... | collective-permute-start | bytes 368648 | tf_op jit(solution)/shard_map/ppermute | solution.py:327
  7.9 2.6 %prepare.1 = (bf16[8,256,512]{2,1,0:T(8,128)(2,1)S(1)}, s32[4,128]{1,0:T(4,128)S(1)}, bf16[2,216,256]{2,1,0:T(8,128)(2,1)S(1)}, bf16[384,128]{1,0:T(8,128)(2,1)S...) custom-call(s32[2,32]{1,0:T(2,128)S(1)} %get-tuple-element.16.refs_0_, bf16[1920,256]{1,0:T(8,128)(2,1)S(1)} %get-tuple-element.17.refs_1_, ...), custom_call_target="tpu_custom_call" | custom-call | flops 536870912 | bytes 4194304 | tf_op jit(solution)/shard_map/prepare/pallas_call | solution.py:332
  10.5 0.0 collective-permute-done.refs_6_
  10.5 0.0 collective-permute-done.1.refs_7_
  10.5 0.7 %collective-permute-done.2.refs_8_ = bf16[32,1920]{1,0:T(8,128)(2,1)S(1)} collective-permute-done((bf16[32,1920]{1,0:T(8,128)(2,1)S(1)}, bf16[32,1920]{1,0:T(8,128)(2,1)S(1)}, u32[]{:S(2)}, u32[]{:S(2)}) %collective-permute-start.2) | collective-permute-done | bytes 122912 | tf_op jit(solution)/shard_map/ppermute | solution.py:327
  11.3 1.9 %elements.1 = bf16[384,128]{1,0:T(8,128)(2,1)S(1)} custom-call(bf16[8,256,512]{2,1,0:T(8,128)(2,1)S(1)} %get-tuple-element.18.refs_0_, s32[4,128]{1,0:T(4,128)S(1)} %get-tuple-element.19.refs_1_, bf16[2,216,256]{2,1,0:T(8,128)(2,1)S(1)} %get-tuple-element.20.refs_2_, bf16[384,128]{1,0:T(8,128)(2,1)S(1)} %get-tuple-element.21.refs_3_, ...), custom_call_target="tpu_custom_call" | custom-call | tf_op jit(solution)/shard_map/elements/pallas_call | solution.py:369
  13.2 10.7 %all_to_all.11 = bf16[8,48,128]{2,1,0:T(8,128)(2,1)S(1)} all-to-all(bf16[8,48,128]{2,1,0:T(8,128)(2,1)S(1)} %bitcast.11), channel_id=1, replica_groups=mesh['groups'=2,'dom'=4,'sub'=2,'rhs'=2] {'dom','sub'}, dimensions={0} | all-to-all | bytes 196608 | tf_op jit(solution)/shard_map/all_to_all | solution.py:379
  23.9 0.9 %voxels.1 = f32[96,128]{1,0:T(8,128)} custom-call(bf16[384,128]{1,0:T(8,128)(2,1)S(1)} %bitcast.12), custom_call_target="tpu_custom_call" | custom-call | tf_op jit(solution)/shard_map/voxels/pallas_call | solution.py:380
Async XLA Ops:
  1.7 8.8 %collective-permute-start = (bf16[32,1920]{1,0:T(8,128)(2,1)S(1)}, bf16[32,1920]{1,0:T(8,128)(2,1)S(1)}, u32[]{:S(2)}, u32[]{:S(2)}) collective-permute-start(bf16[32,1920]{1,0:T(8,128)(2,1)S(1)} %get-tuple-element.24), channel_id=1, source_target_pairs={{0,1},{1,0},{2,3},{3,2},{4,8},{5,9},{6,10},{7,11},{8,4},{9,5},{10,... | collective-permute-start | bytes 368648 | tf_op jit(solution)/shard_map/ppermute | solution.py:324
  2.2 8.3 %collective-permute-start.1 = (bf16[32,1920]{1,0:T(8,128)(2,1)S(1)}, bf16[32,1920]{1,0:T(8,128)(2,1)S(1)}, u32[]{:S(2)}, u32[]{:S(2)}) collective-permute-start(bf16[32,1920]{1,0:T(8,128)(2,1)S(1)} %get-tuple-element.25), channel_id=1, source_target_pairs={{0,4},{1,5},{2,6},{3,7},{4,0},{5,1},{6,2},{7,3},{8,12},{9,13},{10,... | collective-permute-start | bytes 368648 | tf_op jit(solution)/shard_map/ppermute | solution.py:324
  6.4 4.9 %collective-permute-start.2 = (bf16[32,1920]{1,0:T(8,128)(2,1)S(1)}, bf16[32,1920]{1,0:T(8,128)(2,1)S(1)}, u32[]{:S(2)}, u32[]{:S(2)}) collective-permute-start(bf16[32,1920]{1,0:T(8,128)(2,1)S(1)} %get-tuple-element.26), channel_id=1, source_target_pairs={{0,2},{2,0},{1,3},{3,1},{4,6},{6,4},{5,7},{7,5},{8,10},{10,8},{9,1... | collective-permute-start | bytes 368648 | tf_op jit(solution)/shard_map/ppermute | solution.py:327

commit v7 on v6

--- a/solution.py
+++ b/solution.py
@@ -1,3 +1,4 @@
+import itertools
 import math
 
 import jax
@@ -40,8 +41,10 @@
     return lax.rem(index + k, size), lax.rem(index + size - k, size)
 
 
-def halo_order(n_sub):
-    return [1, 0] + list(range(2, n_sub + 1))
+def swapped(messages):
+    first = lax.axis_index("rhs") == 0
+    one, two = messages[1], messages[2]
+    return [messages[0], jnp.where(first, one, two), jnp.where(first, two, one)] + messages[3:]
 
 
 def pack_kernel(n_sub, rows, traces_hbm, dom_hbm, sub_hbm, table_ref, sub_ref, *refs):
@@ -55,9 +58,10 @@
         copy.wait()
     parity = lax.rem(lax.axis_index("dom"), 2)
     within = lax.axis_index("sub")
-    lists = [dom_ref[pl.ds(1 - parity, 1), :], dom_ref[pl.ds(parity, 1), :]]
+    lists = [dom_ref[pl.ds(parity, 1), :], dom_ref[pl.ds(1 - parity, 1), :]]
     for k in range(1, n_sub):
         lists.append(sub_ref[pl.ds(pair_index(within, k, n_sub)[0], 1), :])
+    lists = swapped(lists)
     face = iota((faces, rows), 0)
     picks = [jnp.where(face == row, 1.0, 0.0).T for row in lists]
     picks = jnp.concatenate(picks, axis=0).astype(jnp.bfloat16)
@@ -149,10 +153,10 @@
     own = jnp.concatenate(own, axis=1)
     for b in range(8):
         own_ref[b] = dot(mine_ref[b], own).astype(jnp.bfloat16)
-    blocks = [1 - parity, parity]
+    blocks = [parity, 1 - parity]
     for k in range(1, n_sub):
         blocks.append(2 + pair_index(within, k, n_sub)[1])
-    blocks = [blocks[i] for i in halo_order(n_sub)]
+    blocks = swapped(blocks)
     per_tile = 128 // rows - 1
     for t in range(places_ref.shape[0] // 4):
         lane = jnp.full(elem_face.shape, 127, jnp.int32)
@@ -309,23 +313,23 @@
     )(*in_hbm(table, dom_lists, sub_lists))
 
     n_rhs = lax.axis_size("rhs")
+
+    def partner(message, d, s, c):
+        if message < 2:
+            other = d + 1 if (d + message) % 2 else d - 1
+            if 0 <= other < n_dom:
+                return other, s, c
+            return d, s, n_rhs - 1 - c
+        return d, int(pair_index(s, message - 1, n_sub)[0]), c
+
     halos = []
-    for odd, part in enumerate(packed[:2]):
+    for k, part in enumerate(packed):
         pairs = []
-        for d in range(n_dom):
-            other = d + 1 if (d - odd) % 2 == 0 else d - 1
-            inside = 0 <= other < n_dom
-            for s in range(n_sub):
-                for c in range(n_rhs):
-                    target = (other * n_sub + s) * n_rhs + c
-                    if not inside:
-                        target = (d * n_sub + s) * n_rhs + n_rhs - 1 - c
-                    pairs.append(((d * n_sub + s) * n_rhs + c, target))
+        for d, s, c in itertools.product(range(n_dom), range(n_sub), range(n_rhs)):
+            message = 3 - k if c and k in (1, 2) else k
+            to_d, to_s, to_c = partner(message, d, s, c)
+            pairs.append(((d * n_sub + s) * n_rhs + c, (to_d * n_sub + to_s) * n_rhs + to_c))
         halos.append(lax.ppermute(part, ("dom", "sub", "rhs"), pairs))
-    for k in range(1, n_sub):
-        pairs = [(i, pair_index(i, k, n_sub)[0]) for i in range(n_sub)]
-        halos.append(lax.ppermute(packed[1 + k], "sub", [(i, int(j)) for i, j in pairs]))
-
     slots = owners * capacity
     tiles = -(-(n_sub + 1) // (128 // rows - 1))
     matrix = solver[0].transpose(1, 0, 2)
@@ -371,11 +375,11 @@
         out_shape=jax.ShapeDtypeStruct((slots, 128), jnp.bfloat16),
         scratch_shapes=[
             pltpu.VMEM((8, columns, BLOCK // columns, 4 * elems), jnp.bfloat16),
-            pltpu.VMEM((8 * width, elems), jnp.float32),
+            pltpu.VMEM((8 * width + 8, elems), jnp.float32),
         ],
         compiler_params=params,
         name="elements",
-    )(*fixed, *[halos[i] for i in halo_order(n_sub)])
+    )(*fixed, *halos)
     got = lax.all_to_all(sent, ("dom", "sub"), split_axis=0, concat_axis=0, tiled=True)
     summed = pl.pallas_call(
         lambda *refs: voxel_kernel(width, *refs),

time: 25 us -> 25 us (level)
    ppermute x1 -> x0, starting transfers between devices: 1.49 us -> none  [per_device(): lax.ppermute(packed[1 + k], 'sub', [(i, int(j)) for i, j in pairs])]
    ppermute x2 -> x3, starting transfers between devices: 4.67 us -> 6.16 us  [per_device(): halos.append(lax.ppermute(part, ('dom', 'sub', 'rhs'), pairs))]
    ppermute x1 -> x0, waiting for transfers between devices: 0.74 us -> none  [per_device(): lax.ppermute(packed[1 + k], 'sub', [(i, int(j)) for i, j in pairs])]
    ppermute x2 -> x3, waiting for transfers between devices: 0.01 us -> 0.74 us  [per_device(): halos.append(lax.ppermute(part, ('dom', 'sub', 'rhs'), pairs))]
where the time goes in v7:
time: 25 us; the launch traced here: 24.8 us
  blocking collectives  10.7 us (43%)
  Pallas kernels  7.14 us (29%)
  starting transfers between devices  6.16 us (25%)
  waiting for transfers between devices  0.74 us (3%)
    all_to_all x1, blocking collectives, per_device(): lax.all_to_all(sent, ('dom', 'sub'), split_axis=0, concat_axis=0, tiled=T...  10.7 us
    ppermute x3, starting transfers between devices, per_device(): halos.append(lax.ppermute(part, ('dom', 'sub', 'rhs'), pairs))  6.16 us
    pallas_call x1, Pallas kernels, per_device(): pl.pallas_call(lambda *refs: prepare_kernel(n_sub, capacity, columns, *re...  2.62 us
    pallas_call x1, Pallas kernels, per_device(): pl.pallas_call(lambda *refs: element_kernel(columns, *refs), out_shape=ja...  1.93 us
    pallas_call x1, Pallas kernels, per_device(): pl.pallas_call(lambda *refs: pack_kernel(n_sub, rows, *refs), in_specs=[h...  1.7 us
    pallas_call x1, Pallas kernels, per_device(): pl.pallas_call(lambda *refs: voxel_kernel(width, *refs), out_shape=jax.Sh...  0.89 us
    ppermute x3, waiting for transfers between devices, per_device(): halos.append(lax.ppermute(part, ('dom', 'sub', 'rhs'), pairs))  0.74 us
  transfers between devices with their start and end apart: 3, of which 1 were waited for; matrix products, arithmetic and copies ran while one was open for 0% of the time, Pallas kernels for 11%

profile of v7, /device:TPU:0, one launch (start us, length us, event | category | flops | bytes accessed | tf_op | source)
XLA Modules:
  0.0 24.8 jit_solution(2571703333482070119)
XLA Ops:
  0.0 1.7 %pack.1 = (bf16[1920,256]{1,0:T(8,128)(2,1)S(1)}, s32[2,32]{1,0:T(2,128)S(1)}, bf16[32,1920]{1,0:T(8,128)(2,1)S(1)}, bf16[32,1920]{1,0:T(8,128)(2,1)S(1)}, bf16[32,1920]{1,0:T(8,128)(2,1)S(1)}) custom-call(bf16[1920,256]{1,0:T(8,128)(2,1)} %bitcast.13, s32[2,32]{1,0:T(2,128)} %refs_1_.1, s32[2,32]{1,0:T(2,128)} %refs_2_.2), custom_call_target="tpu_custom_call" | custom-call | tf_op jit(solution)/shard_map/pack/pallas_call | solution.py:301
  1.7 0.5 %collective-permute-start = (bf16[32,1920]{1,0:T(8,128)(2,1)S(1)}, bf16[32,1920]{1,0:T(8,128)(2,1)S(1)}, u32[]{:S(2)}, u32[]{:S(2)}) collective-permute-start(bf16[32,1920]{1,0:T(8,128)(2,1)S(1)} %get-tuple-element.24), channel_id=1, source_target_pairs={{0,1},{1,0},{2,3},{3,2},{4,8},{5,9},{6,10},{7,11},{8,4},{9,5},{10,... | collective-permute-start | bytes 368648 | tf_op jit(solution)/shard_map/ppermute | solution.py:332
  2.2 4.1 %collective-permute-start.1 = (bf16[32,1920]{1,0:T(8,128)(2,1)S(1)}, bf16[32,1920]{1,0:T(8,128)(2,1)S(1)}, u32[]{:S(2)}, u32[]{:S(2)}) collective-permute-start(bf16[32,1920]{1,0:T(8,128)(2,1)S(1)} %get-tuple-element.25), channel_id=1, source_target_pairs={{0,4},{1,3},{2,6},{3,1},{4,0},{5,7},{6,2},{7,5},{8,12},{9,11},{10,... | collective-permute-start | bytes 368648 | tf_op jit(solution)/shard_map/ppermute | solution.py:332
  6.4 1.5 %collective-permute-start.2 = (bf16[32,1920]{1,0:T(8,128)(2,1)S(1)}, bf16[32,1920]{1,0:T(8,128)(2,1)S(1)}, u32[]{:S(2)}, u32[]{:S(2)}) collective-permute-start(bf16[32,1920]{1,0:T(8,128)(2,1)S(1)} %get-tuple-element.26), channel_id=1, source_target_pairs={{0,2},{1,5},{2,0},{3,7},{4,6},{5,1},{6,4},{7,3},{8,10},{9,13},{10,... | collective-permute-start | bytes 368648 | tf_op jit(solution)/shard_map/ppermute | solution.py:332
  7.9 2.6 %prepare.1 = (bf16[8,256,512]{2,1,0:T(8,128)(2,1)S(1)}, s32[4,128]{1,0:T(4,128)S(1)}, bf16[2,216,256]{2,1,0:T(8,128)(2,1)S(1)}, bf16[384,128]{1,0:T(8,128)(2,1)S...) custom-call(s32[2,32]{1,0:T(2,128)S(1)} %get-tuple-element.16.refs_0_, bf16[1920,256]{1,0:T(8,128)(2,1)S(1)} %get-tuple-element.17.refs_1_, ...), custom_call_target="tpu_custom_call" | custom-call | flops 536870912 | bytes 4194304 | tf_op jit(solution)/shard_map/prepare/pallas_call | solution.py:336
  10.5 0.0 collective-permute-done.refs_6_
  10.5 0.0 collective-permute-done.1.refs_7_
  10.5 0.7 %collective-permute-done.2.refs_8_ = bf16[32,1920]{1,0:T(8,128)(2,1)S(1)} collective-permute-done((bf16[32,1920]{1,0:T(8,128)(2,1)S(1)}, bf16[32,1920]{1,0:T(8,128)(2,1)S(1)}, u32[]{:S(2)}, u32[]{:S(2)}) %collective-permute-start.2) | collective-permute-done | bytes 122912 | tf_op jit(solution)/shard_map/ppermute | solution.py:332
  11.3 1.9 %elements.1 = bf16[384,128]{1,0:T(8,128)(2,1)S(1)} custom-call(bf16[8,256,512]{2,1,0:T(8,128)(2,1)S(1)} %get-tuple-element.18.refs_0_, s32[4,128]{1,0:T(4,128)S(1)} %get-tuple-element.19.refs_1_, bf16[2,216,256]{2,1,0:T(8,128)(2,1)S(1)} %get-tuple-element.20.refs_2_, bf16[384,128]{1,0:T(8,128)(2,1)S(1)} %get-tuple-element.21.refs_3_, ...), custom_call_target="tpu_custom_call" | custom-call | tf_op jit(solution)/shard_map/elements/pallas_call | solution.py:373
  13.2 10.7 %all_to_all.11 = bf16[8,48,128]{2,1,0:T(8,128)(2,1)S(1)} all-to-all(bf16[8,48,128]{2,1,0:T(8,128)(2,1)S(1)} %bitcast.11), channel_id=1, replica_groups=mesh['groups'=2,'dom'=4,'sub'=2,'rhs'=2] {'dom','sub'}, dimensions={0} | all-to-all | bytes 196608 | tf_op jit(solution)/shard_map/all_to_all | solution.py:383
  23.9 0.9 %voxels.1 = f32[96,128]{1,0:T(8,128)} custom-call(bf16[384,128]{1,0:T(8,128)(2,1)S(1)} %bitcast.12), custom_call_target="tpu_custom_call" | custom-call | tf_op jit(solution)/shard_map/voxels/pallas_call | solution.py:384
Async XLA Ops:
  1.7 8.8 %collective-permute-start = (bf16[32,1920]{1,0:T(8,128)(2,1)S(1)}, bf16[32,1920]{1,0:T(8,128)(2,1)S(1)}, u32[]{:S(2)}, u32[]{:S(2)}) collective-permute-start(bf16[32,1920]{1,0:T(8,128)(2,1)S(1)} %get-tuple-element.24), channel_id=1, source_target_pairs={{0,1},{1,0},{2,3},{3,2},{4,8},{5,9},{6,10},{7,11},{8,4},{9,5},{10,... | collective-permute-start | bytes 368648 | tf_op jit(solution)/shard_map/ppermute | solution.py:332
  2.2 8.3 %collective-permute-start.1 = (bf16[32,1920]{1,0:T(8,128)(2,1)S(1)}, bf16[32,1920]{1,0:T(8,128)(2,1)S(1)}, u32[]{:S(2)}, u32[]{:S(2)}) collective-permute-start(bf16[32,1920]{1,0:T(8,128)(2,1)S(1)} %get-tuple-element.25), channel_id=1, source_target_pairs={{0,4},{1,3},{2,6},{3,1},{4,0},{5,7},{6,2},{7,5},{8,12},{9,11},{10,... | collective-permute-start | bytes 368648 | tf_op jit(solution)/shard_map/ppermute | solution.py:332
  6.4 4.9 %collective-permute-start.2 = (bf16[32,1920]{1,0:T(8,128)(2,1)S(1)}, bf16[32,1920]{1,0:T(8,128)(2,1)S(1)}, u32[]{:S(2)}, u32[]{:S(2)}) collective-permute-start(bf16[32,1920]{1,0:T(8,128)(2,1)S(1)} %get-tuple-element.26), channel_id=1, source_target_pairs={{0,2},{1,5},{2,0},{3,7},{4,6},{5,1},{6,4},{7,3},{8,10},{9,13},{10,... | collective-permute-start | bytes 368648 | tf_op jit(solution)/shard_map/ppermute | solution.py:332

commit v8 on v7

--- a/solution.py
+++ b/solution.py
@@ -52,8 +52,8 @@
     faces = table_ref.shape[1]
     pairs = [(dom_hbm, dom_ref), (sub_hbm, sub_ref), (traces_hbm, table_ref)]
     copies = [pltpu.make_async_copy(*pair, sems.at[i]) for i, pair in enumerate(pairs)]
-    for copy in copies:
-        copy.start()
+    for i in (2, 0, 1):
+        copies[i].start()
     for copy in copies[:2]:
         copy.wait()
     parity = lax.rem(lax.axis_index("dom"), 2)
@@ -151,8 +151,8 @@
         index = jnp.where(inside, found, elem_face[f : f + 1, :])
         own.append(one_hot(iota((faces, elems), 0) == index))
     own = jnp.concatenate(own, axis=1)
-    for b in range(8):
-        own_ref[b] = dot(mine_ref[b], own).astype(jnp.bfloat16)
+    mine = mine_ref[...].reshape(8 * BLOCK, faces)
+    own_ref[...] = dot(mine, own).astype(jnp.bfloat16).reshape(own_ref.shape)
     blocks = [parity, 1 - parity]
     for k in range(1, n_sub):
         blocks.append(2 + pair_index(within, k, n_sub)[1])
@@ -207,21 +207,39 @@
         parts = [ref[...] for ref in halo_refs[t * per_tile : (t + 1) * per_tile]]
         parts.append(jnp.zeros((128 - rows * len(parts), values), jnp.bfloat16))
         tables.append(jnp.concatenate(parts, axis=0))
-    lanes = [jnp.broadcast_to(places_ref[i : i + 1, :], (BLOCK, elems)) for i in range(4 * tiles)]
     starts = block_starts(columns)
-
-    def gather(b):
-        part = slice(starts[b], starts[b] + BLOCK)
-        others = [dot(reorder, table[:, part], NT) for table in tables]
-        for f in range(4):
-            part = slice(f * elems, (f + 1) * elems)
-            got = own_ref[b, :, part]
-            for t in range(tiles):
-                found = jnp.take_along_axis(
-                    others[t], lanes[4 * t + f], axis=1, mode="promise_in_bounds"
-                )
-                got = got + found.astype(jnp.bfloat16)
-            gathered_ref[b, :, :, part] = got.reshape(columns, per_block, elems)
+    found = 0.0
+    others = []
+    for t in range(tiles):
+        blocks = []
+        for b in range(0, 8, 2):
+            pair = [tables[t][:, start : start + BLOCK] for start in starts[b : b + 2]]
+            pair = dot(reorder, jnp.concatenate(pair, axis=0), NT)
+            blocks += [pair[:, :128], pair[:, 128:]]
+        others.append(blocks)
+        hot = [
+            one_hot(iota((128, elems), 0) == places_ref[i : i + 1, :])
+            for i in range(4 * t, 4 * t + 3)
+        ]
+        stacked = jnp.concatenate([x.astype(jnp.bfloat16) for x in blocks], axis=0)
+        found = found + dot(stacked, jnp.concatenate(hot, axis=1))
+    found = found.astype(jnp.bfloat16)
+    lanes = [
+        jnp.broadcast_to(places_ref[4 * t + 3 : 4 * t + 4, :], (BLOCK, elems))
+        for t in range(tiles)
+    ]
+    for b in range(8):
+        part = slice(0, 3 * elems)
+        got = own_ref[b, :, part] + found[b * BLOCK : (b + 1) * BLOCK]
+        gathered_ref[b, :, :, part] = got.reshape(columns, per_block, 3 * elems)
+        part = slice(3 * elems, 4 * elems)
+        got = own_ref[b, :, part]
+        for t in range(tiles):
+            last = jnp.take_along_axis(
+                others[t][b], lanes[t], axis=1, mode="promise_in_bounds"
+            )
+            got = got + last.astype(jnp.bfloat16)
+        gathered_ref[b, :, :, part] = got.reshape(columns, per_block, elems)
 
     def fields(a, index):
         parts = []
@@ -234,9 +252,6 @@
                 )
             )
         return dot(matrix_ref[a], jnp.concatenate(parts, axis=1))
-
-    for b in range(8):
-        gather(b)
 
     pairs = [(0, 0), (1, 1), (2, 2), (0, 1), (0, 2), (1, 2)]
     split = 6 * FULL
@@ -272,9 +287,9 @@
 
 def voxel_kernel(width, got_ref, out_ref):
     got = got_ref[...]
-    slot = got[:, width : width + 1].astype(jnp.int32)
+    slot = got[:, width : width + 1].astype(jnp.float32)
     voxels = out_ref.shape[1]
-    members = one_hot(slot == iota((got.shape[0], voxels), 1))
+    members = one_hot(slot == iota((got.shape[0], voxels), 1).astype(jnp.float32))
     out_ref[...] = dot(got, members, TN)[:width]
 
 

time: 25 us -> 24.8 us (level)
  no operation moved by 1% of the time
where the time goes in v8:
time: 24.8 us; the launch traced here: 24.6 us
  blocking collectives  10.7 us (43%)
  Pallas kernels  6.95 us (28%)
  starting transfers between devices  6.16 us (25%)
  waiting for transfers between devices  0.75 us (3%)
    all_to_all x1, blocking collectives, per_device(): lax.all_to_all(sent, ('dom', 'sub'), split_axis=0, concat_axis=0, tiled=T...  10.7 us
    ppermute x3, starting transfers between devices, per_device(): halos.append(lax.ppermute(part, ('dom', 'sub', 'rhs'), pairs))  6.16 us
    pallas_call x1, Pallas kernels, per_device(): pl.pallas_call(lambda *refs: prepare_kernel(n_sub, capacity, columns, *re...  2.62 us
    pallas_call x1, Pallas kernels, per_device(): pl.pallas_call(lambda *refs: element_kernel(columns, *refs), out_shape=ja...  1.8 us
    pallas_call x1, Pallas kernels, per_device(): pl.pallas_call(lambda *refs: pack_kernel(n_sub, rows, *refs), in_specs=[h...  1.67 us
    pallas_call x1, Pallas kernels, per_device(): pl.pallas_call(lambda *refs: voxel_kernel(width, *refs), out_shape=jax.Sh...  0.87 us
    ppermute x3, waiting for transfers between devices, per_device(): halos.append(lax.ppermute(part, ('dom', 'sub', 'rhs'), pairs))  0.75 us
  transfers between devices with their start and end apart: 3, of which 1 were waited for; matrix products, arithmetic and copies ran while one was open for 0% of the time, Pallas kernels for 11%

profile of v8, /device:TPU:0, one launch (start us, length us, event | category | flops | bytes accessed | tf_op | source)
XLA Modules:
  0.0 24.6 jit_solution(2508428374952980855)
XLA Ops:
  0.0 1.7 %pack.1 = (bf16[1920,256]{1,0:T(8,128)(2,1)S(1)}, s32[2,32]{1,0:T(2,128)S(1)}, bf16[32,1920]{1,0:T(8,128)(2,1)S(1)}, bf16[32,1920]{1,0:T(8,128)(2,1)S(1)}, bf16[32,1920]{1,0:T(8,128)(2,1)S(1)}) custom-call(bf16[1920,256]{1,0:T(8,128)(2,1)} %bitcast.13, s32[2,32]{1,0:T(2,128)} %refs_1_.1, s32[2,32]{1,0:T(2,128)} %refs_2_.2), custom_call_target="tpu_custom_call" | custom-call | tf_op jit(solution)/shard_map/pack/pallas_call | solution.py:316
  1.7 0.5 %collective-permute-start = (bf16[32,1920]{1,0:T(8,128)(2,1)S(1)}, bf16[32,1920]{1,0:T(8,128)(2,1)S(1)}, u32[]{:S(2)}, u32[]{:S(2)}) collective-permute-start(bf16[32,1920]{1,0:T(8,128)(2,1)S(1)} %get-tuple-element.24), channel_id=1, source_target_pairs={{0,1},{1,0},{2,3},{3,2},{4,8},{5,9},{6,10},{7,11},{8,4},{9,5},{10,... | collective-permute-start | bytes 368648 | tf_op jit(solution)/shard_map/ppermute | solution.py:347
  2.2 4.1 %collective-permute-start.1 = (bf16[32,1920]{1,0:T(8,128)(2,1)S(1)}, bf16[32,1920]{1,0:T(8,128)(2,1)S(1)}, u32[]{:S(2)}, u32[]{:S(2)}) collective-permute-start(bf16[32,1920]{1,0:T(8,128)(2,1)S(1)} %get-tuple-element.25), channel_id=1, source_target_pairs={{0,4},{1,3},{2,6},{3,1},{4,0},{5,7},{6,2},{7,5},{8,12},{9,11},{10,... | collective-permute-start | bytes 368648 | tf_op jit(solution)/shard_map/ppermute | solution.py:347
  6.3 1.5 %collective-permute-start.2 = (bf16[32,1920]{1,0:T(8,128)(2,1)S(1)}, bf16[32,1920]{1,0:T(8,128)(2,1)S(1)}, u32[]{:S(2)}, u32[]{:S(2)}) collective-permute-start(bf16[32,1920]{1,0:T(8,128)(2,1)S(1)} %get-tuple-element.26), channel_id=1, source_target_pairs={{0,2},{1,5},{2,0},{3,7},{4,6},{5,1},{6,4},{7,3},{8,10},{9,13},{10,... | collective-permute-start | bytes 368648 | tf_op jit(solution)/shard_map/ppermute | solution.py:347
  7.8 2.6 %prepare.1 = (bf16[8,256,512]{2,1,0:T(8,128)(2,1)S(1)}, s32[4,128]{1,0:T(4,128)S(1)}, bf16[2,216,256]{2,1,0:T(8,128)(2,1)S(1)}, bf16[384,128]{1,0:T(8,128)(2,1)S...) custom-call(s32[2,32]{1,0:T(2,128)S(1)} %get-tuple-element.16.refs_0_, bf16[1920,256]{1,0:T(8,128)(2,1)S(1)} %get-tuple-element.17.refs_1_, ...), custom_call_target="tpu_custom_call" | custom-call | flops 536870912 | bytes 4194304 | tf_op jit(solution)/shard_map/prepare/pallas_call | solution.py:351
  10.5 0.0 collective-permute-done.refs_6_
  10.5 0.0 collective-permute-done.1.refs_7_
  10.5 0.7 %collective-permute-done.2.refs_8_ = bf16[32,1920]{1,0:T(8,128)(2,1)S(1)} collective-permute-done((bf16[32,1920]{1,0:T(8,128)(2,1)S(1)}, bf16[32,1920]{1,0:T(8,128)(2,1)S(1)}, u32[]{:S(2)}, u32[]{:S(2)}) %collective-permute-start.2) | collective-permute-done | bytes 122912 | tf_op jit(solution)/shard_map/ppermute | solution.py:347
  11.2 1.8 %elements.1 = bf16[384,128]{1,0:T(8,128)(2,1)S(1)} custom-call(bf16[8,256,512]{2,1,0:T(8,128)(2,1)S(1)} %get-tuple-element.18.refs_0_, s32[4,128]{1,0:T(4,128)S(1)} %get-tuple-element.19.refs_1_, bf16[2,216,256]{2,1,0:T(8,128)(2,1)S(1)} %get-tuple-element.20.refs_2_, bf16[384,128]{1,0:T(8,128)(2,1)S(1)} %get-tuple-element.21.refs_3_, ...), custom_call_target="tpu_custom_call" | custom-call | tf_op jit(solution)/shard_map/elements/pallas_call | solution.py:388
  13.0 10.7 %all_to_all.11 = bf16[8,48,128]{2,1,0:T(8,128)(2,1)S(1)} all-to-all(bf16[8,48,128]{2,1,0:T(8,128)(2,1)S(1)} %bitcast.11), channel_id=1, replica_groups=mesh['groups'=2,'dom'=4,'sub'=2,'rhs'=2] {'dom','sub'}, dimensions={0} | all-to-all | bytes 196608 | tf_op jit(solution)/shard_map/all_to_all | solution.py:398
  23.7 0.9 %voxels.1 = f32[96,128]{1,0:T(8,128)} custom-call(bf16[384,128]{1,0:T(8,128)(2,1)S(1)} %bitcast.12), custom_call_target="tpu_custom_call" | custom-call | tf_op jit(solution)/shard_map/voxels/pallas_call | solution.py:399
Async XLA Ops:
  1.7 8.8 %collective-permute-start = (bf16[32,1920]{1,0:T(8,128)(2,1)S(1)}, bf16[32,1920]{1,0:T(8,128)(2,1)S(1)}, u32[]{:S(2)}, u32[]{:S(2)}) collective-permute-start(bf16[32,1920]{1,0:T(8,128)(2,1)S(1)} %get-tuple-element.24), channel_id=1, source_target_pairs={{0,1},{1,0},{2,3},{3,2},{4,8},{5,9},{6,10},{7,11},{8,4},{9,5},{10,... | collective-permute-start | bytes 368648 | tf_op jit(solution)/shard_map/ppermute | solution.py:347
  2.2 8.3 %collective-permute-start.1 = (bf16[32,1920]{1,0:T(8,128)(2,1)S(1)}, bf16[32,1920]{1,0:T(8,128)(2,1)S(1)}, u32[]{:S(2)}, u32[]{:S(2)}) collective-permute-start(bf16[32,1920]{1,0:T(8,128)(2,1)S(1)} %get-tuple-element.25), channel_id=1, source_target_pairs={{0,4},{1,3},{2,6},{3,1},{4,0},{5,7},{6,2},{7,5},{8,12},{9,11},{10,... | collective-permute-start | bytes 368648 | tf_op jit(solution)/shard_map/ppermute | solution.py:347
  6.3 4.9 %collective-permute-start.2 = (bf16[32,1920]{1,0:T(8,128)(2,1)S(1)}, bf16[32,1920]{1,0:T(8,128)(2,1)S(1)}, u32[]{:S(2)}, u32[]{:S(2)}) collective-permute-start(bf16[32,1920]{1,0:T(8,128)(2,1)S(1)} %get-tuple-element.26), channel_id=1, source_target_pairs={{0,2},{1,5},{2,0},{3,7},{4,6},{5,1},{6,4},{7,3},{8,10},{9,13},{10,... | collective-permute-start | bytes 368648 | tf_op jit(solution)/shard_map/ppermute | solution.py:347

commit v9 on v8

--- a/solution.py
+++ b/solution.py
@@ -43,8 +43,8 @@
 
 def swapped(messages):
     first = lax.axis_index("rhs") == 0
-    one, two = messages[1], messages[2]
-    return [messages[0], jnp.where(first, one, two), jnp.where(first, two, one)] + messages[3:]
+    even, slab = messages[1], messages[2]
+    return [messages[0], jnp.where(first, slab, even), jnp.where(first, even, slab)] + messages[3:]
 
 
 def pack_kernel(n_sub, rows, traces_hbm, dom_hbm, sub_hbm, table_ref, sub_ref, *refs):
@@ -341,7 +341,7 @@
     for k, part in enumerate(packed):
         pairs = []
         for d, s, c in itertools.product(range(n_dom), range(n_sub), range(n_rhs)):
-            message = 3 - k if c and k in (1, 2) else k
+            message = 3 - k if c == 0 and k in (1, 2) else k
             to_d, to_s, to_c = partner(message, d, s, c)
             pairs.append(((d * n_sub + s) * n_rhs + c, (to_d * n_sub + to_s) * n_rhs + to_c))
         halos.append(lax.ppermute(part, ("dom", "sub", "rhs"), pairs))

time: 24.8 us -> 24.6 us (level)
  waiting for transfers between devices: 0.75 us -> 0.22 us
  blocking collectives: 10.7 us -> 11 us
    ppermute x3, waiting for transfers between devices: 0.75 us -> 0.22 us  [per_device(): halos.append(lax.ppermute(part, ('dom', 'sub', 'rhs'), pairs))]
    all_to_all x1, blocking collectives: 10.7 us -> 11 us  [per_device(): lax.all_to_all(sent, ('dom', 'sub'), split_axis=0, concat_axis=0, tiled=T...]
where the time goes in v9:
time: 24.6 us; the launch traced here: 24.3 us
  blocking collectives  11 us (45%)
  Pallas kernels  6.94 us (28%)
  starting transfers between devices  6.16 us (25%)
    all_to_all x1, blocking collectives, per_device(): lax.all_to_all(sent, ('dom', 'sub'), split_axis=0, concat_axis=0, tiled=T...  11 us
    ppermute x3, starting transfers between devices, per_device(): halos.append(lax.ppermute(part, ('dom', 'sub', 'rhs'), pairs))  6.16 us
    pallas_call x1, Pallas kernels, per_device(): pl.pallas_call(lambda *refs: prepare_kernel(n_sub, capacity, columns, *re...  2.62 us
    pallas_call x1, Pallas kernels, per_device(): pl.pallas_call(lambda *refs: element_kernel(columns, *refs), out_shape=ja...  1.79 us
    pallas_call x1, Pallas kernels, per_device(): pl.pallas_call(lambda *refs: pack_kernel(n_sub, rows, *refs), in_specs=[h...  1.67 us
    pallas_call x1, Pallas kernels, per_device(): pl.pallas_call(lambda *refs: voxel_kernel(width, *refs), out_shape=jax.Sh...  0.87 us
  transfers between devices with their start and end apart: 3, of which 1 were waited for; matrix products, arithmetic and copies ran while one was open for 0% of the time, Pallas kernels for 11%

profile of v9, /device:TPU:0, one launch (start us, length us, event | category | flops | bytes accessed | tf_op | source)
XLA Modules:
  0.0 24.3 jit_solution(9788958981759513750)
XLA Ops:
  0.0 1.7 %pack.1 = (bf16[1920,256]{1,0:T(8,128)(2,1)S(1)}, s32[2,32]{1,0:T(2,128)S(1)}, bf16[32,1920]{1,0:T(8,128)(2,1)S(1)}, bf16[32,1920]{1,0:T(8,128)(2,1)S(1)}, bf16[32,1920]{1,0:T(8,128)(2,1)S(1)}) custom-call(bf16[1920,256]{1,0:T(8,128)(2,1)} %bitcast.13, s32[2,32]{1,0:T(2,128)} %refs_1_.1, s32[2,32]{1,0:T(2,128)} %refs_2_.2), custom_call_target="tpu_custom_call" | custom-call | tf_op jit(solution)/shard_map/pack/pallas_call | solution.py:316
  1.7 0.5 %collective-permute-start = (bf16[32,1920]{1,0:T(8,128)(2,1)S(1)}, bf16[32,1920]{1,0:T(8,128)(2,1)S(1)}, u32[]{:S(2)}, u32[]{:S(2)}) collective-permute-start(bf16[32,1920]{1,0:T(8,128)(2,1)S(1)} %get-tuple-element.24), channel_id=1, source_target_pairs={{0,1},{1,0},{2,3},{3,2},{4,8},{5,9},{6,10},{7,11},{8,4},{9,5},{10,... | collective-permute-start | bytes 368648 | tf_op jit(solution)/shard_map/ppermute | solution.py:347
  2.2 2.6 %collective-permute-start.1 = (bf16[32,1920]{1,0:T(8,128)(2,1)S(1)}, bf16[32,1920]{1,0:T(8,128)(2,1)S(1)}, u32[]{:S(2)}, u32[]{:S(2)}) collective-permute-start(bf16[32,1920]{1,0:T(8,128)(2,1)S(1)} %get-tuple-element.25), channel_id=1, source_target_pairs={{0,2},{1,5},{2,0},{3,7},{4,6},{5,1},{6,4},{7,3},{8,10},{9,13},{10,... | collective-permute-start | bytes 368648 | tf_op jit(solution)/shard_map/ppermute | solution.py:347
  4.8 3.1 %collective-permute-start.2 = (bf16[32,1920]{1,0:T(8,128)(2,1)S(1)}, bf16[32,1920]{1,0:T(8,128)(2,1)S(1)}, u32[]{:S(2)}, u32[]{:S(2)}) collective-permute-start(bf16[32,1920]{1,0:T(8,128)(2,1)S(1)} %get-tuple-element.26), channel_id=1, source_target_pairs={{0,4},{1,3},{2,6},{3,1},{4,0},{5,7},{6,2},{7,5},{8,12},{9,11},{10,... | collective-permute-start | bytes 368648 | tf_op jit(solution)/shard_map/ppermute | solution.py:347
  7.8 2.6 %prepare.1 = (bf16[8,256,512]{2,1,0:T(8,128)(2,1)S(1)}, s32[4,128]{1,0:T(4,128)S(1)}, bf16[2,216,256]{2,1,0:T(8,128)(2,1)S(1)}, bf16[384,128]{1,0:T(8,128)(2,1)S...) custom-call(s32[2,32]{1,0:T(2,128)S(1)} %get-tuple-element.16.refs_0_, bf16[1920,256]{1,0:T(8,128)(2,1)S(1)} %get-tuple-element.17.refs_1_, ...), custom_call_target="tpu_custom_call" | custom-call | flops 536870912 | bytes 4194304 | tf_op jit(solution)/shard_map/prepare/pallas_call | solution.py:351
  10.5 0.0 collective-permute-done.refs_6_
  10.5 0.0 collective-permute-done.1.refs_7_
  10.5 0.2 collective-permute-done.2.refs_8_
  10.7 1.8 %elements.1 = bf16[384,128]{1,0:T(8,128)(2,1)S(1)} custom-call(bf16[8,256,512]{2,1,0:T(8,128)(2,1)S(1)} %get-tuple-element.18.refs_0_, s32[4,128]{1,0:T(4,128)S(1)} %get-tuple-element.19.refs_1_, bf16[2,216,256]{2,1,0:T(8,128)(2,1)S(1)} %get-tuple-element.20.refs_2_, bf16[384,128]{1,0:T(8,128)(2,1)S(1)} %get-tuple-element.21.refs_3_, ...), custom_call_target="tpu_custom_call" | custom-call | tf_op jit(solution)/shard_map/elements/pallas_call | solution.py:388
  12.5 11.0 %all_to_all.11 = bf16[8,48,128]{2,1,0:T(8,128)(2,1)S(1)} all-to-all(bf16[8,48,128]{2,1,0:T(8,128)(2,1)S(1)} %bitcast.11), channel_id=1, replica_groups=mesh['groups'=2,'dom'=4,'sub'=2,'rhs'=2] {'dom','sub'}, dimensions={0} | all-to-all | bytes 196608 | tf_op jit(solution)/shard_map/all_to_all | solution.py:398
  23.5 0.9 %voxels.1 = f32[96,128]{1,0:T(8,128)} custom-call(bf16[384,128]{1,0:T(8,128)(2,1)S(1)} %bitcast.12), custom_call_target="tpu_custom_call" | custom-call | tf_op jit(solution)/shard_map/voxels/pallas_call | solution.py:399
Async XLA Ops:
  1.7 8.8 %collective-permute-start = (bf16[32,1920]{1,0:T(8,128)(2,1)S(1)}, bf16[32,1920]{1,0:T(8,128)(2,1)S(1)}, u32[]{:S(2)}, u32[]{:S(2)}) collective-permute-start(bf16[32,1920]{1,0:T(8,128)(2,1)S(1)} %get-tuple-element.24), channel_id=1, source_target_pairs={{0,1},{1,0},{2,3},{3,2},{4,8},{5,9},{6,10},{7,11},{8,4},{9,5},{10,... | collective-permute-start | bytes 368648 | tf_op jit(solution)/shard_map/ppermute | solution.py:347
  2.2 8.3 %collective-permute-start.1 = (bf16[32,1920]{1,0:T(8,128)(2,1)S(1)}, bf16[32,1920]{1,0:T(8,128)(2,1)S(1)}, u32[]{:S(2)}, u32[]{:S(2)}) collective-permute-start(bf16[32,1920]{1,0:T(8,128)(2,1)S(1)} %get-tuple-element.25), channel_id=1, source_target_pairs={{0,2},{1,5},{2,0},{3,7},{4,6},{5,1},{6,4},{7,3},{8,10},{9,13},{10,... | collective-permute-start | bytes 368648 | tf_op jit(solution)/shard_map/ppermute | solution.py:347
  4.8 5.9 %collective-permute-start.2 = (bf16[32,1920]{1,0:T(8,128)(2,1)S(1)}, bf16[32,1920]{1,0:T(8,128)(2,1)S(1)}, u32[]{:S(2)}, u32[]{:S(2)}) collective-permute-start(bf16[32,1920]{1,0:T(8,128)(2,1)S(1)} %get-tuple-element.26), channel_id=1, source_target_pairs={{0,4},{1,3},{2,6},{3,1},{4,0},{5,7},{6,2},{7,5},{8,12},{9,11},{10,... | collective-permute-start | bytes 368648 | tf_op jit(solution)/shard_map/ppermute | solution.py:347

commit v10 on v9

--- a/solution.py
+++ b/solution.py
@@ -96,8 +96,8 @@
 
 def prepare_kernel(n_sub, capacity, columns, sub_ref, table_ref, *refs):
     hbm_refs, refs = refs[:N_SMALL], refs[N_SMALL:]
-    own_ref, places_ref, matrix_ref, sends_ref, volume_ref, slot_ref = refs[:6]
-    solver_ref, mass_ref, elem_ref, owner_ref, mine_ref, sems = refs[6:]
+    own_ref, places_ref, matrix_ref, sends_ref, reorder_ref, hot_ref, scale_ref, slot_ref = refs[:8]
+    solver_ref, mass_ref, elem_ref, owner_ref, volume_ref, mine_ref, sems = refs[8:]
     vmem_refs = [elem_ref, owner_ref, solver_ref, mass_ref, volume_ref, slot_ref]
     copies = [
         pltpu.make_async_copy(hbm_refs[i], vmem_refs[i], sems.at[i]) for i in range(N_SMALL)
@@ -112,6 +112,7 @@
     within = lax.axis_index("sub")
 
     reorder = reorder_matrix(columns)
+    reorder_ref[...] = reorder
     for b, start in enumerate(block_starts(columns)):
         mine = dot(reorder, table_ref[start : start + BLOCK, :])
         mine_ref[b] = mine.astype(jnp.bfloat16)
@@ -164,6 +165,8 @@
             offset = elem_face - (faces + block * rows)
             lane = jnp.where((offset >= 0) & (offset < rows), offset + i * rows, lane)
         places_ref[4 * t : 4 * t + 4, :] = lane
+        hot = [one_hot(iota((128, elems), 0) == lane[f : f + 1, :]) for f in range(3)]
+        hot_ref[t] = jnp.concatenate(hot, axis=1)
 
     solver = solver_ref[:PADDED].astype(jnp.float32)
     solver = jnp.concatenate([solver[:, 0, :], solver[:, 1, :]], axis=0).astype(jnp.bfloat16)
@@ -184,6 +187,11 @@
     target = owner * capacity + rank.astype(jnp.int32)
     sends_ref[...] = one_hot(iota((slots, elems), 0) == target)
 
+    width = 6 * columns
+    norm = 1.0 / math.sqrt(70.0)
+    factor = jnp.where(iota((width, 1), 0) < 3 * columns, norm, 0.5 * norm)
+    scale_ref[...] = factor * volume_ref[...]
+
 
 def element_kernel(
     columns,
@@ -191,15 +199,17 @@
     places_ref,
     matrix_ref,
     sends_ref,
-    volume_ref,
+    reorder_ref,
+    hot_ref,
+    scale_ref,
     slot_ref,
     *refs,
 ):
     halo_refs, (out_ref, gathered_ref, sums_ref) = refs[:-3], refs[-3:]
-    elems = volume_ref.shape[1]
+    elems = scale_ref.shape[1]
     per_block = BLOCK // columns
     tiles = places_ref.shape[0] // 4
-    reorder = reorder_matrix(columns)
+    reorder = reorder_ref[...]
     rows, values = halo_refs[0].shape
     per_tile = 128 // rows - 1
     tables = []
@@ -217,12 +227,8 @@
             pair = dot(reorder, jnp.concatenate(pair, axis=0), NT)
             blocks += [pair[:, :128], pair[:, 128:]]
         others.append(blocks)
-        hot = [
-            one_hot(iota((128, elems), 0) == places_ref[i : i + 1, :])
-            for i in range(4 * t, 4 * t + 3)
-        ]
         stacked = jnp.concatenate([x.astype(jnp.bfloat16) for x in blocks], axis=0)
-        found = found + dot(stacked, jnp.concatenate(hot, axis=1))
+        found = found + dot(stacked, hot_ref[t])
     found = found.astype(jnp.bfloat16)
     lanes = [
         jnp.broadcast_to(places_ref[4 * t + 3 : 4 * t + 4, :], (BLOCK, elems))
@@ -277,9 +283,7 @@
     total = sums_ref[pl.ds(0, width, stride=8), :]
     for k in range(1, 8):
         total = total + sums_ref[pl.ds(k, width, stride=8), :]
-    norm = 1.0 / math.sqrt(70.0)
-    factor = jnp.where(iota((width, 1), 0) < 3 * columns, norm, 0.5 * norm)
-    terms = total * (factor * volume_ref[...])
+    terms = total * scale_ref[...]
     slot = jnp.broadcast_to(slot_ref[...].astype(jnp.float32), (128 - width, elems))
     payload = jnp.concatenate([terms, slot], axis=0).astype(jnp.bfloat16)
     out_ref[...] = dot(sends_ref[...], payload, NT).astype(jnp.bfloat16)
@@ -356,15 +360,18 @@
             pltpu.VMEM((4 * tiles, elems), jnp.int32),
             pltpu.VMEM((2, ROWS, BLOCK), jnp.bfloat16),
             pltpu.VMEM((slots, elems), jnp.bfloat16),
-            pltpu.VMEM((1, elems), jnp.float32),
+            pltpu.VMEM((BLOCK, BLOCK), jnp.bfloat16),
+            pltpu.VMEM((tiles, 128, 3 * elems), jnp.bfloat16),
+            pltpu.VMEM((width, elems), jnp.float32),
             pltpu.VMEM((1, elems), jnp.int32),
         ],
-        out_specs=[vmem] * 6,
+        out_specs=[vmem] * 8,
         scratch_shapes=[
             pltpu.VMEM(matrix.shape, jnp.bfloat16),
             pltpu.VMEM(mass.shape[1:], jnp.bfloat16),
             pltpu.VMEM((4, elems), jnp.int32),
             pltpu.VMEM((1, elems), jnp.int32),
+            pltpu.VMEM((1, elems), jnp.float32),
             pltpu.VMEM((8, BLOCK, faces), jnp.bfloat16),
             pltpu.SemaphoreType.DMA((N_SMALL,)),
         ],

time: 24.6 us -> 24.6 us (level)
  no operation moved by 1% of the time
where the time goes in v10:
time: 24.6 us; the launch traced here: 24.3 us
  blocking collectives  11 us (45%)
  Pallas kernels  7.01 us (28%)
  starting transfers between devices  6.16 us (25%)
    all_to_all x1, blocking collectives, per_device(): lax.all_to_all(sent, ('dom', 'sub'), split_axis=0, concat_axis=0, tiled=T...  11 us
    ppermute x3, starting transfers between devices, per_device(): halos.append(lax.ppermute(part, ('dom', 'sub', 'rhs'), pairs))  6.16 us
    pallas_call x1, Pallas kernels, per_device(): pl.pallas_call(lambda *refs: prepare_kernel(n_sub, capacity, columns, *re...  2.68 us
    pallas_call x1, Pallas kernels, per_device(): pl.pallas_call(lambda *refs: element_kernel(columns, *refs), out_shape=ja...  1.8 us
    pallas_call x1, Pallas kernels, per_device(): pl.pallas_call(lambda *refs: pack_kernel(n_sub, rows, *refs), in_specs=[h...  1.67 us
    pallas_call x1, Pallas kernels, per_device(): pl.pallas_call(lambda *refs: voxel_kernel(width, *refs), out_shape=jax.Sh...  0.87 us
  transfers between devices with their start and end apart: 3, of which 1 were waited for; matrix products, arithmetic and copies ran while one was open for 0% of the time, Pallas kernels for 11%

profile of v10, /device:TPU:0, one launch (start us, length us, event | category | flops | bytes accessed | tf_op | source)
XLA Modules:
  0.0 24.3 jit_solution(9237923628660313731)
XLA Ops:
  0.0 1.7 %pack.1 = (bf16[1920,256]{1,0:T(8,128)(2,1)S(1)}, s32[2,32]{1,0:T(2,128)S(1)}, bf16[32,1920]{1,0:T(8,128)(2,1)S(1)}, bf16[32,1920]{1,0:T(8,128)(2,1)S(1)}, bf16[32,1920]{1,0:T(8,128)(2,1)S(1)}) custom-call(bf16[1920,256]{1,0:T(8,128)(2,1)} %bitcast.13, s32[2,32]{1,0:T(2,128)} %refs_1_.1, s32[2,32]{1,0:T(2,128)} %refs_2_.2), custom_call_target="tpu_custom_call" | custom-call | tf_op jit(solution)/shard_map/pack/pallas_call | solution.py:320
  1.7 0.5 %collective-permute-start = (bf16[32,1920]{1,0:T(8,128)(2,1)S(1)}, bf16[32,1920]{1,0:T(8,128)(2,1)S(1)}, u32[]{:S(2)}, u32[]{:S(2)}) collective-permute-start(bf16[32,1920]{1,0:T(8,128)(2,1)S(1)} %get-tuple-element.28), channel_id=1, source_target_pairs={{0,1},{1,0},{2,3},{3,2},{4,8},{5,9},{6,10},{7,11},{8,4},{9,5},{10,... | collective-permute-start | bytes 368648 | tf_op jit(solution)/shard_map/ppermute | solution.py:351
  2.2 2.6 %collective-permute-start.1 = (bf16[32,1920]{1,0:T(8,128)(2,1)S(1)}, bf16[32,1920]{1,0:T(8,128)(2,1)S(1)}, u32[]{:S(2)}, u32[]{:S(2)}) collective-permute-start(bf16[32,1920]{1,0:T(8,128)(2,1)S(1)} %get-tuple-element.29), channel_id=1, source_target_pairs={{0,2},{1,5},{2,0},{3,7},{4,6},{5,1},{6,4},{7,3},{8,10},{9,13},{10,... | collective-permute-start | bytes 368648 | tf_op jit(solution)/shard_map/ppermute | solution.py:351
  4.8 3.1 %collective-permute-start.2 = (bf16[32,1920]{1,0:T(8,128)(2,1)S(1)}, bf16[32,1920]{1,0:T(8,128)(2,1)S(1)}, u32[]{:S(2)}, u32[]{:S(2)}) collective-permute-start(bf16[32,1920]{1,0:T(8,128)(2,1)S(1)} %get-tuple-element.30), channel_id=1, source_target_pairs={{0,4},{1,3},{2,6},{3,1},{4,0},{5,7},{6,2},{7,5},{8,12},{9,11},{10,... | collective-permute-start | bytes 368648 | tf_op jit(solution)/shard_map/ppermute | solution.py:351
  7.8 2.7 %prepare.1 = (bf16[8,256,512]{2,1,0:T(8,128)(2,1)S(1)}, s32[4,128]{1,0:T(4,128)S(1)}, bf16[2,216,256]{2,1,0:T(8,128)(2,1)S(1)}, bf16[384,128]{1,0:T(8,128)(2,1)S...) custom-call(s32[2,32]{1,0:T(2,128)S(1)} %get-tuple-element.18.refs_0, ...), custom_call_target="tpu_custom_call" | custom-call | flops 536870912 | bytes 4194304 | tf_op jit(solution)/shard_map/prepare/pallas_call | solution.py:355
  10.5 0.0 collective-permute-done.refs_8_
  10.5 0.0 collective-permute-done.1.refs_9_
  10.5 0.1 collective-permute-done.2.refs_10_
  10.7 1.8 %elements.1 = bf16[384,128]{1,0:T(8,128)(2,1)S(1)} custom-call(bf16[8,256,512]{2,1,0:T(8,128)(2,1)S(1)} %get-tuple-element.20.refs_0_, s32[4,128]{1,0:T(4,128)S(1)} %get-tuple-element.21.refs_1_, bf16[2,216,256]{2,1,0:T(8,128)(2,1)S(1)} %get-tuple-element.22.refs_2_, bf16[384,128]{1,0:T(8,128)(2,1)S(1)} %get-tuple-element.23.refs_3_, ...), custom_call_target="tpu_custom_call" | custom-call | tf_op jit(solution)/shard_map/elements/pallas_call | solution.py:395
  12.5 11.0 %all_to_all.11 = bf16[8,48,128]{2,1,0:T(8,128)(2,1)S(1)} all-to-all(bf16[8,48,128]{2,1,0:T(8,128)(2,1)S(1)} %bitcast.11), channel_id=1, replica_groups=mesh['groups'=2,'dom'=4,'sub'=2,'rhs'=2] {'dom','sub'}, dimensions={0} | all-to-all | bytes 196608 | tf_op jit(solution)/shard_map/all_to_all | solution.py:405
  23.5 0.9 %voxels.1 = f32[96,128]{1,0:T(8,128)} custom-call(bf16[384,128]{1,0:T(8,128)(2,1)S(1)} %bitcast.12), custom_call_target="tpu_custom_call" | custom-call | tf_op jit(solution)/shard_map/voxels/pallas_call | solution.py:406
Async XLA Ops:
  1.7 8.8 %collective-permute-start = (bf16[32,1920]{1,0:T(8,128)(2,1)S(1)}, bf16[32,1920]{1,0:T(8,128)(2,1)S(1)}, u32[]{:S(2)}, u32[]{:S(2)}) collective-permute-start(bf16[32,1920]{1,0:T(8,128)(2,1)S(1)} %get-tuple-element.28), channel_id=1, source_target_pairs={{0,1},{1,0},{2,3},{3,2},{4,8},{5,9},{6,10},{7,11},{8,4},{9,5},{10,... | collective-permute-start | bytes 368648 | tf_op jit(solution)/shard_map/ppermute | solution.py:351
  2.2 8.3 %collective-permute-start.1 = (bf16[32,1920]{1,0:T(8,128)(2,1)S(1)}, bf16[32,1920]{1,0:T(8,128)(2,1)S(1)}, u32[]{:S(2)}, u32[]{:S(2)}) collective-permute-start(bf16[32,1920]{1,0:T(8,128)(2,1)S(1)} %get-tuple-element.29), channel_id=1, source_target_pairs={{0,2},{1,5},{2,0},{3,7},{4,6},{5,1},{6,4},{7,3},{8,10},{9,13},{10,... | collective-permute-start | bytes 368648 | tf_op jit(solution)/shard_map/ppermute | solution.py:351
  4.8 5.9 %collective-permute-start.2 = (bf16[32,1920]{1,0:T(8,128)(2,1)S(1)}, bf16[32,1920]{1,0:T(8,128)(2,1)S(1)}, u32[]{:S(2)}, u32[]{:S(2)}) collective-permute-start(bf16[32,1920]{1,0:T(8,128)(2,1)S(1)} %get-tuple-element.30), channel_id=1, source_target_pairs={{0,4},{1,3},{2,6},{3,1},{4,0},{5,7},{6,2},{7,5},{8,12},{9,11},{10,... | collective-permute-start | bytes 368648 | tf_op jit(solution)/shard_map/ppermute | solution.py:351

commit v11 on v10

--- a/solution.py
+++ b/solution.py
@@ -218,7 +218,7 @@
         parts.append(jnp.zeros((128 - rows * len(parts), values), jnp.bfloat16))
         tables.append(jnp.concatenate(parts, axis=0))
     starts = block_starts(columns)
-    found = 0.0
+    found = None
     others = []
     for t in range(tiles):
         blocks = []
@@ -228,7 +228,8 @@
             blocks += [pair[:, :128], pair[:, 128:]]
         others.append(blocks)
         stacked = jnp.concatenate([x.astype(jnp.bfloat16) for x in blocks], axis=0)
-        found = found + dot(stacked, hot_ref[t])
+        part = dot(stacked, hot_ref[t])
+        found = part if found is None else found + part
     found = found.astype(jnp.bfloat16)
     lanes = [
         jnp.broadcast_to(places_ref[4 * t + 3 : 4 * t + 4, :], (BLOCK, elems))

time: 24.6 us -> 24.6 us (level)
  no operation moved by 1% of the time
where the time goes in v11:
time: 24.6 us; the launch traced here: 24.3 us
  blocking collectives  11 us (45%)
  Pallas kernels  7.01 us (28%)
  starting transfers between devices  6.16 us (25%)
    all_to_all x1, blocking collectives, per_device(): lax.all_to_all(sent, ('dom', 'sub'), split_axis=0, concat_axis=0, tiled=T...  11 us
    ppermute x3, starting transfers between devices, per_device(): halos.append(lax.ppermute(part, ('dom', 'sub', 'rhs'), pairs))  6.16 us
    pallas_call x1, Pallas kernels, per_device(): pl.pallas_call(lambda *refs: prepare_kernel(n_sub, capacity, columns, *re...  2.68 us
    pallas_call x1, Pallas kernels, per_device(): pl.pallas_call(lambda *refs: element_kernel(columns, *refs), out_shape=ja...  1.8 us
    pallas_call x1, Pallas kernels, per_device(): pl.pallas_call(lambda *refs: pack_kernel(n_sub, rows, *refs), in_specs=[h...  1.67 us
    pallas_call x1, Pallas kernels, per_device(): pl.pallas_call(lambda *refs: voxel_kernel(width, *refs), out_shape=jax.Sh...  0.87 us
  transfers between devices with their start and end apart: 3, of which 1 were waited for; matrix products, arithmetic and copies ran while one was open for 0% of the time, Pallas kernels for 11%

profile of v11, /device:TPU:0, one launch (start us, length us, event | category | flops | bytes accessed | tf_op | source)
XLA Modules:
  0.0 24.3 jit_solution(9237923628660313731)
XLA Ops:
  0.0 1.7 %pack.1 = (bf16[1920,256]{1,0:T(8,128)(2,1)S(1)}, s32[2,32]{1,0:T(2,128)S(1)}, bf16[32,1920]{1,0:T(8,128)(2,1)S(1)}, bf16[32,1920]{1,0:T(8,128)(2,1)S(1)}, bf16[32,1920]{1,0:T(8,128)(2,1)S(1)}) custom-call(bf16[1920,256]{1,0:T(8,128)(2,1)} %bitcast.13, s32[2,32]{1,0:T(2,128)} %refs_1_.1, s32[2,32]{1,0:T(2,128)} %refs_2_.2), custom_call_target="tpu_custom_call" | custom-call | tf_op jit(solution)/shard_map/pack/pallas_call | solution.py:321
  1.7 0.5 %collective-permute-start = (bf16[32,1920]{1,0:T(8,128)(2,1)S(1)}, bf16[32,1920]{1,0:T(8,128)(2,1)S(1)}, u32[]{:S(2)}, u32[]{:S(2)}) collective-permute-start(bf16[32,1920]{1,0:T(8,128)(2,1)S(1)} %get-tuple-element.28), channel_id=1, source_target_pairs={{0,1},{1,0},{2,3},{3,2},{4,8},{5,9},{6,10},{7,11},{8,4},{9,5},{10,... | collective-permute-start | bytes 368648 | tf_op jit(solution)/shard_map/ppermute | solution.py:352
  2.2 2.6 %collective-permute-start.1 = (bf16[32,1920]{1,0:T(8,128)(2,1)S(1)}, bf16[32,1920]{1,0:T(8,128)(2,1)S(1)}, u32[]{:S(2)}, u32[]{:S(2)}) collective-permute-start(bf16[32,1920]{1,0:T(8,128)(2,1)S(1)} %get-tuple-element.29), channel_id=1, source_target_pairs={{0,2},{1,5},{2,0},{3,7},{4,6},{5,1},{6,4},{7,3},{8,10},{9,13},{10,... | collective-permute-start | bytes 368648 | tf_op jit(solution)/shard_map/ppermute | solution.py:352
  4.8 3.1 %collective-permute-start.2 = (bf16[32,1920]{1,0:T(8,128)(2,1)S(1)}, bf16[32,1920]{1,0:T(8,128)(2,1)S(1)}, u32[]{:S(2)}, u32[]{:S(2)}) collective-permute-start(bf16[32,1920]{1,0:T(8,128)(2,1)S(1)} %get-tuple-element.30), channel_id=1, source_target_pairs={{0,4},{1,3},{2,6},{3,1},{4,0},{5,7},{6,2},{7,5},{8,12},{9,11},{10,... | collective-permute-start | bytes 368648 | tf_op jit(solution)/shard_map/ppermute | solution.py:352
  7.8 2.7 %prepare.1 = (bf16[8,256,512]{2,1,0:T(8,128)(2,1)S(1)}, s32[4,128]{1,0:T(4,128)S(1)}, bf16[2,216,256]{2,1,0:T(8,128)(2,1)S(1)}, bf16[384,128]{1,0:T(8,128)(2,1)S...) custom-call(s32[2,32]{1,0:T(2,128)S(1)} %get-tuple-element.18.refs_0, ...), custom_call_target="tpu_custom_call" | custom-call | flops 536870912 | bytes 4194304 | tf_op jit(solution)/shard_map/prepare/pallas_call | solution.py:356
  10.5 0.0 collective-permute-done.refs_8_
  10.5 0.0 collective-permute-done.1.refs_9_
  10.5 0.1 collective-permute-done.2.refs_10_
  10.7 1.8 %elements.1 = bf16[384,128]{1,0:T(8,128)(2,1)S(1)} custom-call(bf16[8,256,512]{2,1,0:T(8,128)(2,1)S(1)} %get-tuple-element.20.refs_0_, s32[4,128]{1,0:T(4,128)S(1)} %get-tuple-element.21.refs_1_, bf16[2,216,256]{2,1,0:T(8,128)(2,1)S(1)} %get-tuple-element.22.refs_2_, bf16[384,128]{1,0:T(8,128)(2,1)S(1)} %get-tuple-element.23.refs_3_, ...), custom_call_target="tpu_custom_call" | custom-call | tf_op jit(solution)/shard_map/elements/pallas_call | solution.py:396
  12.5 11.0 %all_to_all.11 = bf16[8,48,128]{2,1,0:T(8,128)(2,1)S(1)} all-to-all(bf16[8,48,128]{2,1,0:T(8,128)(2,1)S(1)} %bitcast.11), channel_id=1, replica_groups=mesh['groups'=2,'dom'=4,'sub'=2,'rhs'=2] {'dom','sub'}, dimensions={0} | all-to-all | bytes 196608 | tf_op jit(solution)/shard_map/all_to_all | solution.py:406
  23.5 0.9 %voxels.1 = f32[96,128]{1,0:T(8,128)} custom-call(bf16[384,128]{1,0:T(8,128)(2,1)S(1)} %bitcast.12), custom_call_target="tpu_custom_call" | custom-call | tf_op jit(solution)/shard_map/voxels/pallas_call | solution.py:407
Async XLA Ops:
  1.7 8.8 %collective-permute-start = (bf16[32,1920]{1,0:T(8,128)(2,1)S(1)}, bf16[32,1920]{1,0:T(8,128)(2,1)S(1)}, u32[]{:S(2)}, u32[]{:S(2)}) collective-permute-start(bf16[32,1920]{1,0:T(8,128)(2,1)S(1)} %get-tuple-element.28), channel_id=1, source_target_pairs={{0,1},{1,0},{2,3},{3,2},{4,8},{5,9},{6,10},{7,11},{8,4},{9,5},{10,... | collective-permute-start | bytes 368648 | tf_op jit(solution)/shard_map/ppermute | solution.py:352
  2.2 8.3 %collective-permute-start.1 = (bf16[32,1920]{1,0:T(8,128)(2,1)S(1)}, bf16[32,1920]{1,0:T(8,128)(2,1)S(1)}, u32[]{:S(2)}, u32[]{:S(2)}) collective-permute-start(bf16[32,1920]{1,0:T(8,128)(2,1)S(1)} %get-tuple-element.29), channel_id=1, source_target_pairs={{0,2},{1,5},{2,0},{3,7},{4,6},{5,1},{6,4},{7,3},{8,10},{9,13},{10,... | collective-permute-start | bytes 368648 | tf_op jit(solution)/shard_map/ppermute | solution.py:352
  4.8 5.9 %collective-permute-start.2 = (bf16[32,1920]{1,0:T(8,128)(2,1)S(1)}, bf16[32,1920]{1,0:T(8,128)(2,1)S(1)}, u32[]{:S(2)}, u32[]{:S(2)}) collective-permute-start(bf16[32,1920]{1,0:T(8,128)(2,1)S(1)} %get-tuple-element.30), channel_id=1, source_target_pairs={{0,4},{1,3},{2,6},{3,1},{4,0},{5,7},{6,2},{7,5},{8,12},{9,11},{10,... | collective-permute-start | bytes 368648 | tf_op jit(solution)/shard_map/ppermute | solution.py:352
